TPU v7x, 32 devices: a whole 2x2x4 slice. The times are simulated.
32 devices in a mesh: dp: 8 (over z, y), rep: 4 (over x, core).
Axes of the slice: x: 2, y: 2, z: 4, core: 2. Of those that a mesh axis runs over, the one named last changes fastest.
Arguments:
- item_table: bfloat16 [4096, 512], P(('dp', 'rep')), may hold values from -6 to 6
- requests: int32 [32, 32, 2], P(('dp', 'rep')), may hold values from 0 to 127, as said below
- event_slot: int32 [16384], P(('dp', 'rep')), may hold values from 0 to 63, as said below
- lengths: int32 [32, 4], P(('dp', 'rep')), may hold values from 1 to 256, 512 in all within a row
- leaf_ids: int32 [16384, 8], P(('dp', 'rep')), may hold values from 0 to 31
- leaf_table: bfloat16 [256, 512], replicated, may hold values from -2.09375 to 2.09375
- w_in: bfloat16 [512, 2048], replicated, may hold values from -0.25 to 0.25
- w_out: bfloat16 [512, 512], replicated, may hold values from -0.25 to 0.25
- cotangent: bfloat16 [16384, 512], P(('dp', 'rep')), may hold values from -6 to 6
Outputs:
- output: bfloat16 [16384, 512], P(('dp', 'rep'))
- table_grad: float32 [4096, 512], P(('dp', 'rep'))
- leaf_grad: float32 [256, 512], replicated
- w_in_grad: float32 [512, 2048], replicated
- w_out_grad: float32 [512, 512], replicated
Inputs may be any that keep to these rules, and one draw needn't show every extreme that they name: `requests`: for each device and owner the 2 requested rows are distinct. `event_slot`: every one of a device's 64 slots is named by at least one of its events.
All inputs are finite; a program needn't handle non-finite values.
Results may differ from a plain program's by a relative error of at most 0.014.
Values may be sent and summed in bfloat16 or wider, within the bound.
No kernel may reach another device: no remote copies, remote signals or barrier semaphores. Data moves between devices by JAX's collectives and lax.ppermute only.
A program may use at most 64 MiB of HBM per device.

v0:
```python
import functools
import jax
import jax.numpy as jnp
from jax import lax
from jax.experimental import pallas as pl
from jax.experimental.pallas import tpu as pltpu
from jax.sharding import PartitionSpec as P

HEADS = 4
MAXLEN = 256
BLOCK = 128
ROWS = 16
epsilon = 1e-06
f32 = jnp.float32
bf16 = jnp.bfloat16

EARLY = ((0,), (1, 2), (3, 4))
LATE = ((0,), (3,), (4,))
SHARED = ((2,), (1,))
SPLIT = 2048
CHUNKS = 32
STRIP = 32
LAYER_VMEM = 60 * 2**20


def dot(a, b, contract):
    return lax.dot_general(a, b, ((contract[0], contract[1]), ((), ())), preferred_element_type=f32)


def mm(a, b):
    return dot(a, b, ((1,), (0,)))


def mm_nt(a, b):
    return dot(a, b, ((1,), (1,)))


def mm_tn(a, b):
    return dot(a, b, ((0,), (0,)))


def mask_of(group, digit):
    return sum(((digit >> k) & 1) << bit for k, bit in enumerate(group))


def chunk_order(me, route, shared=()):
    masks = [0]
    for group in route + shared:
        masks = [mask ^ mask_of(group, digit) for mask in masks for digit in range(2 ** len(group))]
    for group in shared:
        me = me & ~mask_of(group, 1)
    return [me ^ mask for mask in masks]


def spans(count):
    for start in range(0, count, BLOCK):
        low = max(0, start - (MAXLEN - 1)) // BLOCK * BLOCK
        yield start, low, start + BLOCK


def strips(start, stop):
    return [slice(at, at + STRIP) for at in range(start, stop, STRIP)]


def silu(half):
    curve = jnp.tanh(half)
    value = (half + half * curve).astype(bf16)
    half, curve = half.astype(bf16), curve.astype(bf16)
    return value, (0.5 + 0.5 * curve) * (1.0 + half * (1.0 - curve))


def center(values):
    values = values - jnp.mean(values, axis=-1, keepdims=True)
    return values, lax.rsqrt(jnp.mean(values * values, axis=-1, keepdims=True) + epsilon)


def pull_normalize(change, normed, scale):
    return scale * (
        change
        - jnp.mean(change, axis=-1, keepdims=True)
        - normed * jnp.mean(change * normed, axis=-1, keepdims=True)
    )


def pickers(slots, slot_ref, leaf_ref, leaves):
    count = slot_ref.shape[1]
    picker = lax.broadcasted_iota(jnp.int32, (slots, count), 0) == slot_ref[...]
    trees = leaf_ref.shape[0]
    each = leaves // trees
    spots = lax.broadcasted_iota(jnp.int32, (each, count), 0)
    onehot = [(spots == leaf_ref[t : t + 1, :]).astype(f32).astype(bf16) for t in range(trees)]
    return picker.astype(f32).astype(bf16), jnp.concatenate(onehot, axis=0)


def permute_rows(chunks, source, target):
    for place, chunk in enumerate(chunks):
        start = pl.multiple_of(chunk * ROWS, ROWS)
        target[place * ROWS : (place + 1) * ROWS, :] = source[pl.ds(start, ROWS), :]


def zero_one(condition):
    return jnp.where(condition, 1.0, 0.0).astype(bf16)


def to_tiles(rows):
    parts = rows.shape[1] // BLOCK
    shape = (rows.shape[0] * parts, rows.shape[0])
    row, column = (lax.broadcasted_iota(jnp.int32, shape, axis) for axis in (0, 1))
    total = jnp.zeros((shape[0], BLOCK), f32)
    for part in range(parts):
        place = zero_one(row == column * parts + part)
        total = total + mm(place, rows[:, part * BLOCK : (part + 1) * BLOCK])
    return total.astype(bf16)


def from_tiles(block, width):
    parts = width // BLOCK
    shape = (block.shape[0] // parts, block.shape[0])
    row, column = (lax.broadcasted_iota(jnp.int32, shape, axis) for axis in (0, 1))
    pieces = [mm(zero_one(column == row * parts + part), block) for part in range(parts)]
    return jnp.concatenate(pieces, axis=1).astype(bf16)


def lookup_kernel(asked_ref, table_ref, rows_ref, chosen_ref):
    count, each = asked_ref.shape
    owned, width = table_ref.shape
    parts = width // BLOCK
    many = count * each * parts
    row = lax.broadcasted_iota(jnp.int32, (many, count), 0)
    device = lax.broadcasted_iota(jnp.int32, (many, count), 1)
    own = zero_one(row // (each * parts) == device)
    wanted = mm(own, asked_ref[...].astype(f32).astype(bf16)).astype(jnp.int32)
    spot = lax.broadcasted_iota(jnp.int32, (many, owned), 1)
    row = lax.broadcasted_iota(jnp.int32, (many, owned), 0)
    found = jnp.zeros((many, owned), jnp.bool_)
    for k in range(each):
        here = jnp.logical_and(row // parts % each == k, spot == wanted[:, k : k + 1])
        found = jnp.logical_or(found, here)
    chosen_ref[...] = zero_one(found)
    total = jnp.zeros((many, BLOCK), f32)
    for part in range(parts):
        mine = zero_one(jnp.logical_and(found, row % parts == part))
        total = total + mm(mine, table_ref[:, part * BLOCK : (part + 1) * BLOCK])
    rows_ref[...] = total.astype(bf16)


def run_lookup(asked, table):
    vmem = pl.BlockSpec(memory_space=pltpu.VMEM)
    shape = jax.ShapeDtypeStruct
    many = asked.shape[0] * asked.shape[1] * table.shape[1] // BLOCK
    return pl.pallas_call(
        lookup_kernel,
        name="lookup",
        out_shape=(
            shape((many, BLOCK), bf16),
            shape((many, table.shape[0]), bf16),
        ),
        in_specs=[vmem, vmem],
        out_specs=(vmem,) * 2,
        compiler_params=pltpu.CompilerParams(vmem_limit_bytes=16 * 2**20),
    )(asked, table)


def layer_kernel(
    me_ref, lengths_ref, slot_ref, leaf_ref, rows_ref, table_hbm, in_hbm, out_hbm, tangent_hbm,
    output_hbm, d_rows_ref, keep_hbm, send_hbm, keep_late_hbm, send_late_hbm,
    inputs, gated, d_pre, grads, output,
    normed, turned, moved, hidden, slope, weights, weights_slope, mixed, d_mixed,
    d_score, d_gated, allowed, allowed_scale, keys_t, values_t, d_inputs, leaf_grad, table, w_in, w_out, tangent, sems, out_sems,
):
    count, width = inputs.shape
    head = width // HEADS
    half_scale = 0.5 * head ** (-0.5)
    half_rows = width // 2
    copies = [
        pltpu.make_async_copy(source, target, sems.at[k])
        for k, (source, target) in enumerate(
            ((table_hbm, table), (in_hbm, w_in), (out_hbm, w_out), (tangent_hbm, tangent))
        )
    ]
    for copy in copies:
        copy.start()
    leaving = []

    def leave(source, target):
        copy = pltpu.make_async_copy(source, target, out_sems.at[len(leaving)])
        copy.start()
        leaving.append(copy)

    rows = from_tiles(rows_ref[...], width)
    picker, onehot = pickers(rows.shape[0], slot_ref, leaf_ref, table.shape[0])
    ends = []
    total = 0
    for place in range(lengths_ref.shape[1]):
        total = total + lengths_ref[0, place]
        ends.append(total)
    for start, low, high in spans(count):
        at = slice(start, start + BLOCK)
        row = start + lax.broadcasted_iota(jnp.int32, (BLOCK, high - low), 0)
        column = low + lax.broadcasted_iota(jnp.int32, (BLOCK, high - low), 1)
        first = jnp.zeros_like(row)
        for end in ends[:-1]:
            first = jnp.where(row >= end, end, first)
        seen = jnp.logical_and(column >= first, column <= row)
        allowed[at, low:high] = jnp.where(seen, 1.0, 0.0).astype(bf16)
        allowed_scale[at, low:high] = jnp.where(seen, 2.0 * half_scale, 0.0).astype(bf16)
    copies[0].wait()
    inputs[...] = (mm_tn(picker, rows) + mm_tn(onehot, table[...])).astype(bf16)
    for at in strips(0, count):
        values, scale = center(inputs[at, :].astype(f32))
        normed[at, :] = (values * scale).astype(bf16)
    turned[...] = normed[...].T
    copies[1].wait()
    for start in range(0, 4 * width, 2 * BLOCK):
        to = slice(start, start + 2 * BLOCK)
        halves = mm(normed[...], w_in[:, to]) * 0.5
        for at in strips(0, count):
            value, slope_at = silu(halves[at, :])
            hidden[at, to] = value
            slope[at, to] = slope_at
    keys_t[...] = hidden[:, 3 * width :].T
    values_t[...] = hidden[:, width : 2 * width].T
    for start, low, high in spans(count):
        at = slice(start, start + BLOCK)
        end = start // (2 * BLOCK) * 2 * BLOCK + 2 * BLOCK
        for out in (slice(0, low), slice(high, end)):
            if out.start < out.stop:
                nothing = jnp.zeros((HEADS, BLOCK, out.stop - out.start), bf16)
                weights[:, at, out] = nothing
                d_score[:, at, out] = nothing
    for h in range(HEADS):
        own = slice(h * head, (h + 1) * head)
        value_at = slice(width + h * head, width + (h + 1) * head)
        query_at = slice(2 * width + h * head, 2 * width + (h + 1) * head)
        key_at = slice(3 * width + h * head, 3 * width + (h + 1) * head)
        for start, low, high in spans(count):
            at = slice(start, start + BLOCK)
            halves = mm(hidden[at, query_at], keys_t[own, low:high]) * half_scale
            for strip in strips(0, BLOCK):
                to = slice(start + strip.start, start + strip.stop)
                value, slope_at = silu(halves[strip, :])
                weights[h, to, low:high] = value * allowed[to, low:high]
                weights_slope[h, to, low:high] = slope_at * allowed_scale[to, low:high]
        for start in range(0, count, 2 * BLOCK):
            at = slice(start, start + 2 * BLOCK)
            high = start + 2 * BLOCK
            mixed[at, h * head : (h + 1) * head] = mm(
                weights[h, at, :high], hidden[:high, value_at]
            )
    copies[2].wait()
    copies[3].wait()
    d_gated[...] = mm_nt(tangent[...], w_out[...]).astype(bf16)
    for at in strips(0, count):
        values, scale = center(mixed[at, :])
        values = values * scale
        gates = hidden[at, :width].astype(f32)
        change = d_gated[at, :].astype(f32)
        gated[at, :] = (values * gates).astype(bf16)
        d_pre[at, :width] = (change * values).astype(bf16) * slope[at, :width]
        d_mixed[at, :] = pull_normalize(change * gates, values, scale).astype(bf16)
    for h in range(HEADS):
        own = slice(h * head, (h + 1) * head)
        value_at = slice(width + h * head, width + (h + 1) * head)
        query_at = slice(2 * width + h * head, 2 * width + (h + 1) * head)
        key_at = slice(3 * width + h * head, 3 * width + (h + 1) * head)
        for start, low, high in spans(count):
            at = slice(start, start + BLOCK)
            d_weights = mm(d_mixed[at, own], values_t[own, low:high]).astype(bf16)
            d_score[h, at, low:high] = d_weights * weights_slope[h, at, low:high]
        for start in range(0, count, 2 * BLOCK):
            at = slice(start, start + 2 * BLOCK)
            high = start + 2 * BLOCK
            d_query = mm(d_score[h, at, :high], hidden[:high, key_at])
            d_pre[at, query_at] = d_query.astype(bf16) * slope[at, query_at]
            d_key = mm_tn(d_score[h, start:, at], hidden[start:, query_at])
            d_pre[at, key_at] = d_key.astype(bf16) * slope[at, key_at]
            d_value = mm_tn(weights[h, start:, at], d_mixed[start:, own])
            d_pre[at, value_at] = d_value.astype(bf16) * slope[at, value_at]
    me = me_ref[0]
    early, late = chunk_order(me, EARLY), chunk_order(me, LATE, SHARED)
    permute_rows(early, turned, moved)
    for start in range(0, 4 * width, 2 * BLOCK):
        to = slice(start, start + 2 * BLOCK)
        grads[:, to] = mm(moved[...], d_pre[:, to]).astype(bf16)
    leave(grads.at[half_rows:, :SPLIT], send_hbm)
    leave(grads.at[:half_rows, :SPLIT], keep_hbm)
    turned[...] = gated[...].T
    permute_rows(late, turned, moved)
    grads[:, 4 * width : 5 * width] = mm(moved[...], tangent[...]).astype(bf16)
    output[...] = (mm(gated[...], w_out[...]) + inputs[...].astype(f32)).astype(bf16)
    leave(output, output_hbm)
    normed_change = mm_nt(d_pre[...], w_in[...])
    for at in strips(0, count):
        values, scale = center(inputs[at, :].astype(f32))
        change = pull_normalize(normed_change[at, :], values * scale, scale)
        d_inputs[at, :] = (change + tangent[at, :].astype(f32)).astype(bf16)
    leaves = table.shape[0]
    d_leaf = mm(onehot, d_inputs[...]).astype(bf16)
    leaf_grad[:leaves, :] = d_leaf[:, : width // 2]
    leaf_grad[leaves:, :] = d_leaf[:, width // 2 :]
    permute_rows(late, leaf_grad, grads.at[:, 5 * width :])
    leave(grads.at[half_rows:, SPLIT:], send_late_hbm)
    leave(grads.at[:half_rows, SPLIT:], keep_late_hbm)
    d_rows_ref[...] = to_tiles(mm(picker, d_inputs[...]).astype(bf16))
    for copy in leaving:
        copy.wait()


def run_layer(me, lengths, slot, leaf, rows, table, w_in, w_out, tangent):
    count, width = tangent.shape
    smem = pl.BlockSpec(memory_space=pltpu.SMEM)
    vmem = pl.BlockSpec(memory_space=pltpu.VMEM)
    hbm = pl.BlockSpec(memory_space=pltpu.HBM)
    shape = jax.ShapeDtypeStruct
    columns = 5 * width + width // 2
    return pl.pallas_call(
        layer_kernel,
        name="layer",
        out_shape=(
            shape((count, width), bf16),
            shape(rows.shape, bf16),
            shape((width // 2, SPLIT), bf16),
            shape((width // 2, SPLIT), bf16),
            shape((width // 2, columns - SPLIT), bf16),
            shape((width // 2, columns - SPLIT), bf16),
        ),
        in_specs=[smem, smem] + [vmem] * 3 + [hbm] * 4,
        out_specs=(hbm, vmem, hbm, hbm, hbm, hbm),
        scratch_shapes=[
            pltpu.VMEM((count, width), bf16),
            pltpu.VMEM((count, width), bf16),
            pltpu.VMEM((count, 4 * width), bf16),
            pltpu.VMEM((width, columns), bf16),
            pltpu.VMEM((count, width), bf16),
            pltpu.VMEM((count, width), bf16),
            pltpu.VMEM((width, count), bf16),
            pltpu.VMEM((width, count), bf16),
            pltpu.VMEM((count, 4 * width), bf16),
            pltpu.VMEM((count, 4 * width), bf16),
            pltpu.VMEM((HEADS, count, count), bf16),
            pltpu.VMEM((HEADS, count, count), bf16),
            pltpu.VMEM((count, width), f32),
            pltpu.VMEM((count, width), bf16),
            pltpu.VMEM((HEADS, count, count), bf16),
            pltpu.VMEM((count, width), bf16),
            pltpu.VMEM((count, count), bf16),
            pltpu.VMEM((count, count), bf16),
            pltpu.VMEM((width, count), bf16),
            pltpu.VMEM((width, count), bf16),
            pltpu.VMEM((count, width), bf16),
            pltpu.VMEM((width, width // 2), bf16),
            pltpu.VMEM(table.shape, bf16),
            pltpu.VMEM(w_in.shape, bf16),
            pltpu.VMEM(w_out.shape, bf16),
            pltpu.VMEM(tangent.shape, bf16),
            pltpu.SemaphoreType.DMA((4,)),
            pltpu.SemaphoreType.DMA((5,)),
        ],
        compiler_params=pltpu.CompilerParams(vmem_limit_bytes=LAYER_VMEM),
        cost_estimate=pl.CostEstimate(flops=6 * 10**9, bytes_accessed=10**7, transcendentals=10**6),
    )(me, lengths, slot, leaf, rows, table, w_in, w_out, tangent)


def finish_kernel(
    me_ref, chosen_ref, returned_ref, early_own, early_other, late_own, late_other,
    table_hbm, leaf_hbm, in_hbm, out_hbm, grads, table, sems,
):
    width, columns = grads.shape
    leaves = leaf_hbm.shape[0]
    me = me_ref[0]
    half_rows = width // 2
    leaving = []

    def leave(source, target):
        copy = pltpu.make_async_copy(source, target, sems.at[len(leaving)])
        copy.start()
        leaving.append(copy)

    early, late = chunk_order(me, EARLY), chunk_order(me, LATE, SHARED)

    def place(chunks, own, other, low, high, at):
        for spot, chunk in enumerate(chunks):
            source = own if spot * ROWS < half_rows else other
            row = spot * ROWS % half_rows
            start = pl.multiple_of(chunk * ROWS, ROWS)
            grads[pl.ds(start, ROWS), at + low : at + high] = source[
                row : row + ROWS, low:high
            ].astype(f32)

    place(late, late_own, late_other, 0, width, SPLIT)
    leave(grads.at[:, SPLIT : SPLIT + width], out_hbm)
    place(late, late_own, late_other, width, columns - SPLIT, SPLIT)
    for half in range(2):
        leave(
            grads.at[half * leaves : (half + 1) * leaves, SPLIT + width :],
            leaf_hbm.at[:, half * (width // 2) : (half + 1) * (width // 2)],
        )
    row = lax.broadcasted_iota(jnp.int32, chosen_ref.shape, 0)
    parts = width // BLOCK
    for part in range(parts):
        mine = jnp.where(row % parts == part, chosen_ref[...].astype(f32), 0.0).astype(bf16)
        table[:, part * BLOCK : (part + 1) * BLOCK] = mm_tn(mine, returned_ref[...])
    leave(table, table_hbm)
    for low in range(0, SPLIT, width):
        place(early, early_own, early_other, low, low + width, 0)
        leave(grads.at[:, low : low + width], in_hbm.at[:, low : low + width])
    for copy in leaving:
        copy.wait()


def run_finish(me, chosen, returned, early_own, early_other, late_own, late_other, leaves):
    smem = pl.BlockSpec(memory_space=pltpu.SMEM)
    vmem = pl.BlockSpec(memory_space=pltpu.VMEM)
    hbm = pl.BlockSpec(memory_space=pltpu.HBM)
    shape = jax.ShapeDtypeStruct
    width = early_own.shape[1] // 4
    return pl.pallas_call(
        finish_kernel,
        name="finish",
        out_shape=(
            shape((chosen.shape[1], width), f32),
            shape((leaves, width), f32),
            shape((width, 4 * width), f32),
            shape((width, width), f32),
        ),
        in_specs=[smem] + [vmem] * 6,
        out_specs=(hbm,) * 4,
        scratch_shapes=[
            pltpu.VMEM((width, early_own.shape[1] + late_own.shape[1]), f32),
            pltpu.VMEM((chosen.shape[1], width), f32),
            pltpu.SemaphoreType.DMA((8,)),
        ],
        compiler_params=pltpu.CompilerParams(vmem_limit_bytes=32 * 2**20),
    )(me, chosen, returned, early_own, early_other, late_own, late_other)


def load_kernel(*refs):
    for source, target in zip(refs[: len(refs) // 2], refs[len(refs) // 2 :]):
        target[...] = source[...]


def run_load(*arrays):
    vmem = pl.BlockSpec(memory_space=pltpu.VMEM)
    return pl.pallas_call(
        load_kernel,
        name="load",
        out_shape=tuple(jax.ShapeDtypeStruct(array.shape, array.dtype) for array in arrays),
        in_specs=[vmem] * len(arrays),
        out_specs=(vmem,) * len(arrays),
        compiler_params=pltpu.CompilerParams(vmem_limit_bytes=8 * 2**20),
        cost_estimate=pl.CostEstimate(flops=0, bytes_accessed=4 * 2**20, transcendentals=0),
    )(*arrays)


def merge_kernel(keep_ref, other_ref, *outs):
    rows = outs[0].shape[0]
    for part, out in enumerate(outs):
        at = slice(part * rows, (part + 1) * rows)
        out[...] = (keep_ref[at, :].astype(f32) + other_ref[at, :].astype(f32)).astype(bf16)


def run_merge(keep, other, parts):
    vmem = pl.BlockSpec(memory_space=pltpu.VMEM)
    part = jax.ShapeDtypeStruct((keep.shape[0] // parts, keep.shape[1]), bf16)
    return pl.pallas_call(
        merge_kernel,
        name="merge",
        out_shape=(part,) * parts,
        in_specs=[vmem] * 2,
        out_specs=(vmem,) * parts,
        compiler_params=pltpu.CompilerParams(vmem_limit_bytes=8 * 2**20),
    )(keep, other)


def exchange(blocks):
    return lax.all_to_all(blocks, ("dp", "rep"), split_axis=0, concat_axis=0, tiled=True)


def swap(block, mask, count):
    return lax.ppermute(block, ("dp", "rep"), [(i, i ^ mask) for i in range(count)])


def add(parts):
    return sum(part.astype(f32) for part in parts)


def shares(parts, group):
    size = 2 ** len(group)
    rows = parts[0].shape[0] // size
    return [
        add(part[digit * rows : (digit + 1) * rows] for part in parts).astype(bf16)
        for digit in range(1, size)
    ]


def swap_all(blocks, group, count):
    return [
        swap(block, mask_of(group, digit), count) for digit, block in enumerate(blocks, start=1)
    ]


def extend(parts, got):
    return [part[: got[0].shape[0]] for part in parts] + got


def split_up(parts, group, count):
    return extend(parts, swap_all(shares(parts, group), group, count))


def sum_with(block, group, count):
    return block.astype(f32) + swap(block, mask_of(group, 1), count).astype(f32)


def join(block, group, count):
    pieces = swap_all([block] * (2 ** len(group) - 1), group, count)
    return jnp.concatenate([block] + pieces, axis=0)


def reduce_and_gather(early, late, d_rows, count):
    _, near, far = EARLY
    _, first, second = LATE
    early_other, late_other = swap(early[1], 1, count), swap(late[1], 1, count)
    early_own, late_own = run_load(early[0], late[0])
    early, *early_blocks = run_merge(early_own, early_other, 2 ** len(near))
    late, *late_blocks = run_merge(late_own, late_other, 2 ** len(first))
    early_blocks, late_blocks = lax.optimization_barrier((early_blocks, late_blocks))
    early_got = swap_all(early_blocks, near, count)
    late = split_up([late] + swap_all(late_blocks, first, count), second, count)
    early_got, late = lax.optimization_barrier((early_got, late))
    early, late = split_up([early] + early_got, far, count), add(late).astype(bf16)
    late = sum_with(late, SHARED[0], count).astype(bf16)
    early, late = add(early), sum_with(late, SHARED[1], count)
    reach = CHUNKS
    while reach < count:
        early, late = early + swap(early, reach, count), late + swap(late, reach, count)
        reach *= 2
    early = join((early * (1.0 / count)).astype(bf16), far, count)
    early, late = lax.optimization_barrier((early, (late * (1.0 / count)).astype(bf16)))
    pieces = swap_all([early] * (2 ** len(near) - 1), near, count)
    late, d_rows = lax.optimization_barrier((join(late, second, count), d_rows))
    returned = exchange(d_rows)
    late = join(late, first, count)
    pieces, late, returned = lax.optimization_barrier((pieces, late, returned))
    early = jnp.concatenate([early] + pieces, axis=0)
    return returned, early, swap(early, 1, count), late, swap(late, 1, count)


def on_device(
    item_table, requests, event_slot, lengths, leaf_ids, leaf_table, w_in, w_out, cotangent
):
    count = lax.axis_size("dp") * lax.axis_size("rep")
    place = lax.axis_index(("dp", "rep")).astype(jnp.int32)
    me = (place & (CHUNKS - 1)).reshape(1)
    slot = event_slot.reshape(1, -1)
    leaf = leaf_ids.T
    asked = exchange(requests[0])
    fetched, chosen = run_lookup(asked, item_table)
    arrived = exchange(fetched)
    output, d_rows, keep, send, keep_late, send_late = run_layer(
        me, lengths, slot, leaf, arrived, leaf_table, w_in, w_out, cotangent
    )
    returned, early, early_other, late, late_other = reduce_and_gather(
        (keep, send), (keep_late, send_late), d_rows, count
    )
    table_grad, leaf_mean, in_mean, out_mean = run_finish(
        me, chosen, returned, early, early_other, late, late_other, leaf_table.shape[0]
    )
    return (output, table_grad, leaf_mean, in_mean, out_mean)


def solution(mesh):
    return jax.shard_map(
        on_device,
        mesh=mesh,
        in_specs=(
            P(("dp", "rep"), None),
            P(("dp", "rep"), None, None),
            P(("dp", "rep")),
            P(("dp", "rep"), None),
            P(("dp", "rep"), None),
            P(),
            P(),
            P(),
            P(("dp", "rep"), None),
        ),
        out_specs=(P(("dp", "rep"), None), P(("dp", "rep"), None), P(), P(), P()),
        check_vma=False,
    )
```

profile of v0, /device:TPU:0, one launch (start us, length us, event | category | flops | bytes accessed | tf_op | source)
XLA Modules:
  0.0 105.3 jit_solution(1839520126497049741)
XLA Ops:
  0.6 0.8 copy.15
  1.4 14.2 %all_to_all.34 = s32[32,1,2]{2,1,0:T(1,128)S(1)} all-to-all(s32[32,1,2]{2,1,0:T(1,128)S(1)} %copy.15), channel_id=1, replica_groups=mesh['dp'=8,'rep'=4] {'dp','rep'}, dimensions={0} | all-to-all | bytes 512 | tf_op jit(solution)/shard_map/all_to_all | solution.py:476
  15.6 0.9 copy-done.2
  16.5 1.1 %lookup.1 = (bf16[256,128]{1,0:T(8,128)(2,1)}, bf16[256,128]{1,0:T(8,128)(2,1)S(1)}) custom-call(s32[32,2]{1,0:T(8,128)S(1)} %bitcast.10, bf16[128,512]{1,0:T(8,128)(2,1)S(1)} %copy-done.2), custom_call_target="tpu_custom_call" | custom-call | tf_op jit(solution)/shard_map/lookup/pallas_call | solution.py:151
  17.6 2.6 %all-to-all-start.1 = ((bf16[32,8,128]{2,1,0:T(8,128)(2,1)}), bf16[32,8,128]{2,1,0:T(8,128)(2,1)S(1)}, u32[]{:S(2)}, u32[]{:S(2)}) async-start(bf16[32,8,128]{2,1,0:T(8,128)(2,1)} %bitcast.5), calls=%async_computation.1 | async-start | bytes 131072 | tf_op jit(solution)/shard_map/all_to_all | solution.py:476
  20.2 7.4 %all-to-all-done.1 = bf16[32,8,128]{2,1,0:T(8,128)(2,1)S(1)} async-done(((bf16[32,8,128]{2,1,0:T(8,128)(2,1)}), bf16[32,8,128]{2,1,0:T(8,128)(2,1)S(1)}, u32[]{:S(2)}, u32[]{:S(2)}) %all-to-all-start.1) | async-done | bytes 65568 | tf_op jit(solution)/shard_map/all_to_all | solution.py:476
  27.6 0.6 copy-done.3
  28.3 14.5 %layer.1 = (bf16[512,512]{1,0:T(8,128)(2,1)}, bf16[256,128]{1,0:T(8,128)(2,1)}, bf16[256,2048]{1,0:T(8,128)(2,1)}, bf16[256,2048]{1,0:T(8,128)(2,1)}, bf16[256,7...) custom-call(s32[1]{0:T(128)} %bitcast.me_ref, s32[1,4]{1,0:T(1,128)} %lengths_ref.1, s32[1,512]{1,0:T(1,128)} %bitcast.14, ...), custom_call_target="tpu_custom_call" | custom-call | flops 6000000000 | bytes 10000000 | tf_op jit(solution)/shard_map/layer/pallas_call | solution.py:316
  42.8 0.2 collective-permute-start
  43.0 0.4 collective-permute-start.1
  43.4 1.2 %copy-done = bf16[256,2048]{1,0:T(8,128)(2,1)S(1)} copy-done((bf16[256,2048]{1,0:T(8,128)(2,1)S(1)}, bf16[256,2048]{1,0:T(8,128)(2,1)}, u32[]{:S(2)}) %copy-start) | copy-done | bytes 1048600
  44.6 1.0 copy-done.1
  45.6 0.1 load.1
  45.7 0.6 collective-permute-done.1.other_ref
  46.3 0.1 merge.3
  46.4 0.2 merge.2
  46.7 0.7 collective-permute-start.5
  47.3 0.4 collective-permute-start.2
  47.8 0.9 collective-permute-start.3
  48.6 2.2 %collective-permute-start.4 = (bf16[64,2048]{1,0:T(8,128)(2,1)S(1)}, bf16[64,2048]{1,0:T(8,128)(2,1)S(1)}, u32[]{:S(2)}, u32[]{:S(2)}) collective-permute-start(bf16[64,2048]{1,0:T(8,128)(2,1)S(1)} %get-tuple-element.60), channel_id=1, source_target_pairs={{0,6},{1,7},{2,4},{3,5},{4,2},{5,3},{6,0},{7,1},{8,14},{9,15},{10,... | collective-permute-start | bytes 786440 | tf_op jit(solution)/shard_map/ppermute | solution.py:480
  50.8 2.8 %collective-permute-done.5 = bf16[128,768]{1,0:T(8,128)(2,1)S(1)} collective-permute-done((bf16[128,768]{1,0:T(8,128)(2,1)S(1)}, bf16[128,768]{1,0:T(8,128)(2,1)S(1)}, u32[]{:S(2)}, u32[]{:S(2)}) %collective-permute-start.5) | collective-permute-done | bytes 196640 | tf_op jit(solution)/shard_map/ppermute | solution.py:480
  53.7 0.7 collective-permute-start.6
  54.4 2.1 %collective-permute-done.2 = bf16[64,2048]{1,0:T(8,128)(2,1)S(1)} collective-permute-done((bf16[64,2048]{1,0:T(8,128)(2,1)S(1)}, bf16[64,2048]{1,0:T(8,128)(2,1)S(1)}, u32[]{:S(2)}, u32[]{:S(2)}) %collective-permute-start.2) | collective-permute-done | bytes 262176 | tf_op jit(solution)/shard_map/ppermute | solution.py:480
  56.5 4.6 %collective-permute-done.3 = bf16[64,2048]{1,0:T(8,128)(2,1)S(1)} collective-permute-done((bf16[64,2048]{1,0:T(8,128)(2,1)S(1)}, bf16[64,2048]{1,0:T(8,128)(2,1)S(1)}, u32[]{:S(2)}, u32[]{:S(2)}) %collective-permute-start.3) | collective-permute-done | bytes 262176 | tf_op jit(solution)/shard_map/ppermute | solution.py:480
  61.2 0.1 add_convert_fusion.5
  61.3 1.5 %collective-permute-start.7 = (bf16[16,2048]{1,0:T(8,128)(2,1)S(1)}, bf16[16,2048]{1,0:T(8,128)(2,1)S(1)}, u32[]{:S(2)}, u32[]{:S(2)}) collective-permute-start(bf16[16,2048]{1,0:T(8,128)(2,1)S(1)} %get-tuple-element.83), channel_id=1, source_target_pairs={{0,8},{1,9},{2,10},{3,11},{4,12},{5,13},{6,14},{7,15},{8,0},{9,1},... | collective-permute-start | bytes 196616 | tf_op jit(solution)/shard_map/ppermute | solution.py:480
  62.8 0.9 collective-permute-start.9
  63.6 1.2 %collective-permute-start.8 = (bf16[16,2048]{1,0:T(8,128)(2,1)S(1)}, bf16[16,2048]{1,0:T(8,128)(2,1)S(1)}, u32[]{:S(2)}, u32[]{:S(2)}) collective-permute-start(bf16[16,2048]{1,0:T(8,128)(2,1)S(1)} %get-tuple-element.85), channel_id=1, source_target_pairs={{0,16},{1,17},{2,18},{3,19},{4,20},{5,21},{6,22},{7,23},{8,24},{9,... | collective-permute-start | bytes 196616 | tf_op jit(solution)/shard_map/ppermute | solution.py:480
  64.9 1.4 %collective-permute-start.13 = (bf16[64,768]{1,0:T(8,128)(2,1)S(1)}, bf16[64,768]{1,0:T(8,128)(2,1)S(1)}, u32[]{:S(2)}, u32[]{:S(2)}) collective-permute-start(bf16[64,768]{1,0:T(8,128)(2,1)S(1)} %add_convert_fusion.1), channel_id=1, source_target_pairs={{0,4},{1,5},{2,6},{3,7},{4,0},{5,1},{6,2},{7,3},{8,12},{9,13},{10,... | collective-permute-start | bytes 294920 | tf_op jit(solution)/shard_map/ppermute | solution.py:480
  66.3 0.5 collective-permute-done.7
  66.8 2.1 %collective-permute-done.9 = bf16[16,2048]{1,0:T(8,128)(2,1)S(1)} collective-permute-done((bf16[16,2048]{1,0:T(8,128)(2,1)S(1)}, bf16[16,2048]{1,0:T(8,128)(2,1)S(1)}, u32[]{:S(2)}, u32[]{:S(2)}) %collective-permute-start.9) | collective-permute-done | bytes 65568 | tf_op jit(solution)/shard_map/ppermute | solution.py:480
  68.9 1.4 %collective-permute-done.8 = bf16[16,2048]{1,0:T(8,128)(2,1)S(1)} collective-permute-done((bf16[16,2048]{1,0:T(8,128)(2,1)S(1)}, bf16[16,2048]{1,0:T(8,128)(2,1)S(1)}, u32[]{:S(2)}, u32[]{:S(2)}) %collective-permute-start.8) | collective-permute-done | bytes 65568 | tf_op jit(solution)/shard_map/ppermute | solution.py:480
  70.4 0.1 multiply_convert_fusion.1
  70.4 1.7 %collective-permute-start.12 = (bf16[16,2048]{1,0:T(8,128)(2,1)S(1)}, bf16[16,2048]{1,0:T(8,128)(2,1)S(1)}, u32[]{:S(2)}, u32[]{:S(2)}) collective-permute-start(bf16[16,2048]{1,0:T(8,128)(2,1)S(1)} %multiply_convert_fusion.1), channel_id=1, source_target_pairs={{0,24},{1,25},{2,26},{3,27},{4,28},{5,29},{6,30},{7,31},{8,16},{9,... | collective-permute-start | bytes 196616 | tf_op jit(solution)/shard_map/ppermute | solution.py:480
  72.1 2.8 %collective-permute-start.10 = (bf16[16,2048]{1,0:T(8,128)(2,1)S(1)}, bf16[16,2048]{1,0:T(8,128)(2,1)S(1)}, u32[]{:S(2)}, u32[]{:S(2)}) collective-permute-start(bf16[16,2048]{1,0:T(8,128)(2,1)S(1)} %multiply_convert_fusion.1), channel_id=1, source_target_pairs={{0,8},{1,9},{2,10},{3,11},{4,12},{5,13},{6,14},{7,15},{8,0},{9,1},... | collective-permute-start | bytes 196616 | tf_op jit(solution)/shard_map/ppermute | solution.py:480
  74.9 3.4 %collective-permute-start.14 = (bf16[64,768]{1,0:T(8,128)(2,1)S(1)}, bf16[64,768]{1,0:T(8,128)(2,1)S(1)}, u32[]{:S(2)}, u32[]{:S(2)}) collective-permute-start(bf16[64,768]{1,0:T(8,128)(2,1)S(1)} %add_convert_fusion), channel_id=1, source_target_pairs={{0,2},{1,3},{2,0},{3,1},{4,6},{5,7},{6,4},{7,5},{8,10},{9,11},{10,... | collective-permute-start | bytes 294920 | tf_op jit(solution)/shard_map/ppermute | solution.py:480
  78.3 3.1 %collective-permute-done.14 = bf16[64,768]{1,0:T(8,128)(2,1)S(1)} collective-permute-done((bf16[64,768]{1,0:T(8,128)(2,1)S(1)}, bf16[64,768]{1,0:T(8,128)(2,1)S(1)}, u32[]{:S(2)}, u32[]{:S(2)}) %collective-permute-start.14) | collective-permute-done | bytes 98336 | tf_op jit(solution)/shard_map/ppermute | solution.py:480
  81.5 0.1 collective-permute-start.18
  81.6 0.4 collective-permute-start.17
  82.0 3.6 %collective-permute-start.16 = (bf16[64,2048]{1,0:T(8,128)(2,1)S(1)}, bf16[64,2048]{1,0:T(8,128)(2,1)S(1)}, u32[]{:S(2)}, u32[]{:S(2)}) collective-permute-start(bf16[64,2048]{1,0:T(8,128)(2,1)S(1)} %pad_maximum_fusion.1), channel_id=1, source_target_pairs={{0,4},{1,5},{2,6},{3,7},{4,0},{5,1},{6,2},{7,3},{8,12},{9,13},{10,... | collective-permute-start | bytes 786440 | tf_op jit(solution)/shard_map/ppermute | solution.py:480
  85.6 1.5 %collective-permute-done.18 = bf16[64,768]{1,0:T(8,128)(2,1)S(1)} collective-permute-done((bf16[64,768]{1,0:T(8,128)(2,1)S(1)}, bf16[64,768]{1,0:T(8,128)(2,1)S(1)}, u32[]{:S(2)}, u32[]{:S(2)}) %collective-permute-start.18) | collective-permute-done | bytes 98336 | tf_op jit(solution)/shard_map/ppermute | solution.py:480
  87.1 3.7 %all-to-all-start.2 = ((bf16[32,8,128]{2,1,0:T(8,128)(2,1)}), bf16[32,8,128]{2,1,0:T(8,128)(2,1)S(1)}, u32[]{:S(2)}, u32[]{:S(2)}) async-start(bf16[32,8,128]{2,1,0:T(8,128)(2,1)} %bitcast.7), calls=%async_computation.2 | async-start | bytes 131072 | tf_op jit(solution)/shard_map/all_to_all | solution.py:476
  90.8 1.8 %collective-permute-start.19 = (bf16[128,768]{1,0:T(8,128)(2,1)S(1)}, bf16[128,768]{1,0:T(8,128)(2,1)S(1)}, u32[]{:S(2)}, u32[]{:S(2)}) collective-permute-start(bf16[128,768]{1,0:T(8,128)(2,1)S(1)} %pad_maximum_fusion.2), channel_id=1, source_target_pairs={{0,8},{1,9},{2,10},{3,11},{4,12},{5,13},{6,14},{7,15},{8,0},{9,1},... | collective-permute-start | bytes 589832 | tf_op jit(solution)/shard_map/ppermute | solution.py:480
  92.7 6.3 %collective-permute-done.19 = bf16[128,768]{1,0:T(8,128)(2,1)S(1)} collective-permute-done((bf16[128,768]{1,0:T(8,128)(2,1)S(1)}, bf16[128,768]{1,0:T(8,128)(2,1)S(1)}, u32[]{:S(2)}, u32[]{:S(2)}) %collective-permute-start.19) | collective-permute-done | bytes 196640 | tf_op jit(solution)/shard_map/ppermute | solution.py:480
  99.1 0.1 collective-permute-start.20
  99.2 0.5 collective-permute-start.21
  99.7 2.7 %collective-permute-done.21.late_other = bf16[256,768]{1,0:T(8,128)(2,1)S(1)} collective-permute-done((bf16[256,768]{1,0:T(8,128)(2,1)S(1)}, bf16[256,768]{1,0:T(8,128)(2,1)S(1)}, u32[]{:S(2)}, u32[]{:S(2)}) %collective-permute-start.21) | collective-permute-done | bytes 393248 | tf_op jit(solution)/shard_map/ppermute | solution.py:480
  102.4 2.9 %finish.1 = (f32[128,512]{1,0:T(8,128)}, f32[256,512]{1,0:T(8,128)}, f32[512,2048]{1,0:T(8,128)}, f32[512,512]{1,0:T(8,128)}) custom-call(s32[1]{0:T(128)} %bitcast.me_ref, bf16[256,128]{1,0:T(8,128)(2,1)S(1)} %get-tuple-element.46.chosen_ref, bf16[256,128]{1,0:T(8,128)(2,1)S(1)} %bitcast.9, ...), custom_call_target="tpu_custom_call" | custom-call | tf_op jit(solution)/shard_map/finish/pallas_call | solution.py:417
  (31 shorter events, 0.3 us)
Async XLA Ops:
  15.6 0.9 copy-start.2
  17.6 10.0 %all-to-all-start.1 = ((bf16[32,8,128]{2,1,0:T(8,128)(2,1)}), bf16[32,8,128]{2,1,0:T(8,128)(2,1)S(1)}, u32[]{:S(2)}, u32[]{:S(2)}) async-start(bf16[32,8,128]{2,1,0:T(8,128)(2,1)} %bitcast.5), calls=%async_computation.1 | async-start | bytes 131072 | tf_op jit(solution)/shard_map/all_to_all | solution.py:476
  27.6 0.6 copy-start.3
  42.8 3.6 %collective-permute-start = (bf16[256,2048]{1,0:T(8,128)(2,1)}, bf16[256,2048]{1,0:T(8,128)(2,1)S(1)}, u32[]{:S(2)}, u32[]{:S(2)}) collective-permute-start(bf16[256,2048]{1,0:T(8,128)(2,1)} %get-tuple-element.50), channel_id=1, source_target_pairs={{0,1},{1,0},{2,3},{3,2},{4,5},{5,4},{6,7},{7,6},{8,9},{9,8},{10,11... | collective-permute-start | bytes 3145736 | tf_op jit(solution)/shard_map/ppermute | solution.py:480
  43.0 3.3 %collective-permute-start.1 = (bf16[256,768]{1,0:T(8,128)(2,1)}, bf16[256,768]{1,0:T(8,128)(2,1)S(1)}, u32[]{:S(2)}, u32[]{:S(2)}) collective-permute-start(bf16[256,768]{1,0:T(8,128)(2,1)} %get-tuple-element.56), channel_id=1, source_target_pairs={{0,1},{1,0},{2,3},{3,2},{4,5},{5,4},{6,7},{7,6},{8,9},{9,8},{10,11... | collective-permute-start | bytes 1179656 | tf_op jit(solution)/shard_map/ppermute | solution.py:480
  43.4 1.2 %copy-start = (bf16[256,2048]{1,0:T(8,128)(2,1)S(1)}, bf16[256,2048]{1,0:T(8,128)(2,1)}, u32[]{:S(2)}) copy-start(bf16[256,2048]{1,0:T(8,128)(2,1)} %get-tuple-element.47.refs_0_) | copy-start | bytes 3145732
  44.6 1.0 copy-start.1
  46.7 7.0 %collective-permute-start.5 = (bf16[128,768]{1,0:T(8,128)(2,1)S(1)}, bf16[128,768]{1,0:T(8,128)(2,1)S(1)}, u32[]{:S(2)}, u32[]{:S(2)}) collective-permute-start(bf16[128,768]{1,0:T(8,128)(2,1)S(1)} %get-tuple-element.62), channel_id=1, source_target_pairs={{0,8},{1,9},{2,10},{3,11},{4,12},{5,13},{6,14},{7,15},{8,0},{9,1},... | collective-permute-start | bytes 589832 | tf_op jit(solution)/shard_map/ppermute | solution.py:480
  47.3 9.2 %collective-permute-start.2 = (bf16[64,2048]{1,0:T(8,128)(2,1)S(1)}, bf16[64,2048]{1,0:T(8,128)(2,1)S(1)}, u32[]{:S(2)}, u32[]{:S(2)}) collective-permute-start(bf16[64,2048]{1,0:T(8,128)(2,1)S(1)} %get-tuple-element.58), channel_id=1, source_target_pairs={{0,2},{1,3},{2,0},{3,1},{4,6},{5,7},{6,4},{7,5},{8,10},{9,11},{10,... | collective-permute-start | bytes 786440 | tf_op jit(solution)/shard_map/ppermute | solution.py:480
  47.8 13.4 %collective-permute-start.3 = (bf16[64,2048]{1,0:T(8,128)(2,1)S(1)}, bf16[64,2048]{1,0:T(8,128)(2,1)S(1)}, u32[]{:S(2)}, u32[]{:S(2)}) collective-permute-start(bf16[64,2048]{1,0:T(8,128)(2,1)S(1)} %get-tuple-element.59), channel_id=1, source_target_pairs={{0,4},{1,5},{2,6},{3,7},{4,0},{5,1},{6,2},{7,3},{8,12},{9,13},{10,... | collective-permute-start | bytes 786440 | tf_op jit(solution)/shard_map/ppermute | solution.py:480
  48.6 12.5 %collective-permute-start.4 = (bf16[64,2048]{1,0:T(8,128)(2,1)S(1)}, bf16[64,2048]{1,0:T(8,128)(2,1)S(1)}, u32[]{:S(2)}, u32[]{:S(2)}) collective-permute-start(bf16[64,2048]{1,0:T(8,128)(2,1)S(1)} %get-tuple-element.60), channel_id=1, source_target_pairs={{0,6},{1,7},{2,4},{3,5},{4,2},{5,3},{6,0},{7,1},{8,14},{9,15},{10,... | collective-permute-start | bytes 786440 | tf_op jit(solution)/shard_map/ppermute | solution.py:480
  53.7 7.5 %collective-permute-start.6 = (bf16[64,768]{1,0:T(8,128)(2,1)S(1)}, bf16[64,768]{1,0:T(8,128)(2,1)S(1)}, u32[]{:S(2)}, u32[]{:S(2)}) collective-permute-start(bf16[64,768]{1,0:T(8,128)(2,1)S(1)} %add_convert_fusion.2), channel_id=1, source_target_pairs={{0,16},{1,17},{2,18},{3,19},{4,20},{5,21},{6,22},{7,23},{8,24},{9,... | collective-permute-start | bytes 294920 | tf_op jit(solution)/shard_map/ppermute | solution.py:480
  61.3 5.5 %collective-permute-start.7 = (bf16[16,2048]{1,0:T(8,128)(2,1)S(1)}, bf16[16,2048]{1,0:T(8,128)(2,1)S(1)}, u32[]{:S(2)}, u32[]{:S(2)}) collective-permute-start(bf16[16,2048]{1,0:T(8,128)(2,1)S(1)} %get-tuple-element.83), channel_id=1, source_target_pairs={{0,8},{1,9},{2,10},{3,11},{4,12},{5,13},{6,14},{7,15},{8,0},{9,1},... | collective-permute-start | bytes 196616 | tf_op jit(solution)/shard_map/ppermute | solution.py:480
  62.8 6.2 %collective-permute-start.9 = (bf16[16,2048]{1,0:T(8,128)(2,1)S(1)}, bf16[16,2048]{1,0:T(8,128)(2,1)S(1)}, u32[]{:S(2)}, u32[]{:S(2)}) collective-permute-start(bf16[16,2048]{1,0:T(8,128)(2,1)S(1)} %get-tuple-element.84), channel_id=1, source_target_pairs={{0,24},{1,25},{2,26},{3,27},{4,28},{5,29},{6,30},{7,31},{8,16},{9,... | collective-permute-start | bytes 196616 | tf_op jit(solution)/shard_map/ppermute | solution.py:480
  63.6 6.7 %collective-permute-start.8 = (bf16[16,2048]{1,0:T(8,128)(2,1)S(1)}, bf16[16,2048]{1,0:T(8,128)(2,1)S(1)}, u32[]{:S(2)}, u32[]{:S(2)}) collective-permute-start(bf16[16,2048]{1,0:T(8,128)(2,1)S(1)} %get-tuple-element.85), channel_id=1, source_target_pairs={{0,16},{1,17},{2,18},{3,19},{4,20},{5,21},{6,22},{7,23},{8,24},{9,... | collective-permute-start | bytes 196616 | tf_op jit(solution)/shard_map/ppermute | solution.py:480
  64.9 10.0 %collective-permute-start.13 = (bf16[64,768]{1,0:T(8,128)(2,1)S(1)}, bf16[64,768]{1,0:T(8,128)(2,1)S(1)}, u32[]{:S(2)}, u32[]{:S(2)}) collective-permute-start(bf16[64,768]{1,0:T(8,128)(2,1)S(1)} %add_convert_fusion.1), channel_id=1, source_target_pairs={{0,4},{1,5},{2,6},{3,7},{4,0},{5,1},{6,2},{7,3},{8,12},{9,13},{10,... | collective-permute-start | bytes 294920 | tf_op jit(solution)/shard_map/ppermute | solution.py:480
  70.4 7.9 %collective-permute-start.12 = (bf16[16,2048]{1,0:T(8,128)(2,1)S(1)}, bf16[16,2048]{1,0:T(8,128)(2,1)S(1)}, u32[]{:S(2)}, u32[]{:S(2)}) collective-permute-start(bf16[16,2048]{1,0:T(8,128)(2,1)S(1)} %multiply_convert_fusion.1), channel_id=1, source_target_pairs={{0,24},{1,25},{2,26},{3,27},{4,28},{5,29},{6,30},{7,31},{8,16},{9,... | collective-permute-start | bytes 196616 | tf_op jit(solution)/shard_map/ppermute | solution.py:480
  72.1 6.2 %collective-permute-start.11 = (bf16[16,2048]{1,0:T(8,128)(2,1)S(1)}, bf16[16,2048]{1,0:T(8,128)(2,1)S(1)}, u32[]{:S(2)}, u32[]{:S(2)}) collective-permute-start(bf16[16,2048]{1,0:T(8,128)(2,1)S(1)} %multiply_convert_fusion.1), channel_id=1, source_target_pairs={{0,16},{1,17},{2,18},{3,19},{4,20},{5,21},{6,22},{7,23},{8,24},{9,... | collective-permute-start | bytes 196616 | tf_op jit(solution)/shard_map/ppermute | solution.py:480
  72.1 6.2 %collective-permute-start.10 = (bf16[16,2048]{1,0:T(8,128)(2,1)S(1)}, bf16[16,2048]{1,0:T(8,128)(2,1)S(1)}, u32[]{:S(2)}, u32[]{:S(2)}) collective-permute-start(bf16[16,2048]{1,0:T(8,128)(2,1)S(1)} %multiply_convert_fusion.1), channel_id=1, source_target_pairs={{0,8},{1,9},{2,10},{3,11},{4,12},{5,13},{6,14},{7,15},{8,0},{9,1},... | collective-permute-start | bytes 196616 | tf_op jit(solution)/shard_map/ppermute | solution.py:480
  74.9 6.6 %collective-permute-start.14 = (bf16[64,768]{1,0:T(8,128)(2,1)S(1)}, bf16[64,768]{1,0:T(8,128)(2,1)S(1)}, u32[]{:S(2)}, u32[]{:S(2)}) collective-permute-start(bf16[64,768]{1,0:T(8,128)(2,1)S(1)} %add_convert_fusion), channel_id=1, source_target_pairs={{0,2},{1,3},{2,0},{3,1},{4,6},{5,7},{6,4},{7,5},{8,10},{9,11},{10,... | collective-permute-start | bytes 294920 | tf_op jit(solution)/shard_map/ppermute | solution.py:480
  81.5 5.6 %collective-permute-start.18 = (bf16[64,768]{1,0:T(8,128)(2,1)S(1)}, bf16[64,768]{1,0:T(8,128)(2,1)S(1)}, u32[]{:S(2)}, u32[]{:S(2)}) collective-permute-start(bf16[64,768]{1,0:T(8,128)(2,1)S(1)} %multiply_convert_fusion), channel_id=1, source_target_pairs={{0,16},{1,17},{2,18},{3,19},{4,20},{5,21},{6,22},{7,23},{8,24},{9,... | collective-permute-start | bytes 294920 | tf_op jit(solution)/shard_map/ppermute | solution.py:480
  81.6 17.4 %collective-permute-start.17 = (bf16[64,2048]{1,0:T(8,128)(2,1)S(1)}, bf16[64,2048]{1,0:T(8,128)(2,1)S(1)}, u32[]{:S(2)}, u32[]{:S(2)}) collective-permute-start(bf16[64,2048]{1,0:T(8,128)(2,1)S(1)} %pad_maximum_fusion.1), channel_id=1, source_target_pairs={{0,6},{1,7},{2,4},{3,5},{4,2},{5,3},{6,0},{7,1},{8,14},{9,15},{10,... | collective-permute-start | bytes 786440 | tf_op jit(solution)/shard_map/ppermute | solution.py:480
  82.0 17.0 %collective-permute-start.16 = (bf16[64,2048]{1,0:T(8,128)(2,1)S(1)}, bf16[64,2048]{1,0:T(8,128)(2,1)S(1)}, u32[]{:S(2)}, u32[]{:S(2)}) collective-permute-start(bf16[64,2048]{1,0:T(8,128)(2,1)S(1)} %pad_maximum_fusion.1), channel_id=1, source_target_pairs={{0,4},{1,5},{2,6},{3,7},{4,0},{5,1},{6,2},{7,3},{8,12},{9,13},{10,... | collective-permute-start | bytes 786440 | tf_op jit(solution)/shard_map/ppermute | solution.py:480
  85.6 13.4 %collective-permute-start.15 = (bf16[64,2048]{1,0:T(8,128)(2,1)S(1)}, bf16[64,2048]{1,0:T(8,128)(2,1)S(1)}, u32[]{:S(2)}, u32[]{:S(2)}) collective-permute-start(bf16[64,2048]{1,0:T(8,128)(2,1)S(1)} %pad_maximum_fusion.1), channel_id=1, source_target_pairs={{0,2},{1,3},{2,0},{3,1},{4,6},{5,7},{6,4},{7,5},{8,10},{9,11},{10,... | collective-permute-start | bytes 786440 | tf_op jit(solution)/shard_map/ppermute | solution.py:480
  87.1 11.9 %all-to-all-start.2 = ((bf16[32,8,128]{2,1,0:T(8,128)(2,1)}), bf16[32,8,128]{2,1,0:T(8,128)(2,1)S(1)}, u32[]{:S(2)}, u32[]{:S(2)}) async-start(bf16[32,8,128]{2,1,0:T(8,128)(2,1)} %bitcast.7), calls=%async_computation.2 | async-start | bytes 131072 | tf_op jit(solution)/shard_map/all_to_all | solution.py:476
  90.8 8.1 %collective-permute-start.19 = (bf16[128,768]{1,0:T(8,128)(2,1)S(1)}, bf16[128,768]{1,0:T(8,128)(2,1)S(1)}, u32[]{:S(2)}, u32[]{:S(2)}) collective-permute-start(bf16[128,768]{1,0:T(8,128)(2,1)S(1)} %pad_maximum_fusion.2), channel_id=1, source_target_pairs={{0,8},{1,9},{2,10},{3,11},{4,12},{5,13},{6,14},{7,15},{8,0},{9,1},... | collective-permute-start | bytes 589832 | tf_op jit(solution)/shard_map/ppermute | solution.py:480
  99.1 3.3 %collective-permute-start.20 = (bf16[256,2048]{1,0:T(8,128)(2,1)S(1)}, bf16[256,2048]{1,0:T(8,128)(2,1)S(1)}, u32[]{:S(2)}, u32[]{:S(2)}) collective-permute-start(bf16[256,2048]{1,0:T(8,128)(2,1)S(1)} %constant_dynamic-update-slice_fusion.early_own), channel_id=1, source_target_pairs={{0,1},{1,0},{2,3},{3,2},{4,5},{5,4},{6,7},{7,6},{8,9},{9,8},{10,11... | collective-permute-start | bytes 3145736 | tf_op jit(solution)/shard_map/ppermute | solution.py:480
  99.2 3.2 %collective-permute-start.21 = (bf16[256,768]{1,0:T(8,128)(2,1)S(1)}, bf16[256,768]{1,0:T(8,128)(2,1)S(1)}, u32[]{:S(2)}, u32[]{:S(2)}) collective-permute-start(bf16[256,768]{1,0:T(8,128)(2,1)S(1)} %pad_maximum_fusion.late_own), channel_id=1, source_target_pairs={{0,1},{1,0},{2,3},{3,2},{4,5},{5,4},{6,7},{7,6},{8,9},{9,8},{10,11... | collective-permute-start | bytes 1179656 | tf_op jit(solution)/shard_map/ppermute | solution.py:480
where the time goes:
time: 106 us; the launch traced here: 105 us
  waiting for transfers between devices  35.3 us (33%)
  starting transfers between devices  31 us (29%)
  Pallas kernels  19 us (18%)
  blocking collectives  14.2 us (13%)
  local copies, waits for them, and re-layouts  4.6 us (4%)
    ppermute x22, waiting for transfers between devices, swap(): lax.ppermute(block, ('dp', 'rep'), [(i, i ^ mask) for i in range(count)])  27.9 us
    ppermute x22, starting transfers between devices, swap(): lax.ppermute(block, ('dp', 'rep'), [(i, i ^ mask) for i in range(count)])  24.7 us
    pallas_call x1, Pallas kernels, run_layer(): pl.pallas_call(layer_kernel, name='layer', out_shape=(shape((count, width...  14.5 us
    all_to_all x1, blocking collectives, exchange(): lax.all_to_all(blocks, ('dp', 'rep'), split_axis=0, concat_axis=0, tiled=...  14.2 us
    all_to_all x2, waiting for transfers between devices, exchange(): lax.all_to_all(blocks, ('dp', 'rep'), split_axis=0, concat_axis=0, tiled=...  7.4 us
    all_to_all x2, starting transfers between devices, exchange(): lax.all_to_all(blocks, ('dp', 'rep'), split_axis=0, concat_axis=0, tiled=...  6.27 us
    unnamed x11, local copies, waits for them, and re-layouts  3.81 us
    pallas_call x1, Pallas kernels, run_finish(): pl.pallas_call(finish_kernel, name='finish', out_shape=(shape((chosen.sha...  2.9 us
  transfers between devices with their start and end apart: 24, of which 12 were waited for; matrix products, arithmetic and copies ran while one was open for 0% of the time, Pallas kernels for 0%

commit v1 on v0

--- a/solution.py
+++ b/solution.py
@@ -126,20 +126,19 @@
     owned, width = table_ref.shape
     parts = width // BLOCK
     many = count * each * parts
+    spot = lax.broadcasted_iota(jnp.int32, (count, owned), 1)
     row = lax.broadcasted_iota(jnp.int32, (many, count), 0)
     device = lax.broadcasted_iota(jnp.int32, (many, count), 1)
-    own = zero_one(row // (each * parts) == device)
-    wanted = mm(own, asked_ref[...].astype(f32).astype(bf16)).astype(jnp.int32)
-    spot = lax.broadcasted_iota(jnp.int32, (many, owned), 1)
-    row = lax.broadcasted_iota(jnp.int32, (many, owned), 0)
-    found = jnp.zeros((many, owned), jnp.bool_)
+    chosen = jnp.zeros((many, owned), f32)
     for k in range(each):
-        here = jnp.logical_and(row // parts % each == k, spot == wanted[:, k : k + 1])
-        found = jnp.logical_or(found, here)
-    chosen_ref[...] = zero_one(found)
+        base = (device * each + k) * parts
+        here = zero_one(jnp.logical_and(row >= base, row < base + parts))
+        chosen = chosen + mm(here, zero_one(spot == asked_ref[:, k : k + 1]))
+    chosen_ref[...] = chosen.astype(bf16)
+    part_of = lax.broadcasted_iota(jnp.int32, (many, owned), 0) & (parts - 1)
     total = jnp.zeros((many, BLOCK), f32)
     for part in range(parts):
-        mine = zero_one(jnp.logical_and(found, row % parts == part))
+        mine = jnp.where(part_of == part, chosen, 0.0).astype(bf16)
         total = total + mm(mine, table_ref[:, part * BLOCK : (part + 1) * BLOCK])
     rows_ref[...] = total.astype(bf16)
 
@@ -395,10 +394,10 @@
             grads.at[half * leaves : (half + 1) * leaves, SPLIT + width :],
             leaf_hbm.at[:, half * (width // 2) : (half + 1) * (width // 2)],
         )
-    row = lax.broadcasted_iota(jnp.int32, chosen_ref.shape, 0)
     parts = width // BLOCK
+    part_of = lax.broadcasted_iota(jnp.int32, chosen_ref.shape, 0) & (parts - 1)
     for part in range(parts):
-        mine = jnp.where(row % parts == part, chosen_ref[...].astype(f32), 0.0).astype(bf16)
+        mine = jnp.where(part_of == part, chosen_ref[...].astype(f32), 0.0).astype(bf16)
         table[:, part * BLOCK : (part + 1) * BLOCK] = mm_tn(mine, returned_ref[...])
     leave(table, table_hbm)
     for low in range(0, SPLIT, width):
@@ -525,8 +524,11 @@
     late, *late_blocks = run_merge(late_own, late_other, 2 ** len(first))
     early_blocks, late_blocks = lax.optimization_barrier((early_blocks, late_blocks))
     early_got = swap_all(early_blocks, near, count)
-    late = split_up([late] + swap_all(late_blocks, first, count), second, count)
-    early_got, late = lax.optimization_barrier((early_got, late))
+    late = [late] + swap_all(late_blocks, first, count)
+    late_got = swap_all(shares(late, second), second, count)
+    early_got[0], late, d_rows = lax.optimization_barrier((early_got[0], late, d_rows))
+    returned = exchange(d_rows)
+    early_got, late = lax.optimization_barrier((early_got, extend(late, late_got)))
     early, late = split_up([early] + early_got, far, count), add(late).astype(bf16)
     late = sum_with(late, SHARED[0], count).astype(bf16)
     early, late = add(early), sum_with(late, SHARED[1], count)
@@ -537,10 +539,8 @@
     early = join((early * (1.0 / count)).astype(bf16), far, count)
     early, late = lax.optimization_barrier((early, (late * (1.0 / count)).astype(bf16)))
     pieces = swap_all([early] * (2 ** len(near) - 1), near, count)
-    late, d_rows = lax.optimization_barrier((join(late, second, count), d_rows))
-    returned = exchange(d_rows)
-    late = join(late, first, count)
-    pieces, late, returned = lax.optimization_barrier((pieces, late, returned))
+    late = join(join(late, second, count), first, count)
+    pieces, late = lax.optimization_barrier((pieces, late))
     early = jnp.concatenate([early] + pieces, axis=0)
     return returned, early, swap(early, 1, count), late, swap(late, 1, count)
 
@@ -554,7 +554,8 @@
     slot = event_slot.reshape(1, -1)
     leaf = leaf_ids.T
     asked = exchange(requests[0])
-    fetched, chosen = run_lookup(asked, item_table)
+    (table,) = run_load(item_table)
+    fetched, chosen = run_lookup(asked, table)
     arrived = exchange(fetched)
     output, d_rows, keep, send, keep_late, send_late = run_layer(
         me, lengths, slot, leaf, arrived, leaf_table, w_in, w_out, cotangent

time: 106 us -> 108 us (1.019)
  blocking collectives: 14.2 us -> 11 us
  waiting for transfers between devices: 35.3 us -> 38.4 us
  starting transfers between devices: 31 us -> 32.8 us
    all_to_all x2, waiting for transfers between devices: 7.4 us -> 13.6 us  [exchange(): lax.all_to_all(blocks, ('dp', 'rep'), split_axis=0, concat_axis=0, tiled=...]
    all_to_all x2, starting transfers between devices: 6.27 us -> 9.87 us  [exchange(): lax.all_to_all(blocks, ('dp', 'rep'), split_axis=0, concat_axis=0, tiled=...]
    all_to_all x1, blocking collectives: 14.2 us -> 11 us  [exchange(): lax.all_to_all(blocks, ('dp', 'rep'), split_axis=0, concat_axis=0, tiled=...]
    ppermute x22, waiting for transfers between devices: 27.9 us -> 24.8 us  [swap(): lax.ppermute(block, ('dp', 'rep'), [(i, i ^ mask) for i in range(count)])]
    ppermute x22, starting transfers between devices: 24.7 us -> 22.9 us  [swap(): lax.ppermute(block, ('dp', 'rep'), [(i, i ^ mask) for i in range(count)])]
    unnamed x11 -> x13, local copies, waits for them, and re-layouts: 3.81 us -> 3.81 us
where the time goes in v1:
time: 108 us
  waiting for transfers between devices  38.4 us (36%)
  starting transfers between devices  32.8 us (30%)
  Pallas kernels  18.9 us (17%)
  blocking collectives  11 us (10%)
  local copies, waits for them, and re-layouts  5.21 us (5%)
    ppermute x22, waiting for transfers between devices, swap(): lax.ppermute(block, ('dp', 'rep'), [(i, i ^ mask) for i in range(count)])  24.8 us
    ppermute x22, starting transfers between devices, swap(): lax.ppermute(block, ('dp', 'rep'), [(i, i ^ mask) for i in range(count)])  22.9 us
    pallas_call x1, Pallas kernels, run_layer(): pl.pallas_call(layer_kernel, name='layer', out_shape=(shape((count, width...  14.5 us
    all_to_all x2, waiting for transfers between devices, exchange(): lax.all_to_all(blocks, ('dp', 'rep'), split_axis=0, concat_axis=0, tiled=...  13.6 us
    all_to_all x1, blocking collectives, exchange(): lax.all_to_all(blocks, ('dp', 'rep'), split_axis=0, concat_axis=0, tiled=...  11 us
    all_to_all x2, starting transfers between devices, exchange(): lax.all_to_all(blocks, ('dp', 'rep'), split_axis=0, concat_axis=0, tiled=...  9.87 us
    unnamed x13, local copies, waits for them, and re-layouts  3.81 us
    pallas_call x1, Pallas kernels, run_finish(): pl.pallas_call(finish_kernel, name='finish', out_shape=(shape((chosen.sha...  2.9 us
  transfers between devices with their start and end apart: 24, of which 12 were waited for; matrix products, arithmetic and copies ran while one was open for 0% of the time, Pallas kernels for 0%

profile of v1, /device:TPU:0, one launch (start us, length us, event | category | flops | bytes accessed | tf_op | source)
XLA Modules:
  0.0 107.5 jit_solution(3815319545660967386)
XLA Ops:
  0.6 1.4 %copy.15 = s32[32,1,2]{2,1,0:T(1,128)} copy(s32[32,1,2]{0,2,1:T(2,128)} %bitcast.13) | data formatting | bytes 512 | tf_op jit(solution)/shard_map/all_to_all | solution.py:475
  2.0 7.3 %all-to-all-start = ((s32[32,1,2]{2,1,0:T(1,128)}), s32[32,1,2]{2,1,0:T(1,128)S(1)}, u32[]{:S(2)}, u32[]{:S(2)}) async-start(s32[32,1,2]{2,1,0:T(1,128)} %copy.15), calls=%async_computation | async-start | bytes 32768 | tf_op jit(solution)/shard_map/all_to_all | solution.py:475
  9.3 0.9 copy-done.2
  10.2 6.2 %all-to-all-done = s32[32,1,2]{2,1,0:T(1,128)S(1)} async-done(((s32[32,1,2]{2,1,0:T(1,128)}), s32[32,1,2]{2,1,0:T(1,128)S(1)}, u32[]{:S(2)}, u32[]{:S(2)}) %all-to-all-start) | async-done | bytes 288 | tf_op jit(solution)/shard_map/all_to_all | solution.py:475
  16.4 1.1 %lookup.1 = (bf16[256,128]{1,0:T(8,128)(2,1)}, bf16[256,128]{1,0:T(8,128)(2,1)S(1)}) custom-call(s32[32,2]{1,0:T(8,128)S(1)} %bitcast.10, bf16[128,512]{1,0:T(8,128)(2,1)S(1)} %load.2.table_ref), custom_call_target="tpu_custom_call" | custom-call | tf_op jit(solution)/shard_map/lookup/pallas_call | solution.py:150
  17.5 2.6 %all-to-all-start.1 = ((bf16[32,8,128]{2,1,0:T(8,128)(2,1)}), bf16[32,8,128]{2,1,0:T(8,128)(2,1)S(1)}, u32[]{:S(2)}, u32[]{:S(2)}) async-start(bf16[32,8,128]{2,1,0:T(8,128)(2,1)} %bitcast.5), calls=%async_computation.1 | async-start | bytes 131072 | tf_op jit(solution)/shard_map/all_to_all | solution.py:475
  20.1 7.4 %all-to-all-done.1 = bf16[32,8,128]{2,1,0:T(8,128)(2,1)S(1)} async-done(((bf16[32,8,128]{2,1,0:T(8,128)(2,1)}), bf16[32,8,128]{2,1,0:T(8,128)(2,1)S(1)}, u32[]{:S(2)}, u32[]{:S(2)}) %all-to-all-start.1) | async-done | bytes 65568 | tf_op jit(solution)/shard_map/all_to_all | solution.py:475
  27.5 0.6 copy-done.4
  28.1 14.5 %layer.1 = (bf16[512,512]{1,0:T(8,128)(2,1)}, bf16[256,128]{1,0:T(8,128)(2,1)}, bf16[256,2048]{1,0:T(8,128)(2,1)}, bf16[256,2048]{1,0:T(8,128)(2,1)}, bf16[256,7...) custom-call(s32[1]{0:T(128)} %bitcast.me_ref, s32[1,4]{1,0:T(1,128)} %lengths_ref.1, s32[1,512]{1,0:T(1,128)} %bitcast.15, ...), custom_call_target="tpu_custom_call" | custom-call | flops 6000000000 | bytes 10000000 | tf_op jit(solution)/shard_map/layer/pallas_call | solution.py:315
  42.6 0.2 collective-permute-start
  42.8 0.4 collective-permute-start.1
  43.2 1.2 %copy-done = bf16[256,2048]{1,0:T(8,128)(2,1)S(1)} copy-done((bf16[256,2048]{1,0:T(8,128)(2,1)S(1)}, bf16[256,2048]{1,0:T(8,128)(2,1)}, u32[]{:S(2)}) %copy-start) | copy-done | bytes 1048600
  44.4 1.0 copy-done.1
  45.4 0.1 load.3
  45.5 0.6 collective-permute-done.1.other_ref
  46.1 0.1 merge.3
  46.2 0.2 merge.2
  46.5 0.7 collective-permute-start.3
  47.1 0.4 collective-permute-start.2
  47.6 0.9 collective-permute-start.4
  48.4 2.2 %collective-permute-start.5 = (bf16[64,2048]{1,0:T(8,128)(2,1)S(1)}, bf16[64,2048]{1,0:T(8,128)(2,1)S(1)}, u32[]{:S(2)}, u32[]{:S(2)}) collective-permute-start(bf16[64,2048]{1,0:T(8,128)(2,1)S(1)} %get-tuple-element.66), channel_id=1, source_target_pairs={{0,6},{1,7},{2,4},{3,5},{4,2},{5,3},{6,0},{7,1},{8,14},{9,15},{10,... | collective-permute-start | bytes 786440 | tf_op jit(solution)/shard_map/ppermute | solution.py:479
  50.6 2.9 %collective-permute-done.3 = bf16[128,768]{1,0:T(8,128)(2,1)S(1)} collective-permute-done((bf16[128,768]{1,0:T(8,128)(2,1)S(1)}, bf16[128,768]{1,0:T(8,128)(2,1)S(1)}, u32[]{:S(2)}, u32[]{:S(2)}) %collective-permute-start.3) | collective-permute-done | bytes 196640 | tf_op jit(solution)/shard_map/ppermute | solution.py:479
  53.5 0.7 collective-permute-start.6
  54.2 2.1 %collective-permute-done.2 = bf16[64,2048]{1,0:T(8,128)(2,1)S(1)} collective-permute-done((bf16[64,2048]{1,0:T(8,128)(2,1)S(1)}, bf16[64,2048]{1,0:T(8,128)(2,1)S(1)}, u32[]{:S(2)}, u32[]{:S(2)}) %collective-permute-start.2) | collective-permute-done | bytes 262176 | tf_op jit(solution)/shard_map/ppermute | solution.py:479
  56.4 4.6 %collective-permute-done.4 = bf16[64,2048]{1,0:T(8,128)(2,1)S(1)} collective-permute-done((bf16[64,2048]{1,0:T(8,128)(2,1)S(1)}, bf16[64,2048]{1,0:T(8,128)(2,1)S(1)}, u32[]{:S(2)}, u32[]{:S(2)}) %collective-permute-start.4) | collective-permute-done | bytes 262176 | tf_op jit(solution)/shard_map/ppermute | solution.py:479
  61.0 0.1 add_convert_fusion.5
  61.1 1.5 %collective-permute-start.7 = (bf16[16,2048]{1,0:T(8,128)(2,1)S(1)}, bf16[16,2048]{1,0:T(8,128)(2,1)S(1)}, u32[]{:S(2)}, u32[]{:S(2)}) collective-permute-start(bf16[16,2048]{1,0:T(8,128)(2,1)S(1)} %get-tuple-element.85), channel_id=1, source_target_pairs={{0,8},{1,9},{2,10},{3,11},{4,12},{5,13},{6,14},{7,15},{8,0},{9,1},... | collective-permute-start | bytes 196616 | tf_op jit(solution)/shard_map/ppermute | solution.py:479
  62.6 0.9 collective-permute-start.9
  63.4 1.2 %collective-permute-start.8 = (bf16[16,2048]{1,0:T(8,128)(2,1)S(1)}, bf16[16,2048]{1,0:T(8,128)(2,1)S(1)}, u32[]{:S(2)}, u32[]{:S(2)}) collective-permute-start(bf16[16,2048]{1,0:T(8,128)(2,1)S(1)} %get-tuple-element.87), channel_id=1, source_target_pairs={{0,16},{1,17},{2,18},{3,19},{4,20},{5,21},{6,22},{7,23},{8,24},{9,... | collective-permute-start | bytes 196616 | tf_op jit(solution)/shard_map/ppermute | solution.py:479
  64.7 1.4 %collective-permute-start.13 = (bf16[64,768]{1,0:T(8,128)(2,1)S(1)}, bf16[64,768]{1,0:T(8,128)(2,1)S(1)}, u32[]{:S(2)}, u32[]{:S(2)}) collective-permute-start(bf16[64,768]{1,0:T(8,128)(2,1)S(1)} %add_convert_fusion.1), channel_id=1, source_target_pairs={{0,4},{1,5},{2,6},{3,7},{4,0},{5,1},{6,2},{7,3},{8,12},{9,13},{10,... | collective-permute-start | bytes 294920 | tf_op jit(solution)/shard_map/ppermute | solution.py:479
  66.1 0.5 collective-permute-done.7
  66.6 2.1 %collective-permute-done.9 = bf16[16,2048]{1,0:T(8,128)(2,1)S(1)} collective-permute-done((bf16[16,2048]{1,0:T(8,128)(2,1)S(1)}, bf16[16,2048]{1,0:T(8,128)(2,1)S(1)}, u32[]{:S(2)}, u32[]{:S(2)}) %collective-permute-start.9) | collective-permute-done | bytes 65568 | tf_op jit(solution)/shard_map/ppermute | solution.py:479
  68.7 1.4 %collective-permute-done.8 = bf16[16,2048]{1,0:T(8,128)(2,1)S(1)} collective-permute-done((bf16[16,2048]{1,0:T(8,128)(2,1)S(1)}, bf16[16,2048]{1,0:T(8,128)(2,1)S(1)}, u32[]{:S(2)}, u32[]{:S(2)}) %collective-permute-start.8) | collective-permute-done | bytes 65568 | tf_op jit(solution)/shard_map/ppermute | solution.py:479
  70.2 0.1 multiply_convert_fusion.1
  70.2 1.7 %collective-permute-start.12 = (bf16[16,2048]{1,0:T(8,128)(2,1)S(1)}, bf16[16,2048]{1,0:T(8,128)(2,1)S(1)}, u32[]{:S(2)}, u32[]{:S(2)}) collective-permute-start(bf16[16,2048]{1,0:T(8,128)(2,1)S(1)} %multiply_convert_fusion.1), channel_id=1, source_target_pairs={{0,24},{1,25},{2,26},{3,27},{4,28},{5,29},{6,30},{7,31},{8,16},{9,... | collective-permute-start | bytes 196616 | tf_op jit(solution)/shard_map/ppermute | solution.py:479
  71.9 2.8 %collective-permute-start.10 = (bf16[16,2048]{1,0:T(8,128)(2,1)S(1)}, bf16[16,2048]{1,0:T(8,128)(2,1)S(1)}, u32[]{:S(2)}, u32[]{:S(2)}) collective-permute-start(bf16[16,2048]{1,0:T(8,128)(2,1)S(1)} %multiply_convert_fusion.1), channel_id=1, source_target_pairs={{0,8},{1,9},{2,10},{3,11},{4,12},{5,13},{6,14},{7,15},{8,0},{9,1},... | collective-permute-start | bytes 196616 | tf_op jit(solution)/shard_map/ppermute | solution.py:479
  74.7 3.4 %collective-permute-start.14 = (bf16[64,768]{1,0:T(8,128)(2,1)S(1)}, bf16[64,768]{1,0:T(8,128)(2,1)S(1)}, u32[]{:S(2)}, u32[]{:S(2)}) collective-permute-start(bf16[64,768]{1,0:T(8,128)(2,1)S(1)} %add_convert_fusion), channel_id=1, source_target_pairs={{0,2},{1,3},{2,0},{3,1},{4,6},{5,7},{6,4},{7,5},{8,10},{9,11},{10,... | collective-permute-start | bytes 294920 | tf_op jit(solution)/shard_map/ppermute | solution.py:479
  78.2 3.2 %collective-permute-done.14 = bf16[64,768]{1,0:T(8,128)(2,1)S(1)} collective-permute-done((bf16[64,768]{1,0:T(8,128)(2,1)S(1)}, bf16[64,768]{1,0:T(8,128)(2,1)S(1)}, u32[]{:S(2)}, u32[]{:S(2)}) %collective-permute-start.14) | collective-permute-done | bytes 98336 | tf_op jit(solution)/shard_map/ppermute | solution.py:479
  81.4 0.1 collective-permute-start.18
  81.4 0.4 collective-permute-start.17
  81.9 3.6 %collective-permute-start.16 = (bf16[64,2048]{1,0:T(8,128)(2,1)S(1)}, bf16[64,2048]{1,0:T(8,128)(2,1)S(1)}, u32[]{:S(2)}, u32[]{:S(2)}) collective-permute-start(bf16[64,2048]{1,0:T(8,128)(2,1)S(1)} %pad_maximum_fusion.1), channel_id=1, source_target_pairs={{0,4},{1,5},{2,6},{3,7},{4,0},{5,1},{6,2},{7,3},{8,12},{9,13},{10,... | collective-permute-start | bytes 786440 | tf_op jit(solution)/shard_map/ppermute | solution.py:479
  85.4 1.7 %collective-permute-done.18 = bf16[64,768]{1,0:T(8,128)(2,1)S(1)} collective-permute-done((bf16[64,768]{1,0:T(8,128)(2,1)S(1)}, bf16[64,768]{1,0:T(8,128)(2,1)S(1)}, u32[]{:S(2)}, u32[]{:S(2)}) %collective-permute-start.18) | collective-permute-done | bytes 98336 | tf_op jit(solution)/shard_map/ppermute | solution.py:479
  87.2 0.1 collective-permute-start.19
  87.3 5.6 %collective-permute-done.19 = bf16[128,768]{1,0:T(8,128)(2,1)S(1)} collective-permute-done((bf16[128,768]{1,0:T(8,128)(2,1)S(1)}, bf16[128,768]{1,0:T(8,128)(2,1)S(1)}, u32[]{:S(2)}, u32[]{:S(2)}) %collective-permute-start.19) | collective-permute-done | bytes 196640 | tf_op jit(solution)/shard_map/ppermute | solution.py:479
  93.1 0.1 collective-permute-start.20
  93.2 0.5 collective-permute-start.21
  93.7 11.0 %all_to_all.33 = bf16[32,8,128]{2,1,0:T(8,128)(2,1)S(1)} all-to-all(bf16[32,8,128]{2,1,0:T(8,128)(2,1)S(1)} %bitcast.11), channel_id=1, replica_groups=mesh['dp'=8,'rep'=4] {'dp','rep'}, dimensions={0} | all-to-all | bytes 131072 | tf_op jit(solution)/shard_map/all_to_all | solution.py:475
  104.6 2.9 %finish.1 = (f32[128,512]{1,0:T(8,128)}, f32[256,512]{1,0:T(8,128)}, f32[512,2048]{1,0:T(8,128)}, f32[512,512]{1,0:T(8,128)}) custom-call(s32[1]{0:T(128)} %bitcast.me_ref, bf16[256,128]{1,0:T(8,128)(2,1)S(1)} %get-tuple-element.47.chosen_ref, bf16[256,128]{1,0:T(8,128)(2,1)S(1)} %bitcast.9, ...), custom_call_target="tpu_custom_call" | custom-call | tf_op jit(solution)/shard_map/finish/pallas_call | solution.py:416
  (34 shorter events, 0.3 us)
Async XLA Ops:
  2.0 14.4 %all-to-all-start = ((s32[32,1,2]{2,1,0:T(1,128)}), s32[32,1,2]{2,1,0:T(1,128)S(1)}, u32[]{:S(2)}, u32[]{:S(2)}) async-start(s32[32,1,2]{2,1,0:T(1,128)} %copy.15), calls=%async_computation | async-start | bytes 32768 | tf_op jit(solution)/shard_map/all_to_all | solution.py:475
  9.3 0.9 copy-start.2
  17.5 10.0 %all-to-all-start.1 = ((bf16[32,8,128]{2,1,0:T(8,128)(2,1)}), bf16[32,8,128]{2,1,0:T(8,128)(2,1)S(1)}, u32[]{:S(2)}, u32[]{:S(2)}) async-start(bf16[32,8,128]{2,1,0:T(8,128)(2,1)} %bitcast.5), calls=%async_computation.1 | async-start | bytes 131072 | tf_op jit(solution)/shard_map/all_to_all | solution.py:475
  27.5 0.6 copy-start.4
  42.6 3.6 %collective-permute-start = (bf16[256,2048]{1,0:T(8,128)(2,1)}, bf16[256,2048]{1,0:T(8,128)(2,1)S(1)}, u32[]{:S(2)}, u32[]{:S(2)}) collective-permute-start(bf16[256,2048]{1,0:T(8,128)(2,1)} %get-tuple-element.51), channel_id=1, source_target_pairs={{0,1},{1,0},{2,3},{3,2},{4,5},{5,4},{6,7},{7,6},{8,9},{9,8},{10,11... | collective-permute-start | bytes 3145736 | tf_op jit(solution)/shard_map/ppermute | solution.py:479
  42.8 3.3 %collective-permute-start.1 = (bf16[256,768]{1,0:T(8,128)(2,1)}, bf16[256,768]{1,0:T(8,128)(2,1)S(1)}, u32[]{:S(2)}, u32[]{:S(2)}) collective-permute-start(bf16[256,768]{1,0:T(8,128)(2,1)} %get-tuple-element.56), channel_id=1, source_target_pairs={{0,1},{1,0},{2,3},{3,2},{4,5},{5,4},{6,7},{7,6},{8,9},{9,8},{10,11... | collective-permute-start | bytes 1179656 | tf_op jit(solution)/shard_map/ppermute | solution.py:479
  43.2 1.2 %copy-start = (bf16[256,2048]{1,0:T(8,128)(2,1)S(1)}, bf16[256,2048]{1,0:T(8,128)(2,1)}, u32[]{:S(2)}) copy-start(bf16[256,2048]{1,0:T(8,128)(2,1)} %get-tuple-element.48.refs_0_) | copy-start | bytes 3145732
  44.4 1.0 copy-start.1
  46.2 47.4 %copy-start.3 = (bf16[256,128]{1,0:T(8,128)(2,1)S(1)}, bf16[256,128]{1,0:T(8,128)(2,1)}, u32[]{:S(2)}) copy-start(bf16[256,128]{1,0:T(8,128)(2,1)} %get-tuple-element.62) | copy-start | bytes 196612
  46.5 7.0 %collective-permute-start.3 = (bf16[128,768]{1,0:T(8,128)(2,1)S(1)}, bf16[128,768]{1,0:T(8,128)(2,1)S(1)}, u32[]{:S(2)}, u32[]{:S(2)}) collective-permute-start(bf16[128,768]{1,0:T(8,128)(2,1)S(1)} %get-tuple-element.60), channel_id=1, source_target_pairs={{0,8},{1,9},{2,10},{3,11},{4,12},{5,13},{6,14},{7,15},{8,0},{9,1},... | collective-permute-start | bytes 589832 | tf_op jit(solution)/shard_map/ppermute | solution.py:479
  47.1 9.2 %collective-permute-start.2 = (bf16[64,2048]{1,0:T(8,128)(2,1)S(1)}, bf16[64,2048]{1,0:T(8,128)(2,1)S(1)}, u32[]{:S(2)}, u32[]{:S(2)}) collective-permute-start(bf16[64,2048]{1,0:T(8,128)(2,1)S(1)} %get-tuple-element.58), channel_id=1, source_target_pairs={{0,2},{1,3},{2,0},{3,1},{4,6},{5,7},{6,4},{7,5},{8,10},{9,11},{10,... | collective-permute-start | bytes 786440 | tf_op jit(solution)/shard_map/ppermute | solution.py:479
  47.6 13.4 %collective-permute-start.4 = (bf16[64,2048]{1,0:T(8,128)(2,1)S(1)}, bf16[64,2048]{1,0:T(8,128)(2,1)S(1)}, u32[]{:S(2)}, u32[]{:S(2)}) collective-permute-start(bf16[64,2048]{1,0:T(8,128)(2,1)S(1)} %get-tuple-element.65), channel_id=1, source_target_pairs={{0,4},{1,5},{2,6},{3,7},{4,0},{5,1},{6,2},{7,3},{8,12},{9,13},{10,... | collective-permute-start | bytes 786440 | tf_op jit(solution)/shard_map/ppermute | solution.py:479
  48.4 12.5 %collective-permute-start.5 = (bf16[64,2048]{1,0:T(8,128)(2,1)S(1)}, bf16[64,2048]{1,0:T(8,128)(2,1)S(1)}, u32[]{:S(2)}, u32[]{:S(2)}) collective-permute-start(bf16[64,2048]{1,0:T(8,128)(2,1)S(1)} %get-tuple-element.66), channel_id=1, source_target_pairs={{0,6},{1,7},{2,4},{3,5},{4,2},{5,3},{6,0},{7,1},{8,14},{9,15},{10,... | collective-permute-start | bytes 786440 | tf_op jit(solution)/shard_map/ppermute | solution.py:479
  53.5 7.5 %collective-permute-start.6 = (bf16[64,768]{1,0:T(8,128)(2,1)S(1)}, bf16[64,768]{1,0:T(8,128)(2,1)S(1)}, u32[]{:S(2)}, u32[]{:S(2)}) collective-permute-start(bf16[64,768]{1,0:T(8,128)(2,1)S(1)} %add_convert_fusion.2), channel_id=1, source_target_pairs={{0,16},{1,17},{2,18},{3,19},{4,20},{5,21},{6,22},{7,23},{8,24},{9,... | collective-permute-start | bytes 294920 | tf_op jit(solution)/shard_map/ppermute | solution.py:479
  61.1 5.5 %collective-permute-start.7 = (bf16[16,2048]{1,0:T(8,128)(2,1)S(1)}, bf16[16,2048]{1,0:T(8,128)(2,1)S(1)}, u32[]{:S(2)}, u32[]{:S(2)}) collective-permute-start(bf16[16,2048]{1,0:T(8,128)(2,1)S(1)} %get-tuple-element.85), channel_id=1, source_target_pairs={{0,8},{1,9},{2,10},{3,11},{4,12},{5,13},{6,14},{7,15},{8,0},{9,1},... | collective-permute-start | bytes 196616 | tf_op jit(solution)/shard_map/ppermute | solution.py:479
  62.6 6.2 %collective-permute-start.9 = (bf16[16,2048]{1,0:T(8,128)(2,1)S(1)}, bf16[16,2048]{1,0:T(8,128)(2,1)S(1)}, u32[]{:S(2)}, u32[]{:S(2)}) collective-permute-start(bf16[16,2048]{1,0:T(8,128)(2,1)S(1)} %get-tuple-element.86), channel_id=1, source_target_pairs={{0,24},{1,25},{2,26},{3,27},{4,28},{5,29},{6,30},{7,31},{8,16},{9,... | collective-permute-start | bytes 196616 | tf_op jit(solution)/shard_map/ppermute | solution.py:479
  63.4 6.7 %collective-permute-start.8 = (bf16[16,2048]{1,0:T(8,128)(2,1)S(1)}, bf16[16,2048]{1,0:T(8,128)(2,1)S(1)}, u32[]{:S(2)}, u32[]{:S(2)}) collective-permute-start(bf16[16,2048]{1,0:T(8,128)(2,1)S(1)} %get-tuple-element.87), channel_id=1, source_target_pairs={{0,16},{1,17},{2,18},{3,19},{4,20},{5,21},{6,22},{7,23},{8,24},{9,... | collective-permute-start | bytes 196616 | tf_op jit(solution)/shard_map/ppermute | solution.py:479
  64.7 10.0 %collective-permute-start.13 = (bf16[64,768]{1,0:T(8,128)(2,1)S(1)}, bf16[64,768]{1,0:T(8,128)(2,1)S(1)}, u32[]{:S(2)}, u32[]{:S(2)}) collective-permute-start(bf16[64,768]{1,0:T(8,128)(2,1)S(1)} %add_convert_fusion.1), channel_id=1, source_target_pairs={{0,4},{1,5},{2,6},{3,7},{4,0},{5,1},{6,2},{7,3},{8,12},{9,13},{10,... | collective-permute-start | bytes 294920 | tf_op jit(solution)/shard_map/ppermute | solution.py:479
  70.2 7.9 %collective-permute-start.12 = (bf16[16,2048]{1,0:T(8,128)(2,1)S(1)}, bf16[16,2048]{1,0:T(8,128)(2,1)S(1)}, u32[]{:S(2)}, u32[]{:S(2)}) collective-permute-start(bf16[16,2048]{1,0:T(8,128)(2,1)S(1)} %multiply_convert_fusion.1), channel_id=1, source_target_pairs={{0,24},{1,25},{2,26},{3,27},{4,28},{5,29},{6,30},{7,31},{8,16},{9,... | collective-permute-start | bytes 196616 | tf_op jit(solution)/shard_map/ppermute | solution.py:479
  71.9 6.2 %collective-permute-start.11 = (bf16[16,2048]{1,0:T(8,128)(2,1)S(1)}, bf16[16,2048]{1,0:T(8,128)(2,1)S(1)}, u32[]{:S(2)}, u32[]{:S(2)}) collective-permute-start(bf16[16,2048]{1,0:T(8,128)(2,1)S(1)} %multiply_convert_fusion.1), channel_id=1, source_target_pairs={{0,16},{1,17},{2,18},{3,19},{4,20},{5,21},{6,22},{7,23},{8,24},{9,... | collective-permute-start | bytes 196616 | tf_op jit(solution)/shard_map/ppermute | solution.py:479
  71.9 6.2 %collective-permute-start.10 = (bf16[16,2048]{1,0:T(8,128)(2,1)S(1)}, bf16[16,2048]{1,0:T(8,128)(2,1)S(1)}, u32[]{:S(2)}, u32[]{:S(2)}) collective-permute-start(bf16[16,2048]{1,0:T(8,128)(2,1)S(1)} %multiply_convert_fusion.1), channel_id=1, source_target_pairs={{0,8},{1,9},{2,10},{3,11},{4,12},{5,13},{6,14},{7,15},{8,0},{9,1},... | collective-permute-start | bytes 196616 | tf_op jit(solution)/shard_map/ppermute | solution.py:479
  74.7 6.6 %collective-permute-start.14 = (bf16[64,768]{1,0:T(8,128)(2,1)S(1)}, bf16[64,768]{1,0:T(8,128)(2,1)S(1)}, u32[]{:S(2)}, u32[]{:S(2)}) collective-permute-start(bf16[64,768]{1,0:T(8,128)(2,1)S(1)} %add_convert_fusion), channel_id=1, source_target_pairs={{0,2},{1,3},{2,0},{3,1},{4,6},{5,7},{6,4},{7,5},{8,10},{9,11},{10,... | collective-permute-start | bytes 294920 | tf_op jit(solution)/shard_map/ppermute | solution.py:479
  81.4 5.8 %collective-permute-start.18 = (bf16[64,768]{1,0:T(8,128)(2,1)S(1)}, bf16[64,768]{1,0:T(8,128)(2,1)S(1)}, u32[]{:S(2)}, u32[]{:S(2)}) collective-permute-start(bf16[64,768]{1,0:T(8,128)(2,1)S(1)} %multiply_convert_fusion), channel_id=1, source_target_pairs={{0,16},{1,17},{2,18},{3,19},{4,20},{5,21},{6,22},{7,23},{8,24},{9,... | collective-permute-start | bytes 294920 | tf_op jit(solution)/shard_map/ppermute | solution.py:479
  81.4 11.5 %collective-permute-start.17 = (bf16[64,2048]{1,0:T(8,128)(2,1)S(1)}, bf16[64,2048]{1,0:T(8,128)(2,1)S(1)}, u32[]{:S(2)}, u32[]{:S(2)}) collective-permute-start(bf16[64,2048]{1,0:T(8,128)(2,1)S(1)} %pad_maximum_fusion.1), channel_id=1, source_target_pairs={{0,6},{1,7},{2,4},{3,5},{4,2},{5,3},{6,0},{7,1},{8,14},{9,15},{10,... | collective-permute-start | bytes 786440 | tf_op jit(solution)/shard_map/ppermute | solution.py:479
  81.9 11.1 %collective-permute-start.16 = (bf16[64,2048]{1,0:T(8,128)(2,1)S(1)}, bf16[64,2048]{1,0:T(8,128)(2,1)S(1)}, u32[]{:S(2)}, u32[]{:S(2)}) collective-permute-start(bf16[64,2048]{1,0:T(8,128)(2,1)S(1)} %pad_maximum_fusion.1), channel_id=1, source_target_pairs={{0,4},{1,5},{2,6},{3,7},{4,0},{5,1},{6,2},{7,3},{8,12},{9,13},{10,... | collective-permute-start | bytes 786440 | tf_op jit(solution)/shard_map/ppermute | solution.py:479
  85.4 7.5 %collective-permute-start.15 = (bf16[64,2048]{1,0:T(8,128)(2,1)S(1)}, bf16[64,2048]{1,0:T(8,128)(2,1)S(1)}, u32[]{:S(2)}, u32[]{:S(2)}) collective-permute-start(bf16[64,2048]{1,0:T(8,128)(2,1)S(1)} %pad_maximum_fusion.1), channel_id=1, source_target_pairs={{0,2},{1,3},{2,0},{3,1},{4,6},{5,7},{6,4},{7,5},{8,10},{9,11},{10,... | collective-permute-start | bytes 786440 | tf_op jit(solution)/shard_map/ppermute | solution.py:479
  87.2 5.7 %collective-permute-start.19 = (bf16[128,768]{1,0:T(8,128)(2,1)S(1)}, bf16[128,768]{1,0:T(8,128)(2,1)S(1)}, u32[]{:S(2)}, u32[]{:S(2)}) collective-permute-start(bf16[128,768]{1,0:T(8,128)(2,1)S(1)} %pad_maximum_fusion.2), channel_id=1, source_target_pairs={{0,8},{1,9},{2,10},{3,11},{4,12},{5,13},{6,14},{7,15},{8,0},{9,1},... | collective-permute-start | bytes 589832 | tf_op jit(solution)/shard_map/ppermute | solution.py:479
  93.1 11.5 %collective-permute-start.20 = (bf16[256,2048]{1,0:T(8,128)(2,1)S(1)}, bf16[256,2048]{1,0:T(8,128)(2,1)S(1)}, u32[]{:S(2)}, u32[]{:S(2)}) collective-permute-start(bf16[256,2048]{1,0:T(8,128)(2,1)S(1)} %constant_dynamic-update-slice_fusion.early_own), channel_id=1, source_target_pairs={{0,1},{1,0},{2,3},{3,2},{4,5},{5,4},{6,7},{7,6},{8,9},{9,8},{10,11... | collective-permute-start | bytes 3145736 | tf_op jit(solution)/shard_map/ppermute | solution.py:479
  93.2 11.5 %collective-permute-start.21 = (bf16[256,768]{1,0:T(8,128)(2,1)S(1)}, bf16[256,768]{1,0:T(8,128)(2,1)S(1)}, u32[]{:S(2)}, u32[]{:S(2)}) collective-permute-start(bf16[256,768]{1,0:T(8,128)(2,1)S(1)} %pad_maximum_fusion.late_own), channel_id=1, source_target_pairs={{0,1},{1,0},{2,3},{3,2},{4,5},{5,4},{6,7},{7,6},{8,9},{9,8},{10,11... | collective-permute-start | bytes 1179656 | tf_op jit(solution)/shard_map/ppermute | solution.py:479

commit v2 on v1

--- a/solution.py
+++ b/solution.py
@@ -536,7 +536,8 @@
     while reach < count:
         early, late = early + swap(early, reach, count), late + swap(late, reach, count)
         reach *= 2
-    early = join((early * (1.0 / count)).astype(bf16), far, count)
+    early, returned = lax.optimization_barrier(((early * (1.0 / count)).astype(bf16), returned))
+    early = join(early, far, count)
     early, late = lax.optimization_barrier((early, (late * (1.0 / count)).astype(bf16)))
     pieces = swap_all([early] * (2 ** len(near) - 1), near, count)
     late = join(join(late, second, count), first, count)

time: 108 us -> 101 us (0.935)
  blocking collectives: 11 us -> 0 us
  waiting for transfers between devices: 38.4 us -> 41.7 us
    all_to_all x1 -> x0, blocking collectives: 11 us -> none  [exchange(): lax.all_to_all(blocks, ('dp', 'rep'), split_axis=0, concat_axis=0, tiled=...]
    ppermute x22, waiting for transfers between devices: 24.8 us -> 28.1 us  [swap(): lax.ppermute(block, ('dp', 'rep'), [(i, i ^ mask) for i in range(count)])]
    all_to_all x2 -> x3, starting transfers between devices: 9.87 us -> 12.4 us  [exchange(): lax.all_to_all(blocks, ('dp', 'rep'), split_axis=0, concat_axis=0, tiled=...]
    ppermute x22, starting transfers between devices: 22.9 us -> 20.8 us  [swap(): lax.ppermute(block, ('dp', 'rep'), [(i, i ^ mask) for i in range(count)])]
    unnamed x13 -> x11, local copies, waits for them, and re-layouts: 3.81 us -> 3.8 us
    all_to_all x2 -> x3, waiting for transfers between devices: 13.6 us -> 13.6 us  [exchange(): lax.all_to_all(blocks, ('dp', 'rep'), split_axis=0, concat_axis=0, tiled=...]
  transfers between devices with their start and end apart: 24 -> 25, of which waited for: 12 -> 16; matrix products, arithmetic and copies ran while one was open for 0% -> 0% of each run, Pallas kernels for 0% -> 0%
where the time goes in v2:
time: 101 us; the launch traced here: 100 us
  waiting for transfers between devices  41.7 us (41%)
  starting transfers between devices  33.2 us (33%)
  Pallas kernels  18.9 us (19%)
  local copies, waits for them, and re-layouts  5.2 us (5%)
    ppermute x22, waiting for transfers between devices, swap(): lax.ppermute(block, ('dp', 'rep'), [(i, i ^ mask) for i in range(count)])  28.1 us
    ppermute x22, starting transfers between devices, swap(): lax.ppermute(block, ('dp', 'rep'), [(i, i ^ mask) for i in range(count)])  20.8 us
    pallas_call x1, Pallas kernels, run_layer(): pl.pallas_call(layer_kernel, name='layer', out_shape=(shape((count, width...  14.5 us
    all_to_all x3, waiting for transfers between devices, exchange(): lax.all_to_all(blocks, ('dp', 'rep'), split_axis=0, concat_axis=0, tiled=...  13.6 us
    all_to_all x3, starting transfers between devices, exchange(): lax.all_to_all(blocks, ('dp', 'rep'), split_axis=0, concat_axis=0, tiled=...  12.4 us
    unnamed x11, local copies, waits for them, and re-layouts  3.8 us
    pallas_call x1, Pallas kernels, run_finish(): pl.pallas_call(finish_kernel, name='finish', out_shape=(shape((chosen.sha...  2.9 us
  transfers between devices with their start and end apart: 25, of which 16 were waited for; matrix products, arithmetic and copies ran while one was open for 0% of the time, Pallas kernels for 0%

profile of v2, /device:TPU:0, one launch (start us, length us, event | category | flops | bytes accessed | tf_op | source)
XLA Modules:
  0.0 100.2 jit_solution(15039210538017349769)
XLA Ops:
  0.6 1.4 %copy.15 = s32[32,1,2]{2,1,0:T(1,128)} copy(s32[32,1,2]{0,2,1:T(2,128)} %bitcast.12) | data formatting | bytes 512 | tf_op jit(solution)/shard_map/all_to_all | solution.py:475
  2.0 7.3 %all-to-all-start = ((s32[32,1,2]{2,1,0:T(1,128)}), s32[32,1,2]{2,1,0:T(1,128)S(1)}, u32[]{:S(2)}, u32[]{:S(2)}) async-start(s32[32,1,2]{2,1,0:T(1,128)} %copy.15), calls=%async_computation | async-start | bytes 32768 | tf_op jit(solution)/shard_map/all_to_all | solution.py:475
  9.3 0.9 copy-done.2
  10.2 6.2 %all-to-all-done = s32[32,1,2]{2,1,0:T(1,128)S(1)} async-done(((s32[32,1,2]{2,1,0:T(1,128)}), s32[32,1,2]{2,1,0:T(1,128)S(1)}, u32[]{:S(2)}, u32[]{:S(2)}) %all-to-all-start) | async-done | bytes 288 | tf_op jit(solution)/shard_map/all_to_all | solution.py:475
  16.4 1.1 %lookup.1 = (bf16[256,128]{1,0:T(8,128)(2,1)}, bf16[256,128]{1,0:T(8,128)(2,1)S(1)}) custom-call(s32[32,2]{1,0:T(8,128)S(1)} %bitcast.10, bf16[128,512]{1,0:T(8,128)(2,1)S(1)} %load.2.table_ref), custom_call_target="tpu_custom_call" | custom-call | tf_op jit(solution)/shard_map/lookup/pallas_call | solution.py:150
  17.5 2.6 %all-to-all-start.1 = ((bf16[32,8,128]{2,1,0:T(8,128)(2,1)}), bf16[32,8,128]{2,1,0:T(8,128)(2,1)S(1)}, u32[]{:S(2)}, u32[]{:S(2)}) async-start(bf16[32,8,128]{2,1,0:T(8,128)(2,1)} %bitcast.5), calls=%async_computation.1 | async-start | bytes 131072 | tf_op jit(solution)/shard_map/all_to_all | solution.py:475
  20.1 7.4 %all-to-all-done.1 = bf16[32,8,128]{2,1,0:T(8,128)(2,1)S(1)} async-done(((bf16[32,8,128]{2,1,0:T(8,128)(2,1)}), bf16[32,8,128]{2,1,0:T(8,128)(2,1)S(1)}, u32[]{:S(2)}, u32[]{:S(2)}) %all-to-all-start.1) | async-done | bytes 65568 | tf_op jit(solution)/shard_map/all_to_all | solution.py:475
  27.5 0.6 copy-done.3
  28.1 14.5 %layer.1 = (bf16[512,512]{1,0:T(8,128)(2,1)}, bf16[256,128]{1,0:T(8,128)(2,1)}, bf16[256,2048]{1,0:T(8,128)(2,1)}, bf16[256,2048]{1,0:T(8,128)(2,1)}, bf16[256,7...) custom-call(s32[1]{0:T(128)} %bitcast.me_ref, s32[1,4]{1,0:T(1,128)} %lengths_ref.1, s32[1,512]{1,0:T(1,128)} %bitcast.14, ...), custom_call_target="tpu_custom_call" | custom-call | flops 6000000000 | bytes 10000000 | tf_op jit(solution)/shard_map/layer/pallas_call | solution.py:315
  42.6 0.2 collective-permute-start
  42.8 0.4 collective-permute-start.1
  43.2 1.2 %copy-done = bf16[256,2048]{1,0:T(8,128)(2,1)S(1)} copy-done((bf16[256,2048]{1,0:T(8,128)(2,1)S(1)}, bf16[256,2048]{1,0:T(8,128)(2,1)}, u32[]{:S(2)}) %copy-start) | copy-done | bytes 1048600
  44.4 1.0 copy-done.1
  45.5 0.6 collective-permute-done.1.other_ref
  46.2 0.2 merge.2
  46.5 0.7 collective-permute-start.3
  47.1 0.4 collective-permute-start.2
  47.6 0.9 collective-permute-start.4
  48.4 2.2 %collective-permute-start.5 = (bf16[64,2048]{1,0:T(8,128)(2,1)S(1)}, bf16[64,2048]{1,0:T(8,128)(2,1)S(1)}, u32[]{:S(2)}, u32[]{:S(2)}) collective-permute-start(bf16[64,2048]{1,0:T(8,128)(2,1)S(1)} %get-tuple-element.67), channel_id=1, source_target_pairs={{0,6},{1,7},{2,4},{3,5},{4,2},{5,3},{6,0},{7,1},{8,14},{9,15},{10,... | collective-permute-start | bytes 786440 | tf_op jit(solution)/shard_map/ppermute | solution.py:479
  50.6 2.9 %collective-permute-done.3 = bf16[128,768]{1,0:T(8,128)(2,1)S(1)} collective-permute-done((bf16[128,768]{1,0:T(8,128)(2,1)S(1)}, bf16[128,768]{1,0:T(8,128)(2,1)S(1)}, u32[]{:S(2)}, u32[]{:S(2)}) %collective-permute-start.3) | collective-permute-done | bytes 196640 | tf_op jit(solution)/shard_map/ppermute | solution.py:479
  53.5 0.7 collective-permute-start.6
  54.2 2.1 %collective-permute-done.2 = bf16[64,2048]{1,0:T(8,128)(2,1)S(1)} collective-permute-done((bf16[64,2048]{1,0:T(8,128)(2,1)S(1)}, bf16[64,2048]{1,0:T(8,128)(2,1)S(1)}, u32[]{:S(2)}, u32[]{:S(2)}) %collective-permute-start.2) | collective-permute-done | bytes 262176 | tf_op jit(solution)/shard_map/ppermute | solution.py:479
  56.3 2.6 %all-to-all-start.2 = ((bf16[32,8,128]{2,1,0:T(8,128)(2,1)}), bf16[32,8,128]{2,1,0:T(8,128)(2,1)S(1)}, u32[]{:S(2)}, u32[]{:S(2)}) async-start(bf16[32,8,128]{2,1,0:T(8,128)(2,1)} %bitcast.7), calls=%async_computation.2 | async-start | bytes 131072 | tf_op jit(solution)/shard_map/all_to_all | solution.py:475
  58.9 2.0 %collective-permute-done.4 = bf16[64,2048]{1,0:T(8,128)(2,1)S(1)} collective-permute-done((bf16[64,2048]{1,0:T(8,128)(2,1)S(1)}, bf16[64,2048]{1,0:T(8,128)(2,1)S(1)}, u32[]{:S(2)}, u32[]{:S(2)}) %collective-permute-start.4) | collective-permute-done | bytes 262176 | tf_op jit(solution)/shard_map/ppermute | solution.py:479
  61.0 0.1 add_convert_fusion.5
  61.1 1.5 %collective-permute-start.7 = (bf16[16,2048]{1,0:T(8,128)(2,1)S(1)}, bf16[16,2048]{1,0:T(8,128)(2,1)S(1)}, u32[]{:S(2)}, u32[]{:S(2)}) collective-permute-start(bf16[16,2048]{1,0:T(8,128)(2,1)S(1)} %get-tuple-element.89), channel_id=1, source_target_pairs={{0,8},{1,9},{2,10},{3,11},{4,12},{5,13},{6,14},{7,15},{8,0},{9,1},... | collective-permute-start | bytes 196616 | tf_op jit(solution)/shard_map/ppermute | solution.py:479
  62.6 0.9 collective-permute-start.9
  63.4 1.2 %collective-permute-start.8 = (bf16[16,2048]{1,0:T(8,128)(2,1)S(1)}, bf16[16,2048]{1,0:T(8,128)(2,1)S(1)}, u32[]{:S(2)}, u32[]{:S(2)}) collective-permute-start(bf16[16,2048]{1,0:T(8,128)(2,1)S(1)} %get-tuple-element.91), channel_id=1, source_target_pairs={{0,16},{1,17},{2,18},{3,19},{4,20},{5,21},{6,22},{7,23},{8,24},{9,... | collective-permute-start | bytes 196616 | tf_op jit(solution)/shard_map/ppermute | solution.py:479
  64.7 1.4 %collective-permute-start.13 = (bf16[64,768]{1,0:T(8,128)(2,1)S(1)}, bf16[64,768]{1,0:T(8,128)(2,1)S(1)}, u32[]{:S(2)}, u32[]{:S(2)}) collective-permute-start(bf16[64,768]{1,0:T(8,128)(2,1)S(1)} %add_convert_fusion.1), channel_id=1, source_target_pairs={{0,4},{1,5},{2,6},{3,7},{4,0},{5,1},{6,2},{7,3},{8,12},{9,13},{10,... | collective-permute-start | bytes 294920 | tf_op jit(solution)/shard_map/ppermute | solution.py:479
  66.1 2.6 %collective-permute-done.9 = bf16[16,2048]{1,0:T(8,128)(2,1)S(1)} collective-permute-done((bf16[16,2048]{1,0:T(8,128)(2,1)S(1)}, bf16[16,2048]{1,0:T(8,128)(2,1)S(1)}, u32[]{:S(2)}, u32[]{:S(2)}) %collective-permute-start.9) | collective-permute-done | bytes 65568 | tf_op jit(solution)/shard_map/ppermute | solution.py:479
  68.6 2.2 %collective-permute-done.8 = bf16[16,2048]{1,0:T(8,128)(2,1)S(1)} collective-permute-done((bf16[16,2048]{1,0:T(8,128)(2,1)S(1)}, bf16[16,2048]{1,0:T(8,128)(2,1)S(1)}, u32[]{:S(2)}, u32[]{:S(2)}) %collective-permute-start.8) | collective-permute-done | bytes 65568 | tf_op jit(solution)/shard_map/ppermute | solution.py:479
  70.9 1.7 %collective-permute-start.12 = (bf16[16,2048]{1,0:T(8,128)(2,1)S(1)}, bf16[16,2048]{1,0:T(8,128)(2,1)S(1)}, u32[]{:S(2)}, u32[]{:S(2)}) collective-permute-start(bf16[16,2048]{1,0:T(8,128)(2,1)S(1)} %multiply_convert_fusion.1), channel_id=1, source_target_pairs={{0,24},{1,25},{2,26},{3,27},{4,28},{5,29},{6,30},{7,31},{8,16},{9,... | collective-permute-start | bytes 196616 | tf_op jit(solution)/shard_map/ppermute | solution.py:479
  72.6 2.8 %collective-permute-start.10 = (bf16[16,2048]{1,0:T(8,128)(2,1)S(1)}, bf16[16,2048]{1,0:T(8,128)(2,1)S(1)}, u32[]{:S(2)}, u32[]{:S(2)}) collective-permute-start(bf16[16,2048]{1,0:T(8,128)(2,1)S(1)} %multiply_convert_fusion.1), channel_id=1, source_target_pairs={{0,8},{1,9},{2,10},{3,11},{4,12},{5,13},{6,14},{7,15},{8,0},{9,1},... | collective-permute-start | bytes 196616 | tf_op jit(solution)/shard_map/ppermute | solution.py:479
  75.4 1.6 %collective-permute-start.14 = (bf16[64,768]{1,0:T(8,128)(2,1)S(1)}, bf16[64,768]{1,0:T(8,128)(2,1)S(1)}, u32[]{:S(2)}, u32[]{:S(2)}) collective-permute-start(bf16[64,768]{1,0:T(8,128)(2,1)S(1)} %add_convert_fusion), channel_id=1, source_target_pairs={{0,2},{1,3},{2,0},{3,1},{4,6},{5,7},{6,4},{7,5},{8,10},{9,11},{10,... | collective-permute-start | bytes 294920 | tf_op jit(solution)/shard_map/ppermute | solution.py:479
  77.0 0.6 collective-permute-done.12
  77.6 1.5 %collective-permute-done.11 = bf16[16,2048]{1,0:T(8,128)(2,1)S(1)} collective-permute-done((bf16[16,2048]{1,0:T(8,128)(2,1)S(1)}, bf16[16,2048]{1,0:T(8,128)(2,1)S(1)}, u32[]{:S(2)}, u32[]{:S(2)}) %collective-permute-start.11) | collective-permute-done | bytes 65568 | tf_op jit(solution)/shard_map/ppermute | solution.py:479
  79.1 1.0 collective-permute-done.14
  80.1 0.2 collective-permute-start.18
  80.3 2.5 %collective-permute-start.17 = (bf16[64,2048]{1,0:T(8,128)(2,1)S(1)}, bf16[64,2048]{1,0:T(8,128)(2,1)S(1)}, u32[]{:S(2)}, u32[]{:S(2)}) collective-permute-start(bf16[64,2048]{1,0:T(8,128)(2,1)S(1)} %pad_maximum_fusion.1), channel_id=1, source_target_pairs={{0,6},{1,7},{2,4},{3,5},{4,2},{5,3},{6,0},{7,1},{8,14},{9,15},{10,... | collective-permute-start | bytes 786440 | tf_op jit(solution)/shard_map/ppermute | solution.py:479
  82.8 0.5 collective-permute-start.16
  83.3 0.5 collective-permute-start.15
  83.8 2.4 %collective-permute-done.18 = bf16[64,768]{1,0:T(8,128)(2,1)S(1)} collective-permute-done((bf16[64,768]{1,0:T(8,128)(2,1)S(1)}, bf16[64,768]{1,0:T(8,128)(2,1)S(1)}, u32[]{:S(2)}, u32[]{:S(2)}) %collective-permute-start.18) | collective-permute-done | bytes 98336 | tf_op jit(solution)/shard_map/ppermute | solution.py:479
  86.3 5.6 %collective-permute-done.19 = bf16[128,768]{1,0:T(8,128)(2,1)S(1)} collective-permute-done((bf16[128,768]{1,0:T(8,128)(2,1)S(1)}, bf16[128,768]{1,0:T(8,128)(2,1)S(1)}, u32[]{:S(2)}, u32[]{:S(2)}) %collective-permute-start.19) | collective-permute-done | bytes 196640 | tf_op jit(solution)/shard_map/ppermute | solution.py:479
  92.0 1.8 %collective-permute-done.16 = bf16[64,2048]{1,0:T(8,128)(2,1)S(1)} collective-permute-done((bf16[64,2048]{1,0:T(8,128)(2,1)S(1)}, bf16[64,2048]{1,0:T(8,128)(2,1)S(1)}, u32[]{:S(2)}, u32[]{:S(2)}) %collective-permute-start.16) | collective-permute-done | bytes 262176 | tf_op jit(solution)/shard_map/ppermute | solution.py:479
  93.8 0.1 collective-permute-done.15
  94.1 0.5 collective-permute-start.21
  94.6 2.7 %collective-permute-done.21.late_other = bf16[256,768]{1,0:T(8,128)(2,1)S(1)} collective-permute-done((bf16[256,768]{1,0:T(8,128)(2,1)S(1)}, bf16[256,768]{1,0:T(8,128)(2,1)S(1)}, u32[]{:S(2)}, u32[]{:S(2)}) %collective-permute-start.21) | collective-permute-done | bytes 393248 | tf_op jit(solution)/shard_map/ppermute | solution.py:479
  97.3 2.9 %finish.1 = (f32[128,512]{1,0:T(8,128)}, f32[256,512]{1,0:T(8,128)}, f32[512,2048]{1,0:T(8,128)}, f32[512,512]{1,0:T(8,128)}) custom-call(s32[1]{0:T(128)} %bitcast.me_ref, bf16[256,128]{1,0:T(8,128)(2,1)S(1)} %get-tuple-element.49.chosen_ref, bf16[256,128]{1,0:T(8,128)(2,1)S(1)} %bitcast.9, ...), custom_call_target="tpu_custom_call" | custom-call | tf_op jit(solution)/shard_map/finish/pallas_call | solution.py:416
  (33 shorter events, 0.7 us)
Async XLA Ops:
  2.0 14.4 %all-to-all-start = ((s32[32,1,2]{2,1,0:T(1,128)}), s32[32,1,2]{2,1,0:T(1,128)S(1)}, u32[]{:S(2)}, u32[]{:S(2)}) async-start(s32[32,1,2]{2,1,0:T(1,128)} %copy.15), calls=%async_computation | async-start | bytes 32768 | tf_op jit(solution)/shard_map/all_to_all | solution.py:475
  9.3 0.9 copy-start.2
  17.5 10.0 %all-to-all-start.1 = ((bf16[32,8,128]{2,1,0:T(8,128)(2,1)}), bf16[32,8,128]{2,1,0:T(8,128)(2,1)S(1)}, u32[]{:S(2)}, u32[]{:S(2)}) async-start(bf16[32,8,128]{2,1,0:T(8,128)(2,1)} %bitcast.5), calls=%async_computation.1 | async-start | bytes 131072 | tf_op jit(solution)/shard_map/all_to_all | solution.py:475
  27.5 0.6 copy-start.3
  42.6 3.6 %collective-permute-start = (bf16[256,2048]{1,0:T(8,128)(2,1)}, bf16[256,2048]{1,0:T(8,128)(2,1)S(1)}, u32[]{:S(2)}, u32[]{:S(2)}) collective-permute-start(bf16[256,2048]{1,0:T(8,128)(2,1)} %get-tuple-element.53), channel_id=1, source_target_pairs={{0,1},{1,0},{2,3},{3,2},{4,5},{5,4},{6,7},{7,6},{8,9},{9,8},{10,11... | collective-permute-start | bytes 3145736 | tf_op jit(solution)/shard_map/ppermute | solution.py:479
  42.8 3.3 %collective-permute-start.1 = (bf16[256,768]{1,0:T(8,128)(2,1)}, bf16[256,768]{1,0:T(8,128)(2,1)S(1)}, u32[]{:S(2)}, u32[]{:S(2)}) collective-permute-start(bf16[256,768]{1,0:T(8,128)(2,1)} %get-tuple-element.59), channel_id=1, source_target_pairs={{0,1},{1,0},{2,3},{3,2},{4,5},{5,4},{6,7},{7,6},{8,9},{9,8},{10,11... | collective-permute-start | bytes 1179656 | tf_op jit(solution)/shard_map/ppermute | solution.py:479
  43.2 1.2 %copy-start = (bf16[256,2048]{1,0:T(8,128)(2,1)S(1)}, bf16[256,2048]{1,0:T(8,128)(2,1)}, u32[]{:S(2)}) copy-start(bf16[256,2048]{1,0:T(8,128)(2,1)} %get-tuple-element.50.refs_0_) | copy-start | bytes 3145732
  44.4 1.0 copy-start.1
  46.5 7.0 %collective-permute-start.3 = (bf16[128,768]{1,0:T(8,128)(2,1)S(1)}, bf16[128,768]{1,0:T(8,128)(2,1)S(1)}, u32[]{:S(2)}, u32[]{:S(2)}) collective-permute-start(bf16[128,768]{1,0:T(8,128)(2,1)S(1)} %get-tuple-element.63), channel_id=1, source_target_pairs={{0,8},{1,9},{2,10},{3,11},{4,12},{5,13},{6,14},{7,15},{8,0},{9,1},... | collective-permute-start | bytes 589832 | tf_op jit(solution)/shard_map/ppermute | solution.py:479
  47.1 9.2 %collective-permute-start.2 = (bf16[64,2048]{1,0:T(8,128)(2,1)S(1)}, bf16[64,2048]{1,0:T(8,128)(2,1)S(1)}, u32[]{:S(2)}, u32[]{:S(2)}) collective-permute-start(bf16[64,2048]{1,0:T(8,128)(2,1)S(1)} %get-tuple-element.61), channel_id=1, source_target_pairs={{0,2},{1,3},{2,0},{3,1},{4,6},{5,7},{6,4},{7,5},{8,10},{9,11},{10,... | collective-permute-start | bytes 786440 | tf_op jit(solution)/shard_map/ppermute | solution.py:479
  47.6 13.4 %collective-permute-start.4 = (bf16[64,2048]{1,0:T(8,128)(2,1)S(1)}, bf16[64,2048]{1,0:T(8,128)(2,1)S(1)}, u32[]{:S(2)}, u32[]{:S(2)}) collective-permute-start(bf16[64,2048]{1,0:T(8,128)(2,1)S(1)} %get-tuple-element.66), channel_id=1, source_target_pairs={{0,4},{1,5},{2,6},{3,7},{4,0},{5,1},{6,2},{7,3},{8,12},{9,13},{10,... | collective-permute-start | bytes 786440 | tf_op jit(solution)/shard_map/ppermute | solution.py:479
  48.4 12.5 %collective-permute-start.5 = (bf16[64,2048]{1,0:T(8,128)(2,1)S(1)}, bf16[64,2048]{1,0:T(8,128)(2,1)S(1)}, u32[]{:S(2)}, u32[]{:S(2)}) collective-permute-start(bf16[64,2048]{1,0:T(8,128)(2,1)S(1)} %get-tuple-element.67), channel_id=1, source_target_pairs={{0,6},{1,7},{2,4},{3,5},{4,2},{5,3},{6,0},{7,1},{8,14},{9,15},{10,... | collective-permute-start | bytes 786440 | tf_op jit(solution)/shard_map/ppermute | solution.py:479
  53.5 7.5 %collective-permute-start.6 = (bf16[64,768]{1,0:T(8,128)(2,1)S(1)}, bf16[64,768]{1,0:T(8,128)(2,1)S(1)}, u32[]{:S(2)}, u32[]{:S(2)}) collective-permute-start(bf16[64,768]{1,0:T(8,128)(2,1)S(1)} %add_convert_fusion.2), channel_id=1, source_target_pairs={{0,16},{1,17},{2,18},{3,19},{4,20},{5,21},{6,22},{7,23},{8,24},{9,... | collective-permute-start | bytes 294920 | tf_op jit(solution)/shard_map/ppermute | solution.py:479
  56.3 14.6 %all-to-all-start.2 = ((bf16[32,8,128]{2,1,0:T(8,128)(2,1)}), bf16[32,8,128]{2,1,0:T(8,128)(2,1)S(1)}, u32[]{:S(2)}, u32[]{:S(2)}) async-start(bf16[32,8,128]{2,1,0:T(8,128)(2,1)} %bitcast.7), calls=%async_computation.2 | async-start | bytes 131072 | tf_op jit(solution)/shard_map/all_to_all | solution.py:475
  61.1 5.0 %collective-permute-start.7 = (bf16[16,2048]{1,0:T(8,128)(2,1)S(1)}, bf16[16,2048]{1,0:T(8,128)(2,1)S(1)}, u32[]{:S(2)}, u32[]{:S(2)}) collective-permute-start(bf16[16,2048]{1,0:T(8,128)(2,1)S(1)} %get-tuple-element.89), channel_id=1, source_target_pairs={{0,8},{1,9},{2,10},{3,11},{4,12},{5,13},{6,14},{7,15},{8,0},{9,1},... | collective-permute-start | bytes 196616 | tf_op jit(solution)/shard_map/ppermute | solution.py:479
  62.6 6.1 %collective-permute-start.9 = (bf16[16,2048]{1,0:T(8,128)(2,1)S(1)}, bf16[16,2048]{1,0:T(8,128)(2,1)S(1)}, u32[]{:S(2)}, u32[]{:S(2)}) collective-permute-start(bf16[16,2048]{1,0:T(8,128)(2,1)S(1)} %get-tuple-element.90), channel_id=1, source_target_pairs={{0,24},{1,25},{2,26},{3,27},{4,28},{5,29},{6,30},{7,31},{8,16},{9,... | collective-permute-start | bytes 196616 | tf_op jit(solution)/shard_map/ppermute | solution.py:479
  63.4 7.4 %collective-permute-start.8 = (bf16[16,2048]{1,0:T(8,128)(2,1)S(1)}, bf16[16,2048]{1,0:T(8,128)(2,1)S(1)}, u32[]{:S(2)}, u32[]{:S(2)}) collective-permute-start(bf16[16,2048]{1,0:T(8,128)(2,1)S(1)} %get-tuple-element.91), channel_id=1, source_target_pairs={{0,16},{1,17},{2,18},{3,19},{4,20},{5,21},{6,22},{7,23},{8,24},{9,... | collective-permute-start | bytes 196616 | tf_op jit(solution)/shard_map/ppermute | solution.py:479
  64.7 10.7 %collective-permute-start.13 = (bf16[64,768]{1,0:T(8,128)(2,1)S(1)}, bf16[64,768]{1,0:T(8,128)(2,1)S(1)}, u32[]{:S(2)}, u32[]{:S(2)}) collective-permute-start(bf16[64,768]{1,0:T(8,128)(2,1)S(1)} %add_convert_fusion.1), channel_id=1, source_target_pairs={{0,4},{1,5},{2,6},{3,7},{4,0},{5,1},{6,2},{7,3},{8,12},{9,13},{10,... | collective-permute-start | bytes 294920 | tf_op jit(solution)/shard_map/ppermute | solution.py:479
  70.9 6.7 %collective-permute-start.12 = (bf16[16,2048]{1,0:T(8,128)(2,1)S(1)}, bf16[16,2048]{1,0:T(8,128)(2,1)S(1)}, u32[]{:S(2)}, u32[]{:S(2)}) collective-permute-start(bf16[16,2048]{1,0:T(8,128)(2,1)S(1)} %multiply_convert_fusion.1), channel_id=1, source_target_pairs={{0,24},{1,25},{2,26},{3,27},{4,28},{5,29},{6,30},{7,31},{8,16},{9,... | collective-permute-start | bytes 196616 | tf_op jit(solution)/shard_map/ppermute | solution.py:479
  72.6 6.5 %collective-permute-start.11 = (bf16[16,2048]{1,0:T(8,128)(2,1)S(1)}, bf16[16,2048]{1,0:T(8,128)(2,1)S(1)}, u32[]{:S(2)}, u32[]{:S(2)}) collective-permute-start(bf16[16,2048]{1,0:T(8,128)(2,1)S(1)} %multiply_convert_fusion.1), channel_id=1, source_target_pairs={{0,16},{1,17},{2,18},{3,19},{4,20},{5,21},{6,22},{7,23},{8,24},{9,... | collective-permute-start | bytes 196616 | tf_op jit(solution)/shard_map/ppermute | solution.py:479
  72.6 6.5 %collective-permute-start.10 = (bf16[16,2048]{1,0:T(8,128)(2,1)S(1)}, bf16[16,2048]{1,0:T(8,128)(2,1)S(1)}, u32[]{:S(2)}, u32[]{:S(2)}) collective-permute-start(bf16[16,2048]{1,0:T(8,128)(2,1)S(1)} %multiply_convert_fusion.1), channel_id=1, source_target_pairs={{0,8},{1,9},{2,10},{3,11},{4,12},{5,13},{6,14},{7,15},{8,0},{9,1},... | collective-permute-start | bytes 196616 | tf_op jit(solution)/shard_map/ppermute | solution.py:479
  75.4 4.7 %collective-permute-start.14 = (bf16[64,768]{1,0:T(8,128)(2,1)S(1)}, bf16[64,768]{1,0:T(8,128)(2,1)S(1)}, u32[]{:S(2)}, u32[]{:S(2)}) collective-permute-start(bf16[64,768]{1,0:T(8,128)(2,1)S(1)} %add_convert_fusion), channel_id=1, source_target_pairs={{0,2},{1,3},{2,0},{3,1},{4,6},{5,7},{6,4},{7,5},{8,10},{9,11},{10,... | collective-permute-start | bytes 294920 | tf_op jit(solution)/shard_map/ppermute | solution.py:479
  80.1 6.1 %collective-permute-start.18 = (bf16[64,768]{1,0:T(8,128)(2,1)S(1)}, bf16[64,768]{1,0:T(8,128)(2,1)S(1)}, u32[]{:S(2)}, u32[]{:S(2)}) collective-permute-start(bf16[64,768]{1,0:T(8,128)(2,1)S(1)} %multiply_convert_fusion), channel_id=1, source_target_pairs={{0,16},{1,17},{2,18},{3,19},{4,20},{5,21},{6,22},{7,23},{8,24},{9,... | collective-permute-start | bytes 294920 | tf_op jit(solution)/shard_map/ppermute | solution.py:479
  80.3 11.7 %collective-permute-start.17 = (bf16[64,2048]{1,0:T(8,128)(2,1)S(1)}, bf16[64,2048]{1,0:T(8,128)(2,1)S(1)}, u32[]{:S(2)}, u32[]{:S(2)}) collective-permute-start(bf16[64,2048]{1,0:T(8,128)(2,1)S(1)} %pad_maximum_fusion.1), channel_id=1, source_target_pairs={{0,6},{1,7},{2,4},{3,5},{4,2},{5,3},{6,0},{7,1},{8,14},{9,15},{10,... | collective-permute-start | bytes 786440 | tf_op jit(solution)/shard_map/ppermute | solution.py:479
  82.8 11.0 %collective-permute-start.16 = (bf16[64,2048]{1,0:T(8,128)(2,1)S(1)}, bf16[64,2048]{1,0:T(8,128)(2,1)S(1)}, u32[]{:S(2)}, u32[]{:S(2)}) collective-permute-start(bf16[64,2048]{1,0:T(8,128)(2,1)S(1)} %pad_maximum_fusion.1), channel_id=1, source_target_pairs={{0,4},{1,5},{2,6},{3,7},{4,0},{5,1},{6,2},{7,3},{8,12},{9,13},{10,... | collective-permute-start | bytes 786440 | tf_op jit(solution)/shard_map/ppermute | solution.py:479
  83.3 10.7 %collective-permute-start.15 = (bf16[64,2048]{1,0:T(8,128)(2,1)S(1)}, bf16[64,2048]{1,0:T(8,128)(2,1)S(1)}, u32[]{:S(2)}, u32[]{:S(2)}) collective-permute-start(bf16[64,2048]{1,0:T(8,128)(2,1)S(1)} %pad_maximum_fusion.1), channel_id=1, source_target_pairs={{0,2},{1,3},{2,0},{3,1},{4,6},{5,7},{6,4},{7,5},{8,10},{9,11},{10,... | collective-permute-start | bytes 786440 | tf_op jit(solution)/shard_map/ppermute | solution.py:479
  86.2 5.7 %collective-permute-start.19 = (bf16[128,768]{1,0:T(8,128)(2,1)S(1)}, bf16[128,768]{1,0:T(8,128)(2,1)S(1)}, u32[]{:S(2)}, u32[]{:S(2)}) collective-permute-start(bf16[128,768]{1,0:T(8,128)(2,1)S(1)} %pad_maximum_fusion.2), channel_id=1, source_target_pairs={{0,8},{1,9},{2,10},{3,11},{4,12},{5,13},{6,14},{7,15},{8,0},{9,1},... | collective-permute-start | bytes 589832 | tf_op jit(solution)/shard_map/ppermute | solution.py:479
  94.0 3.3 %collective-permute-start.20 = (bf16[256,2048]{1,0:T(8,128)(2,1)S(1)}, bf16[256,2048]{1,0:T(8,128)(2,1)S(1)}, u32[]{:S(2)}, u32[]{:S(2)}) collective-permute-start(bf16[256,2048]{1,0:T(8,128)(2,1)S(1)} %constant_dynamic-update-slice_fusion.early_own), channel_id=1, source_target_pairs={{0,1},{1,0},{2,3},{3,2},{4,5},{5,4},{6,7},{7,6},{8,9},{9,8},{10,11... | collective-permute-start | bytes 3145736 | tf_op jit(solution)/shard_map/ppermute | solution.py:479
  94.1 3.2 %collective-permute-start.21 = (bf16[256,768]{1,0:T(8,128)(2,1)S(1)}, bf16[256,768]{1,0:T(8,128)(2,1)S(1)}, u32[]{:S(2)}, u32[]{:S(2)}) collective-permute-start(bf16[256,768]{1,0:T(8,128)(2,1)S(1)} %pad_maximum_fusion.late_own), channel_id=1, source_target_pairs={{0,1},{1,0},{2,3},{3,2},{4,5},{5,4},{6,7},{7,6},{8,9},{9,8},{10,11... | collective-permute-start | bytes 1179656 | tf_op jit(solution)/shard_map/ppermute | solution.py:479

commit v3 on v2

--- a/solution.py
+++ b/solution.py
@@ -20,7 +20,7 @@
 SPLIT = 2048
 CHUNKS = 32
 STRIP = 32
-LAYER_VMEM = 60 * 2**20
+LAYER_VMEM = 56 * 2**20
 
 
 def dot(a, b, contract):
@@ -129,17 +129,17 @@
     spot = lax.broadcasted_iota(jnp.int32, (count, owned), 1)
     row = lax.broadcasted_iota(jnp.int32, (many, count), 0)
     device = lax.broadcasted_iota(jnp.int32, (many, count), 1)
-    chosen = jnp.zeros((many, owned), f32)
+    here, wanted = [], []
     for k in range(each):
         base = (device * each + k) * parts
-        here = zero_one(jnp.logical_and(row >= base, row < base + parts))
-        chosen = chosen + mm(here, zero_one(spot == asked_ref[:, k : k + 1]))
+        here.append(zero_one(jnp.logical_and(row >= base, row < base + parts)))
+        wanted.append(zero_one(spot == asked_ref[:, k : k + 1]))
+    chosen = mm(jnp.concatenate(here, axis=1), jnp.concatenate(wanted, axis=0))
     chosen_ref[...] = chosen.astype(bf16)
     part_of = lax.broadcasted_iota(jnp.int32, (many, owned), 0) & (parts - 1)
-    total = jnp.zeros((many, BLOCK), f32)
-    for part in range(parts):
-        mine = jnp.where(part_of == part, chosen, 0.0).astype(bf16)
-        total = total + mm(mine, table_ref[:, part * BLOCK : (part + 1) * BLOCK])
+    mine = [jnp.where(part_of == part, chosen, 0.0).astype(bf16) for part in range(parts)]
+    blocks = [table_ref[:, part * BLOCK : (part + 1) * BLOCK] for part in range(parts)]
+    total = mm(jnp.concatenate(mine, axis=1), jnp.concatenate(blocks, axis=0))
     rows_ref[...] = total.astype(bf16)
 
 
@@ -360,14 +360,11 @@
     )(me, lengths, slot, leaf, rows, table, w_in, w_out, tangent)
 
 
-def finish_kernel(
-    me_ref, chosen_ref, returned_ref, early_own, early_other, late_own, late_other,
-    table_hbm, leaf_hbm, in_hbm, out_hbm, grads, table, sems,
-):
-    width, columns = grads.shape
+def write_chunks(me, half, early_ref, late_ref, leaf_hbm, in_hbm, out_hbm, grads, sems):
+    width = in_hbm.shape[0]
     leaves = leaf_hbm.shape[0]
-    me = me_ref[0]
-    half_rows = width // 2
+    places = early_ref.shape[0] // ROWS
+    early, late = chunk_order(me, EARLY), chunk_order(me, LATE, SHARED)
     leaving = []
 
     def leave(source, target):
@@ -375,62 +372,90 @@
         copy.start()
         leaving.append(copy)
 
-    early, late = chunk_order(me, EARLY), chunk_order(me, LATE, SHARED)
-
-    def place(chunks, own, other, low, high, at):
-        for spot, chunk in enumerate(chunks):
-            source = own if spot * ROWS < half_rows else other
-            row = spot * ROWS % half_rows
-            start = pl.multiple_of(chunk * ROWS, ROWS)
-            grads[pl.ds(start, ROWS), at + low : at + high] = source[
-                row : row + ROWS, low:high
-            ].astype(f32)
-
-    place(late, late_own, late_other, 0, width, SPLIT)
-    leave(grads.at[:, SPLIT : SPLIT + width], out_hbm)
-    place(late, late_own, late_other, width, columns - SPLIT, SPLIT)
-    for half in range(2):
+    for place in range(places):
+        at = slice(place * ROWS, (place + 1) * ROWS)
+        grads[at, :SPLIT] = early_ref[at, :].astype(f32)
+        start = pl.multiple_of(early[half * places + place] * ROWS, ROWS)
+        leave(grads.at[at, :SPLIT], in_hbm.at[pl.ds(start, ROWS), :])
+        grads[at, SPLIT:] = late_ref[at, :].astype(f32)
+        start = pl.multiple_of(late[half * places + place] * ROWS, ROWS)
+        leave(grads.at[at, SPLIT : SPLIT + width], out_hbm.at[pl.ds(start, ROWS), :])
+        side = (start >= leaves).astype(jnp.int32)
+        start = pl.multiple_of(start - side * leaves, ROWS)
+        column = pl.multiple_of(side * (width // 2), width // 2)
         leave(
-            grads.at[half * leaves : (half + 1) * leaves, SPLIT + width :],
-            leaf_hbm.at[:, half * (width // 2) : (half + 1) * (width // 2)],
+            grads.at[at, SPLIT + width :],
+            leaf_hbm.at[pl.ds(start, ROWS), pl.ds(column, width // 2)],
         )
-    parts = width // BLOCK
+    return leaving
+
+
+def finish_own_kernel(
+    me_ref, chosen_ref, returned_ref, early_ref, late_ref,
+    table_ref, leaf_hbm, in_hbm, out_hbm, grads, sems,
+):
+    leaving = write_chunks(
+        me_ref[0], 0, early_ref, late_ref, leaf_hbm, in_hbm, out_hbm, grads, sems
+    )
+    parts = table_ref.shape[1] // BLOCK
     part_of = lax.broadcasted_iota(jnp.int32, chosen_ref.shape, 0) & (parts - 1)
     for part in range(parts):
         mine = jnp.where(part_of == part, chosen_ref[...].astype(f32), 0.0).astype(bf16)
-        table[:, part * BLOCK : (part + 1) * BLOCK] = mm_tn(mine, returned_ref[...])
-    leave(table, table_hbm)
-    for low in range(0, SPLIT, width):
-        place(early, early_own, early_other, low, low + width, 0)
-        leave(grads.at[:, low : low + width], in_hbm.at[:, low : low + width])
+        table_ref[:, part * BLOCK : (part + 1) * BLOCK] = mm_tn(mine, returned_ref[...])
     for copy in leaving:
         copy.wait()
+
+
+def finish_other_kernel(
+    me_ref, early_ref, late_ref, leaf_in, in_in, out_in, leaf_hbm, in_hbm, out_hbm, grads, sems
+):
+    leaving = write_chunks(
+        me_ref[0], 1, early_ref, late_ref, leaf_hbm, in_hbm, out_hbm, grads, sems
+    )
+    for copy in leaving:
+        copy.wait()
+
+
+def finish_scratch(early, late):
+    return [
+        pltpu.VMEM((early.shape[0], early.shape[1] + late.shape[1]), f32),
+        pltpu.SemaphoreType.DMA((3 * early.shape[0] // ROWS,)),
+    ]
 
 
 def run_finish(me, chosen, returned, early_own, early_other, late_own, late_other, leaves):
     smem = pl.BlockSpec(memory_space=pltpu.SMEM)
     vmem = pl.BlockSpec(memory_space=pltpu.VMEM)
     hbm = pl.BlockSpec(memory_space=pltpu.HBM)
-    shape = jax.ShapeDtypeStruct
     width = early_own.shape[1] // 4
-    return pl.pallas_call(
-        finish_kernel,
-        name="finish",
-        out_shape=(
-            shape((chosen.shape[1], width), f32),
-            shape((leaves, width), f32),
-            shape((width, 4 * width), f32),
-            shape((width, width), f32),
-        ),
-        in_specs=[smem] + [vmem] * 6,
-        out_specs=(hbm,) * 4,
-        scratch_shapes=[
-            pltpu.VMEM((width, early_own.shape[1] + late_own.shape[1]), f32),
-            pltpu.VMEM((chosen.shape[1], width), f32),
-            pltpu.SemaphoreType.DMA((8,)),
-        ],
-        compiler_params=pltpu.CompilerParams(vmem_limit_bytes=32 * 2**20),
-    )(me, chosen, returned, early_own, early_other, late_own, late_other)
+    shapes = tuple(
+        jax.ShapeDtypeStruct(shape, f32)
+        for shape in (
+            (chosen.shape[1], width), (leaves, width), (width, 4 * width), (width, width)
+        )
+    )
+    table, *written = pl.pallas_call(
+        finish_own_kernel,
+        name="finish_own",
+        out_shape=shapes,
+        in_specs=[smem] + [vmem] * 4,
+        out_specs=(vmem, hbm, hbm, hbm),
+        scratch_shapes=finish_scratch(early_own, late_own),
+        compiler_params=pltpu.CompilerParams(vmem_limit_bytes=16 * 2**20),
+        cost_estimate=pl.CostEstimate(flops=10**8, bytes_accessed=5 * 10**6, transcendentals=0),
+    )(me, chosen, returned, early_own, late_own)
+    written = pl.pallas_call(
+        finish_other_kernel,
+        name="finish_other",
+        out_shape=shapes[1:],
+        in_specs=[smem] + [vmem] * 2 + [hbm] * 3,
+        out_specs=(hbm,) * 3,
+        scratch_shapes=finish_scratch(early_own, late_own),
+        input_output_aliases={3: 0, 4: 1, 5: 2},
+        compiler_params=pltpu.CompilerParams(vmem_limit_bytes=16 * 2**20),
+        cost_estimate=pl.CostEstimate(flops=0, bytes_accessed=5 * 10**6, transcendentals=0),
+    )(me, early_other, late_other, *written)
+    return (table, *written)
 
 
 def load_kernel(*refs):

time: 101 us -> 100 us (0.990)
  waiting for transfers between devices: 41.7 us -> 38.7 us
  Pallas kernels: 18.9 us -> 20.8 us
    ppermute x22, waiting for transfers between devices: 28.1 us -> 25.1 us  [swap(): lax.ppermute(block, ('dp', 'rep'), [(i, i ^ mask) for i in range(count)])]
    pallas_call x1 -> x2, Pallas kernels: 2.9 us -> 4.86 us  [the longest x1 2.84 us: run_finish(): pl.pallas_call(finish_own_kernel, name='finish_own', out_shape=shapes, in...]
  transfers between devices with their start and end apart: 25 -> 25, of which waited for: 16 -> 15; matrix products, arithmetic and copies ran while one was open for 0% -> 0% of each run, Pallas kernels for 0% -> 3%
where the time goes in v3:
time: 100 us; the launch traced here: 99.6 us
  waiting for transfers between devices  38.7 us (39%)
  starting transfers between devices  33.5 us (34%)
  Pallas kernels  20.8 us (21%)
  local copies, waits for them, and re-layouts  5.2 us (5%)
  between operations  1.01 us (1%)
    ppermute x22, waiting for transfers between devices, swap(): lax.ppermute(block, ('dp', 'rep'), [(i, i ^ mask) for i in range(count)])  25.1 us
    ppermute x22, starting transfers between devices, swap(): lax.ppermute(block, ('dp', 'rep'), [(i, i ^ mask) for i in range(count)])  20.9 us
    pallas_call x1, Pallas kernels, run_layer(): pl.pallas_call(layer_kernel, name='layer', out_shape=(shape((count, width...  14.5 us
    all_to_all x3, waiting for transfers between devices, exchange(): lax.all_to_all(blocks, ('dp', 'rep'), split_axis=0, concat_axis=0, tiled=...  13.6 us
    all_to_all x3, starting transfers between devices, exchange(): lax.all_to_all(blocks, ('dp', 'rep'), split_axis=0, concat_axis=0, tiled=...  12.6 us
    unnamed x11, local copies, waits for them, and re-layouts  3.8 us
    pallas_call x1, Pallas kernels, run_finish(): pl.pallas_call(finish_own_kernel, name='finish_own', out_shape=shapes, in...  2.84 us
    pallas_call x1, Pallas kernels, run_finish(): pl.pallas_call(finish_other_kernel, name='finish_other', out_shape=shapes...  2.02 us
  transfers between devices with their start and end apart: 25, of which 15 were waited for; matrix products, arithmetic and copies ran while one was open for 0% of the time, Pallas kernels for 3%

profile of v3, /device:TPU:0, one launch (start us, length us, event | category | flops | bytes accessed | tf_op | source)
XLA Modules:
  0.0 99.6 jit_solution(9194091675341166894)
XLA Ops:
  0.6 1.4 %copy.18 = s32[32,1,2]{2,1,0:T(1,128)} copy(s32[32,1,2]{0,2,1:T(2,128)} %bitcast.12) | data formatting | bytes 512 | tf_op jit(solution)/shard_map/all_to_all | solution.py:500
  2.0 7.3 %all-to-all-start = ((s32[32,1,2]{2,1,0:T(1,128)}), s32[32,1,2]{2,1,0:T(1,128)S(1)}, u32[]{:S(2)}, u32[]{:S(2)}) async-start(s32[32,1,2]{2,1,0:T(1,128)} %copy.18), calls=%async_computation | async-start | bytes 32768 | tf_op jit(solution)/shard_map/all_to_all | solution.py:500
  9.3 0.9 copy-done.2
  10.2 6.2 %all-to-all-done = s32[32,1,2]{2,1,0:T(1,128)S(1)} async-done(((s32[32,1,2]{2,1,0:T(1,128)}), s32[32,1,2]{2,1,0:T(1,128)S(1)}, u32[]{:S(2)}, u32[]{:S(2)}) %all-to-all-start) | async-done | bytes 288 | tf_op jit(solution)/shard_map/all_to_all | solution.py:500
  16.4 1.0 %lookup.1 = (bf16[256,128]{1,0:T(8,128)(2,1)}, bf16[256,128]{1,0:T(8,128)(2,1)S(1)}) custom-call(s32[32,2]{1,0:T(8,128)S(1)} %bitcast.10, bf16[128,512]{1,0:T(8,128)(2,1)S(1)} %load.2.table_ref), custom_call_target="tpu_custom_call" | custom-call | tf_op jit(solution)/shard_map/lookup/pallas_call | solution.py:150
  17.4 2.6 %all-to-all-start.1 = ((bf16[32,8,128]{2,1,0:T(8,128)(2,1)}), bf16[32,8,128]{2,1,0:T(8,128)(2,1)S(1)}, u32[]{:S(2)}, u32[]{:S(2)}) async-start(bf16[32,8,128]{2,1,0:T(8,128)(2,1)} %bitcast.5), calls=%async_computation.1 | async-start | bytes 131072 | tf_op jit(solution)/shard_map/all_to_all | solution.py:500
  20.0 7.4 %all-to-all-done.1 = bf16[32,8,128]{2,1,0:T(8,128)(2,1)S(1)} async-done(((bf16[32,8,128]{2,1,0:T(8,128)(2,1)}), bf16[32,8,128]{2,1,0:T(8,128)(2,1)S(1)}, u32[]{:S(2)}, u32[]{:S(2)}) %all-to-all-start.1) | async-done | bytes 65568 | tf_op jit(solution)/shard_map/all_to_all | solution.py:500
  27.4 0.6 copy-done.3
  28.0 14.5 %layer.1 = (bf16[512,512]{1,0:T(8,128)(2,1)}, bf16[256,128]{1,0:T(8,128)(2,1)}, bf16[256,2048]{1,0:T(8,128)(2,1)}, bf16[256,2048]{1,0:T(8,128)(2,1)}, bf16[256,7...) custom-call(s32[1]{0:T(128)} %bitcast.me_ref, s32[1,4]{1,0:T(1,128)} %lengths_ref.1, s32[1,512]{1,0:T(1,128)} %bitcast.14, ...), custom_call_target="tpu_custom_call" | custom-call | flops 6000000000 | bytes 10000000 | tf_op jit(solution)/shard_map/layer/pallas_call | solution.py:315
  42.5 0.2 collective-permute-start
  42.7 0.4 collective-permute-start.1
  43.1 1.2 %copy-done = bf16[256,2048]{1,0:T(8,128)(2,1)S(1)} copy-done((bf16[256,2048]{1,0:T(8,128)(2,1)S(1)}, bf16[256,2048]{1,0:T(8,128)(2,1)}, u32[]{:S(2)}) %copy-start) | copy-done | bytes 1048600
  44.3 1.0 copy-done.1
  45.4 0.6 collective-permute-done.1.other_ref
  46.1 0.2 merge.2
  46.4 0.7 collective-permute-start.3
  47.1 0.4 collective-permute-start.2
  47.5 0.9 collective-permute-start.4
  48.4 2.2 %collective-permute-start.5 = (bf16[64,2048]{1,0:T(8,128)(2,1)S(1)}, bf16[64,2048]{1,0:T(8,128)(2,1)S(1)}, u32[]{:S(2)}, u32[]{:S(2)}) collective-permute-start(bf16[64,2048]{1,0:T(8,128)(2,1)S(1)} %get-tuple-element.70), channel_id=1, source_target_pairs={{0,6},{1,7},{2,4},{3,5},{4,2},{5,3},{6,0},{7,1},{8,14},{9,15},{10,... | collective-permute-start | bytes 786440 | tf_op jit(solution)/shard_map/ppermute | solution.py:504
  50.6 2.8 %collective-permute-done.3 = bf16[128,768]{1,0:T(8,128)(2,1)S(1)} collective-permute-done((bf16[128,768]{1,0:T(8,128)(2,1)S(1)}, bf16[128,768]{1,0:T(8,128)(2,1)S(1)}, u32[]{:S(2)}, u32[]{:S(2)}) %collective-permute-start.3) | collective-permute-done | bytes 196640 | tf_op jit(solution)/shard_map/ppermute | solution.py:504
  53.4 0.7 collective-permute-start.6
  54.2 2.1 %collective-permute-done.2 = bf16[64,2048]{1,0:T(8,128)(2,1)S(1)} collective-permute-done((bf16[64,2048]{1,0:T(8,128)(2,1)S(1)}, bf16[64,2048]{1,0:T(8,128)(2,1)S(1)}, u32[]{:S(2)}, u32[]{:S(2)}) %collective-permute-start.2) | collective-permute-done | bytes 262176 | tf_op jit(solution)/shard_map/ppermute | solution.py:504
  56.3 2.7 %all-to-all-start.2 = ((bf16[32,8,128]{2,1,0:T(8,128)(2,1)}), bf16[32,8,128]{2,1,0:T(8,128)(2,1)S(1)}, u32[]{:S(2)}, u32[]{:S(2)}) async-start(bf16[32,8,128]{2,1,0:T(8,128)(2,1)} %bitcast.7), calls=%async_computation.2 | async-start | bytes 131072 | tf_op jit(solution)/shard_map/all_to_all | solution.py:500
  59.0 1.9 %collective-permute-done.4 = bf16[64,2048]{1,0:T(8,128)(2,1)S(1)} collective-permute-done((bf16[64,2048]{1,0:T(8,128)(2,1)S(1)}, bf16[64,2048]{1,0:T(8,128)(2,1)S(1)}, u32[]{:S(2)}, u32[]{:S(2)}) %collective-permute-start.4) | collective-permute-done | bytes 262176 | tf_op jit(solution)/shard_map/ppermute | solution.py:504
  60.9 0.1 add_convert_fusion.5
  61.0 1.5 %collective-permute-start.7 = (bf16[16,2048]{1,0:T(8,128)(2,1)S(1)}, bf16[16,2048]{1,0:T(8,128)(2,1)S(1)}, u32[]{:S(2)}, u32[]{:S(2)}) collective-permute-start(bf16[16,2048]{1,0:T(8,128)(2,1)S(1)} %get-tuple-element.95), channel_id=1, source_target_pairs={{0,8},{1,9},{2,10},{3,11},{4,12},{5,13},{6,14},{7,15},{8,0},{9,1},... | collective-permute-start | bytes 196616 | tf_op jit(solution)/shard_map/ppermute | solution.py:504
  62.5 0.9 collective-permute-start.9
  63.4 1.2 %collective-permute-start.8 = (bf16[16,2048]{1,0:T(8,128)(2,1)S(1)}, bf16[16,2048]{1,0:T(8,128)(2,1)S(1)}, u32[]{:S(2)}, u32[]{:S(2)}) collective-permute-start(bf16[16,2048]{1,0:T(8,128)(2,1)S(1)} %get-tuple-element.97), channel_id=1, source_target_pairs={{0,16},{1,17},{2,18},{3,19},{4,20},{5,21},{6,22},{7,23},{8,24},{9,... | collective-permute-start | bytes 196616 | tf_op jit(solution)/shard_map/ppermute | solution.py:504
  64.6 1.4 %collective-permute-start.13 = (bf16[64,768]{1,0:T(8,128)(2,1)S(1)}, bf16[64,768]{1,0:T(8,128)(2,1)S(1)}, u32[]{:S(2)}, u32[]{:S(2)}) collective-permute-start(bf16[64,768]{1,0:T(8,128)(2,1)S(1)} %add_convert_fusion.1), channel_id=1, source_target_pairs={{0,4},{1,5},{2,6},{3,7},{4,0},{5,1},{6,2},{7,3},{8,12},{9,13},{10,... | collective-permute-start | bytes 294920 | tf_op jit(solution)/shard_map/ppermute | solution.py:504
  66.0 2.6 %collective-permute-done.9 = bf16[16,2048]{1,0:T(8,128)(2,1)S(1)} collective-permute-done((bf16[16,2048]{1,0:T(8,128)(2,1)S(1)}, bf16[16,2048]{1,0:T(8,128)(2,1)S(1)}, u32[]{:S(2)}, u32[]{:S(2)}) %collective-permute-start.9) | collective-permute-done | bytes 65568 | tf_op jit(solution)/shard_map/ppermute | solution.py:504
  68.6 2.2 %collective-permute-done.8 = bf16[16,2048]{1,0:T(8,128)(2,1)S(1)} collective-permute-done((bf16[16,2048]{1,0:T(8,128)(2,1)S(1)}, bf16[16,2048]{1,0:T(8,128)(2,1)S(1)}, u32[]{:S(2)}, u32[]{:S(2)}) %collective-permute-start.8) | collective-permute-done | bytes 65568 | tf_op jit(solution)/shard_map/ppermute | solution.py:504
  70.8 1.7 %collective-permute-start.12 = (bf16[16,2048]{1,0:T(8,128)(2,1)S(1)}, bf16[16,2048]{1,0:T(8,128)(2,1)S(1)}, u32[]{:S(2)}, u32[]{:S(2)}) collective-permute-start(bf16[16,2048]{1,0:T(8,128)(2,1)S(1)} %multiply_convert_fusion.1), channel_id=1, source_target_pairs={{0,24},{1,25},{2,26},{3,27},{4,28},{5,29},{6,30},{7,31},{8,16},{9,... | collective-permute-start | bytes 196616 | tf_op jit(solution)/shard_map/ppermute | solution.py:504
  72.5 2.7 %collective-permute-start.10 = (bf16[16,2048]{1,0:T(8,128)(2,1)S(1)}, bf16[16,2048]{1,0:T(8,128)(2,1)S(1)}, u32[]{:S(2)}, u32[]{:S(2)}) collective-permute-start(bf16[16,2048]{1,0:T(8,128)(2,1)S(1)} %multiply_convert_fusion.1), channel_id=1, source_target_pairs={{0,8},{1,9},{2,10},{3,11},{4,12},{5,13},{6,14},{7,15},{8,0},{9,1},... | collective-permute-start | bytes 196616 | tf_op jit(solution)/shard_map/ppermute | solution.py:504
  75.3 1.6 %collective-permute-start.14 = (bf16[64,768]{1,0:T(8,128)(2,1)S(1)}, bf16[64,768]{1,0:T(8,128)(2,1)S(1)}, u32[]{:S(2)}, u32[]{:S(2)}) collective-permute-start(bf16[64,768]{1,0:T(8,128)(2,1)S(1)} %add_convert_fusion), channel_id=1, source_target_pairs={{0,2},{1,3},{2,0},{3,1},{4,6},{5,7},{6,4},{7,5},{8,10},{9,11},{10,... | collective-permute-start | bytes 294920 | tf_op jit(solution)/shard_map/ppermute | solution.py:504
  76.9 0.5 collective-permute-done.12
  77.4 1.5 %collective-permute-done.11 = bf16[16,2048]{1,0:T(8,128)(2,1)S(1)} collective-permute-done((bf16[16,2048]{1,0:T(8,128)(2,1)S(1)}, bf16[16,2048]{1,0:T(8,128)(2,1)S(1)}, u32[]{:S(2)}, u32[]{:S(2)}) %collective-permute-start.11) | collective-permute-done | bytes 65568 | tf_op jit(solution)/shard_map/ppermute | solution.py:504
  79.0 1.0 collective-permute-done.14
  80.0 0.2 collective-permute-start.18
  80.3 2.5 %collective-permute-start.17 = (bf16[64,2048]{1,0:T(8,128)(2,1)S(1)}, bf16[64,2048]{1,0:T(8,128)(2,1)S(1)}, u32[]{:S(2)}, u32[]{:S(2)}) collective-permute-start(bf16[64,2048]{1,0:T(8,128)(2,1)S(1)} %pad_maximum_fusion.1), channel_id=1, source_target_pairs={{0,6},{1,7},{2,4},{3,5},{4,2},{5,3},{6,0},{7,1},{8,14},{9,15},{10,... | collective-permute-start | bytes 786440 | tf_op jit(solution)/shard_map/ppermute | solution.py:504
  82.7 0.5 collective-permute-start.16
  83.2 0.5 collective-permute-start.15
  83.7 2.3 %collective-permute-done.18 = bf16[64,768]{1,0:T(8,128)(2,1)S(1)} collective-permute-done((bf16[64,768]{1,0:T(8,128)(2,1)S(1)}, bf16[64,768]{1,0:T(8,128)(2,1)S(1)}, u32[]{:S(2)}, u32[]{:S(2)}) %collective-permute-start.18) | collective-permute-done | bytes 98336 | tf_op jit(solution)/shard_map/ppermute | solution.py:504
  86.2 5.6 %collective-permute-done.19 = bf16[128,768]{1,0:T(8,128)(2,1)S(1)} collective-permute-done((bf16[128,768]{1,0:T(8,128)(2,1)S(1)}, bf16[128,768]{1,0:T(8,128)(2,1)S(1)}, u32[]{:S(2)}, u32[]{:S(2)}) %collective-permute-start.19) | collective-permute-done | bytes 196640 | tf_op jit(solution)/shard_map/ppermute | solution.py:504
  91.9 1.8 %collective-permute-done.16 = bf16[64,2048]{1,0:T(8,128)(2,1)S(1)} collective-permute-done((bf16[64,2048]{1,0:T(8,128)(2,1)S(1)}, bf16[64,2048]{1,0:T(8,128)(2,1)S(1)}, u32[]{:S(2)}, u32[]{:S(2)}) %collective-permute-start.16) | collective-permute-done | bytes 262176 | tf_op jit(solution)/shard_map/ppermute | solution.py:504
  93.7 0.1 collective-permute-done.15
  94.0 0.5 collective-permute-start.21
  94.5 2.8 %finish_own.1 = (f32[128,512]{1,0:T(8,128)}, f32[256,512]{1,0:T(8,128)}, f32[512,2048]{1,0:T(8,128)}, f32[512,512]{1,0:T(8,128)}) custom-call(s32[1]{0:T(128)} %bitcast.me_ref, bf16[256,128]{1,0:T(8,128)(2,1)S(1)} %get-tuple-element.52.chosen_ref, bf16[256,128]{1,0:T(8,128)(2,1)S(1)} %bitcast.9, ...), custom_call_target="tpu_custom_call" | custom-call | flops 100000000 | bytes 5000000 | tf_op jit(solution)/shard_map/finish_own/pallas_call | solution.py:437
  97.4 2.0 %finish_other.1 = (f32[256,512]{1,0:T(8,128)}, f32[512,2048]{1,0:T(8,128)}, f32[512,512]{1,0:T(8,128)}) custom-call(s32[1]{0:T(128)} %bitcast.me_ref, bf16[256,2048]{1,0:T(8,128)(2,1)S(1)} %collective-permute-done.20.early_ref, bf16[256,768]{1,0:T(8,128)(2,1)S(1)} %collective-permute-done.21.late_ref, ...), custom_call_target="tpu_custom_call", output_to_operand_aliasing={{0}: (3, {}), {1}: (4, {}), {2}: (5, {})} | custom-call | bytes 5000000 | tf_op jit(solution)/shard_map/finish_other/pallas_call | solution.py:447
  (34 shorter events, 0.7 us)
Async XLA Ops:
  2.0 14.4 %all-to-all-start = ((s32[32,1,2]{2,1,0:T(1,128)}), s32[32,1,2]{2,1,0:T(1,128)S(1)}, u32[]{:S(2)}, u32[]{:S(2)}) async-start(s32[32,1,2]{2,1,0:T(1,128)} %copy.18), calls=%async_computation | async-start | bytes 32768 | tf_op jit(solution)/shard_map/all_to_all | solution.py:500
  9.3 0.9 copy-start.2
  17.4 10.0 %all-to-all-start.1 = ((bf16[32,8,128]{2,1,0:T(8,128)(2,1)}), bf16[32,8,128]{2,1,0:T(8,128)(2,1)S(1)}, u32[]{:S(2)}, u32[]{:S(2)}) async-start(bf16[32,8,128]{2,1,0:T(8,128)(2,1)} %bitcast.5), calls=%async_computation.1 | async-start | bytes 131072 | tf_op jit(solution)/shard_map/all_to_all | solution.py:500
  27.4 0.6 copy-start.3
  42.5 3.6 %collective-permute-start = (bf16[256,2048]{1,0:T(8,128)(2,1)}, bf16[256,2048]{1,0:T(8,128)(2,1)S(1)}, u32[]{:S(2)}, u32[]{:S(2)}) collective-permute-start(bf16[256,2048]{1,0:T(8,128)(2,1)} %get-tuple-element.56), channel_id=1, source_target_pairs={{0,1},{1,0},{2,3},{3,2},{4,5},{5,4},{6,7},{7,6},{8,9},{9,8},{10,11... | collective-permute-start | bytes 3145736 | tf_op jit(solution)/shard_map/ppermute | solution.py:504
  42.7 3.3 %collective-permute-start.1 = (bf16[256,768]{1,0:T(8,128)(2,1)}, bf16[256,768]{1,0:T(8,128)(2,1)S(1)}, u32[]{:S(2)}, u32[]{:S(2)}) collective-permute-start(bf16[256,768]{1,0:T(8,128)(2,1)} %get-tuple-element.62), channel_id=1, source_target_pairs={{0,1},{1,0},{2,3},{3,2},{4,5},{5,4},{6,7},{7,6},{8,9},{9,8},{10,11... | collective-permute-start | bytes 1179656 | tf_op jit(solution)/shard_map/ppermute | solution.py:504
  43.1 1.2 %copy-start = (bf16[256,2048]{1,0:T(8,128)(2,1)S(1)}, bf16[256,2048]{1,0:T(8,128)(2,1)}, u32[]{:S(2)}) copy-start(bf16[256,2048]{1,0:T(8,128)(2,1)} %get-tuple-element.53.refs_0_) | copy-start | bytes 3145732
  44.3 1.0 %copy-start.1 = (bf16[256,768]{1,0:T(8,128)(2,1)S(1)}, bf16[256,768]{1,0:T(8,128)(2,1)}, u32[]{:S(2)}) copy-start(bf16[256,768]{1,0:T(8,128)(2,1)} %get-tuple-element.54.refs_1_) | copy-start | bytes 1179652
  46.4 7.0 %collective-permute-start.3 = (bf16[128,768]{1,0:T(8,128)(2,1)S(1)}, bf16[128,768]{1,0:T(8,128)(2,1)S(1)}, u32[]{:S(2)}, u32[]{:S(2)}) collective-permute-start(bf16[128,768]{1,0:T(8,128)(2,1)S(1)} %get-tuple-element.66), channel_id=1, source_target_pairs={{0,8},{1,9},{2,10},{3,11},{4,12},{5,13},{6,14},{7,15},{8,0},{9,1},... | collective-permute-start | bytes 589832 | tf_op jit(solution)/shard_map/ppermute | solution.py:504
  47.1 9.2 %collective-permute-start.2 = (bf16[64,2048]{1,0:T(8,128)(2,1)S(1)}, bf16[64,2048]{1,0:T(8,128)(2,1)S(1)}, u32[]{:S(2)}, u32[]{:S(2)}) collective-permute-start(bf16[64,2048]{1,0:T(8,128)(2,1)S(1)} %get-tuple-element.64), channel_id=1, source_target_pairs={{0,2},{1,3},{2,0},{3,1},{4,6},{5,7},{6,4},{7,5},{8,10},{9,11},{10,... | collective-permute-start | bytes 786440 | tf_op jit(solution)/shard_map/ppermute | solution.py:504
  47.5 13.4 %collective-permute-start.4 = (bf16[64,2048]{1,0:T(8,128)(2,1)S(1)}, bf16[64,2048]{1,0:T(8,128)(2,1)S(1)}, u32[]{:S(2)}, u32[]{:S(2)}) collective-permute-start(bf16[64,2048]{1,0:T(8,128)(2,1)S(1)} %get-tuple-element.69), channel_id=1, source_target_pairs={{0,4},{1,5},{2,6},{3,7},{4,0},{5,1},{6,2},{7,3},{8,12},{9,13},{10,... | collective-permute-start | bytes 786440 | tf_op jit(solution)/shard_map/ppermute | solution.py:504
  48.4 12.5 %collective-permute-start.5 = (bf16[64,2048]{1,0:T(8,128)(2,1)S(1)}, bf16[64,2048]{1,0:T(8,128)(2,1)S(1)}, u32[]{:S(2)}, u32[]{:S(2)}) collective-permute-start(bf16[64,2048]{1,0:T(8,128)(2,1)S(1)} %get-tuple-element.70), channel_id=1, source_target_pairs={{0,6},{1,7},{2,4},{3,5},{4,2},{5,3},{6,0},{7,1},{8,14},{9,15},{10,... | collective-permute-start | bytes 786440 | tf_op jit(solution)/shard_map/ppermute | solution.py:504
  53.4 7.5 %collective-permute-start.6 = (bf16[64,768]{1,0:T(8,128)(2,1)S(1)}, bf16[64,768]{1,0:T(8,128)(2,1)S(1)}, u32[]{:S(2)}, u32[]{:S(2)}) collective-permute-start(bf16[64,768]{1,0:T(8,128)(2,1)S(1)} %add_convert_fusion.2), channel_id=1, source_target_pairs={{0,16},{1,17},{2,18},{3,19},{4,20},{5,21},{6,22},{7,23},{8,24},{9,... | collective-permute-start | bytes 294920 | tf_op jit(solution)/shard_map/ppermute | solution.py:504
  56.3 14.5 %all-to-all-start.2 = ((bf16[32,8,128]{2,1,0:T(8,128)(2,1)}), bf16[32,8,128]{2,1,0:T(8,128)(2,1)S(1)}, u32[]{:S(2)}, u32[]{:S(2)}) async-start(bf16[32,8,128]{2,1,0:T(8,128)(2,1)} %bitcast.7), calls=%async_computation.2 | async-start | bytes 131072 | tf_op jit(solution)/shard_map/all_to_all | solution.py:500
  61.0 5.0 %collective-permute-start.7 = (bf16[16,2048]{1,0:T(8,128)(2,1)S(1)}, bf16[16,2048]{1,0:T(8,128)(2,1)S(1)}, u32[]{:S(2)}, u32[]{:S(2)}) collective-permute-start(bf16[16,2048]{1,0:T(8,128)(2,1)S(1)} %get-tuple-element.95), channel_id=1, source_target_pairs={{0,8},{1,9},{2,10},{3,11},{4,12},{5,13},{6,14},{7,15},{8,0},{9,1},... | collective-permute-start | bytes 196616 | tf_op jit(solution)/shard_map/ppermute | solution.py:504
  62.5 6.1 %collective-permute-start.9 = (bf16[16,2048]{1,0:T(8,128)(2,1)S(1)}, bf16[16,2048]{1,0:T(8,128)(2,1)S(1)}, u32[]{:S(2)}, u32[]{:S(2)}) collective-permute-start(bf16[16,2048]{1,0:T(8,128)(2,1)S(1)} %get-tuple-element.96), channel_id=1, source_target_pairs={{0,24},{1,25},{2,26},{3,27},{4,28},{5,29},{6,30},{7,31},{8,16},{9,... | collective-permute-start | bytes 196616 | tf_op jit(solution)/shard_map/ppermute | solution.py:504
  63.4 7.4 %collective-permute-start.8 = (bf16[16,2048]{1,0:T(8,128)(2,1)S(1)}, bf16[16,2048]{1,0:T(8,128)(2,1)S(1)}, u32[]{:S(2)}, u32[]{:S(2)}) collective-permute-start(bf16[16,2048]{1,0:T(8,128)(2,1)S(1)} %get-tuple-element.97), channel_id=1, source_target_pairs={{0,16},{1,17},{2,18},{3,19},{4,20},{5,21},{6,22},{7,23},{8,24},{9,... | collective-permute-start | bytes 196616 | tf_op jit(solution)/shard_map/ppermute | solution.py:504
  64.6 10.7 %collective-permute-start.13 = (bf16[64,768]{1,0:T(8,128)(2,1)S(1)}, bf16[64,768]{1,0:T(8,128)(2,1)S(1)}, u32[]{:S(2)}, u32[]{:S(2)}) collective-permute-start(bf16[64,768]{1,0:T(8,128)(2,1)S(1)} %add_convert_fusion.1), channel_id=1, source_target_pairs={{0,4},{1,5},{2,6},{3,7},{4,0},{5,1},{6,2},{7,3},{8,12},{9,13},{10,... | collective-permute-start | bytes 294920 | tf_op jit(solution)/shard_map/ppermute | solution.py:504
  70.8 6.6 %collective-permute-start.12 = (bf16[16,2048]{1,0:T(8,128)(2,1)S(1)}, bf16[16,2048]{1,0:T(8,128)(2,1)S(1)}, u32[]{:S(2)}, u32[]{:S(2)}) collective-permute-start(bf16[16,2048]{1,0:T(8,128)(2,1)S(1)} %multiply_convert_fusion.1), channel_id=1, source_target_pairs={{0,24},{1,25},{2,26},{3,27},{4,28},{5,29},{6,30},{7,31},{8,16},{9,... | collective-permute-start | bytes 196616 | tf_op jit(solution)/shard_map/ppermute | solution.py:504
  72.5 6.5 %collective-permute-start.11 = (bf16[16,2048]{1,0:T(8,128)(2,1)S(1)}, bf16[16,2048]{1,0:T(8,128)(2,1)S(1)}, u32[]{:S(2)}, u32[]{:S(2)}) collective-permute-start(bf16[16,2048]{1,0:T(8,128)(2,1)S(1)} %multiply_convert_fusion.1), channel_id=1, source_target_pairs={{0,16},{1,17},{2,18},{3,19},{4,20},{5,21},{6,22},{7,23},{8,24},{9,... | collective-permute-start | bytes 196616 | tf_op jit(solution)/shard_map/ppermute | solution.py:504
  72.5 6.5 %collective-permute-start.10 = (bf16[16,2048]{1,0:T(8,128)(2,1)S(1)}, bf16[16,2048]{1,0:T(8,128)(2,1)S(1)}, u32[]{:S(2)}, u32[]{:S(2)}) collective-permute-start(bf16[16,2048]{1,0:T(8,128)(2,1)S(1)} %multiply_convert_fusion.1), channel_id=1, source_target_pairs={{0,8},{1,9},{2,10},{3,11},{4,12},{5,13},{6,14},{7,15},{8,0},{9,1},... | collective-permute-start | bytes 196616 | tf_op jit(solution)/shard_map/ppermute | solution.py:504
  75.3 4.7 %collective-permute-start.14 = (bf16[64,768]{1,0:T(8,128)(2,1)S(1)}, bf16[64,768]{1,0:T(8,128)(2,1)S(1)}, u32[]{:S(2)}, u32[]{:S(2)}) collective-permute-start(bf16[64,768]{1,0:T(8,128)(2,1)S(1)} %add_convert_fusion), channel_id=1, source_target_pairs={{0,2},{1,3},{2,0},{3,1},{4,6},{5,7},{6,4},{7,5},{8,10},{9,11},{10,... | collective-permute-start | bytes 294920 | tf_op jit(solution)/shard_map/ppermute | solution.py:504
  80.0 6.1 %collective-permute-start.18 = (bf16[64,768]{1,0:T(8,128)(2,1)S(1)}, bf16[64,768]{1,0:T(8,128)(2,1)S(1)}, u32[]{:S(2)}, u32[]{:S(2)}) collective-permute-start(bf16[64,768]{1,0:T(8,128)(2,1)S(1)} %multiply_convert_fusion), channel_id=1, source_target_pairs={{0,16},{1,17},{2,18},{3,19},{4,20},{5,21},{6,22},{7,23},{8,24},{9,... | collective-permute-start | bytes 294920 | tf_op jit(solution)/shard_map/ppermute | solution.py:504
  80.3 11.6 %collective-permute-start.17 = (bf16[64,2048]{1,0:T(8,128)(2,1)S(1)}, bf16[64,2048]{1,0:T(8,128)(2,1)S(1)}, u32[]{:S(2)}, u32[]{:S(2)}) collective-permute-start(bf16[64,2048]{1,0:T(8,128)(2,1)S(1)} %pad_maximum_fusion.1), channel_id=1, source_target_pairs={{0,6},{1,7},{2,4},{3,5},{4,2},{5,3},{6,0},{7,1},{8,14},{9,15},{10,... | collective-permute-start | bytes 786440 | tf_op jit(solution)/shard_map/ppermute | solution.py:504
  82.7 11.0 %collective-permute-start.16 = (bf16[64,2048]{1,0:T(8,128)(2,1)S(1)}, bf16[64,2048]{1,0:T(8,128)(2,1)S(1)}, u32[]{:S(2)}, u32[]{:S(2)}) collective-permute-start(bf16[64,2048]{1,0:T(8,128)(2,1)S(1)} %pad_maximum_fusion.1), channel_id=1, source_target_pairs={{0,4},{1,5},{2,6},{3,7},{4,0},{5,1},{6,2},{7,3},{8,12},{9,13},{10,... | collective-permute-start | bytes 786440 | tf_op jit(solution)/shard_map/ppermute | solution.py:504
  83.2 10.7 %collective-permute-start.15 = (bf16[64,2048]{1,0:T(8,128)(2,1)S(1)}, bf16[64,2048]{1,0:T(8,128)(2,1)S(1)}, u32[]{:S(2)}, u32[]{:S(2)}) collective-permute-start(bf16[64,2048]{1,0:T(8,128)(2,1)S(1)} %pad_maximum_fusion.1), channel_id=1, source_target_pairs={{0,2},{1,3},{2,0},{3,1},{4,6},{5,7},{6,4},{7,5},{8,10},{9,11},{10,... | collective-permute-start | bytes 786440 | tf_op jit(solution)/shard_map/ppermute | solution.py:504
  86.1 5.7 %collective-permute-start.19 = (bf16[128,768]{1,0:T(8,128)(2,1)S(1)}, bf16[128,768]{1,0:T(8,128)(2,1)S(1)}, u32[]{:S(2)}, u32[]{:S(2)}) collective-permute-start(bf16[128,768]{1,0:T(8,128)(2,1)S(1)} %pad_maximum_fusion.2), channel_id=1, source_target_pairs={{0,8},{1,9},{2,10},{3,11},{4,12},{5,13},{6,14},{7,15},{8,0},{9,1},... | collective-permute-start | bytes 589832 | tf_op jit(solution)/shard_map/ppermute | solution.py:504
  93.9 3.4 %collective-permute-start.20 = (bf16[256,2048]{1,0:T(8,128)(2,1)S(1)}, bf16[256,2048]{1,0:T(8,128)(2,1)S(1)}, u32[]{:S(2)}, u32[]{:S(2)}) collective-permute-start(bf16[256,2048]{1,0:T(8,128)(2,1)S(1)} %constant_dynamic-update-slice_fusion.early_ref), channel_id=1, source_target_pairs={{0,1},{1,0},{2,3},{3,2},{4,5},{5,4},{6,7},{7,6},{8,9},{9,8},{10,11... | collective-permute-start | bytes 3145736 | tf_op jit(solution)/shard_map/ppermute | solution.py:504
  94.0 3.3 %collective-permute-start.21 = (bf16[256,768]{1,0:T(8,128)(2,1)S(1)}, bf16[256,768]{1,0:T(8,128)(2,1)S(1)}, u32[]{:S(2)}, u32[]{:S(2)}) collective-permute-start(bf16[256,768]{1,0:T(8,128)(2,1)S(1)} %pad_maximum_fusion.late_ref), channel_id=1, source_target_pairs={{0,1},{1,0},{2,3},{3,2},{4,5},{5,4},{6,7},{7,6},{8,9},{9,8},{10,11... | collective-permute-start | bytes 1179656 | tf_op jit(solution)/shard_map/ppermute | solution.py:504

commit v4 on v3

--- a/solution.py
+++ b/solution.py
@@ -160,39 +160,34 @@
     )(asked, table)
 
 
-def layer_kernel(
-    me_ref, lengths_ref, slot_ref, leaf_ref, rows_ref, table_hbm, in_hbm, out_hbm, tangent_hbm,
-    output_hbm, d_rows_ref, keep_hbm, send_hbm, keep_late_hbm, send_late_hbm,
-    inputs, gated, d_pre, grads, output,
-    normed, turned, moved, hidden, slope, weights, weights_slope, mixed, d_mixed,
-    d_score, d_gated, allowed, allowed_scale, keys_t, values_t, d_inputs, leaf_grad, table, w_in, w_out, tangent, sems, out_sems,
-):
-    count, width = inputs.shape
-    head = width // HEADS
-    half_scale = 0.5 * head ** (-0.5)
-    half_rows = width // 2
+def start_all(sems, *pairs):
     copies = [
         pltpu.make_async_copy(source, target, sems.at[k])
-        for k, (source, target) in enumerate(
-            ((table_hbm, table), (in_hbm, w_in), (out_hbm, w_out), (tangent_hbm, tangent))
-        )
+        for k, (source, target) in enumerate(pairs)
     ]
     for copy in copies:
         copy.start()
-    leaving = []
-
-    def leave(source, target):
-        copy = pltpu.make_async_copy(source, target, out_sems.at[len(leaving)])
-        copy.start()
-        leaving.append(copy)
-
-    rows = from_tiles(rows_ref[...], width)
-    picker, onehot = pickers(rows.shape[0], slot_ref, leaf_ref, table.shape[0])
+    return copies
+
+
+def prepare_kernel(
+    lengths_ref, slot_ref, leaf_ref, table_hbm, out_hbm, tangent_hbm,
+    picker_ref, onehot_ref, leaf_sum_ref, allowed, allowed_scale, d_gated_ref,
+    table, w_out, tangent, sems,
+):
+    count, width = d_gated_ref.shape
+    half_scale = 0.5 * (width // HEADS) ** (-0.5)
+    loads = start_all(sems, (table_hbm, table), (out_hbm, w_out), (tangent_hbm, tangent))
+    picker, onehot = pickers(picker_ref.shape[0], slot_ref, leaf_ref, table.shape[0])
+    picker_ref[...] = picker
+    onehot_ref[...] = onehot
     ends = []
     total = 0
     for place in range(lengths_ref.shape[1]):
         total = total + lengths_ref[0, place]
         ends.append(total)
+    allowed[...] = jnp.zeros_like(allowed)
+    allowed_scale[...] = jnp.zeros_like(allowed_scale)
     for start, low, high in spans(count):
         at = slice(start, start + BLOCK)
         row = start + lax.broadcasted_iota(jnp.int32, (BLOCK, high - low), 0)
@@ -203,13 +198,79 @@
         seen = jnp.logical_and(column >= first, column <= row)
         allowed[at, low:high] = jnp.where(seen, 1.0, 0.0).astype(bf16)
         allowed_scale[at, low:high] = jnp.where(seen, 2.0 * half_scale, 0.0).astype(bf16)
-    copies[0].wait()
-    inputs[...] = (mm_tn(picker, rows) + mm_tn(onehot, table[...])).astype(bf16)
+    loads[0].wait()
+    leaf_sum_ref[...] = mm_tn(onehot, table[...])
+    loads[1].wait()
+    loads[2].wait()
+    d_gated_ref[...] = mm_nt(tangent[...], w_out[...]).astype(bf16)
+
+
+def run_prepare(lengths, slot, leaf, table, w_out, tangent, slots):
+    count, width = tangent.shape
+    smem = pl.BlockSpec(memory_space=pltpu.SMEM)
+    vmem = pl.BlockSpec(memory_space=pltpu.VMEM)
+    hbm = pl.BlockSpec(memory_space=pltpu.HBM)
+    shape = jax.ShapeDtypeStruct
+    return pl.pallas_call(
+        prepare_kernel,
+        name="prepare",
+        out_shape=(
+            shape((slots, count), bf16),
+            shape((table.shape[0], count), bf16),
+            shape((count, width), f32),
+            shape((count, count), bf16),
+            shape((count, count), bf16),
+            shape((count, width), bf16),
+        ),
+        in_specs=[smem, vmem, vmem] + [hbm] * 3,
+        out_specs=(vmem,) * 6,
+        scratch_shapes=[
+            pltpu.VMEM(table.shape, bf16),
+            pltpu.VMEM(w_out.shape, bf16),
+            pltpu.VMEM(tangent.shape, bf16),
+            pltpu.SemaphoreType.DMA((3,)),
+        ],
+        compiler_params=pltpu.CompilerParams(vmem_limit_bytes=LAYER_VMEM),
+        cost_estimate=pl.CostEstimate(flops=6 * 10**8, bytes_accessed=5 * 10**6, transcendentals=0),
+    )(lengths, slot, leaf, table, w_out, tangent)
+
+
+def layer_kernel(
+    me_ref, rows_hbm, picker_hbm, onehot_hbm, leaf_sum_hbm, allowed_hbm, allowed_scale_hbm,
+    d_gated_hbm, in_hbm, tangent_hbm,
+    inputs_hbm, gated_hbm, d_rows_ref, keep_hbm, send_hbm, keep_late_hbm, send_late_hbm,
+    inputs, gated, d_pre, grads,
+    normed, turned, moved, hidden, slope, weights, weights_slope, mixed, d_mixed,
+    d_score, rows, picker, onehot, leaf_sum, allowed, allowed_scale, d_gated, w_in, tangent,
+    keys_t, values_t, d_inputs, leaf_grad, sems, out_sems,
+):
+    count, width = inputs.shape
+    head = width // HEADS
+    half_scale = 0.5 * head ** (-0.5)
+    half_rows = width // 2
+    loads = start_all(
+        sems,
+        (rows_hbm, rows), (picker_hbm, picker), (leaf_sum_hbm, leaf_sum), (in_hbm, w_in),
+        (allowed_hbm, allowed), (allowed_scale_hbm, allowed_scale), (d_gated_hbm, d_gated),
+        (tangent_hbm, tangent), (onehot_hbm, onehot),
+    )
+    leaving = []
+
+    def leave(source, target):
+        copy = pltpu.make_async_copy(source, target, out_sems.at[len(leaving)])
+        copy.start()
+        leaving.append(copy)
+
+    for load in loads[:3]:
+        load.wait()
+    fetched = from_tiles(rows[...], width)
+    inputs[...] = (mm_tn(picker[...], fetched) + leaf_sum[...]).astype(bf16)
+    leave(inputs, inputs_hbm)
     for at in strips(0, count):
         values, scale = center(inputs[at, :].astype(f32))
         normed[at, :] = (values * scale).astype(bf16)
     turned[...] = normed[...].T
-    copies[1].wait()
+    loads[3].wait()
     for start in range(0, 4 * width, 2 * BLOCK):
         to = slice(start, start + 2 * BLOCK)
         halves = mm(normed[...], w_in[:, to]) * 0.5
@@ -217,6 +278,8 @@
             value, slope_at = silu(halves[at, :])
             hidden[at, to] = value
             slope[at, to] = slope_at
+    for load in loads[4:]:
+        load.wait()
     keys_t[...] = hidden[:, 3 * width :].T
     values_t[...] = hidden[:, width : 2 * width].T
     for start, low, high in spans(count):
@@ -246,9 +309,6 @@
             mixed[at, h * head : (h + 1) * head] = mm(
                 weights[h, at, :high], hidden[:high, value_at]
             )
-    copies[2].wait()
-    copies[3].wait()
-    d_gated[...] = mm_nt(tangent[...], w_out[...]).astype(bf16)
     for at in strips(0, count):
         values, scale = center(mixed[at, :])
         values = values * scale
@@ -283,39 +343,43 @@
         grads[:, to] = mm(moved[...], d_pre[:, to]).astype(bf16)
     leave(grads.at[half_rows:, :SPLIT], send_hbm)
     leave(grads.at[:half_rows, :SPLIT], keep_hbm)
+    leave(gated, gated_hbm)
     turned[...] = gated[...].T
     permute_rows(late, turned, moved)
     grads[:, 4 * width : 5 * width] = mm(moved[...], tangent[...]).astype(bf16)
-    output[...] = (mm(gated[...], w_out[...]) + inputs[...].astype(f32)).astype(bf16)
-    leave(output, output_hbm)
     normed_change = mm_nt(d_pre[...], w_in[...])
     for at in strips(0, count):
         values, scale = center(inputs[at, :].astype(f32))
         change = pull_normalize(normed_change[at, :], values * scale, scale)
         d_inputs[at, :] = (change + tangent[at, :].astype(f32)).astype(bf16)
-    leaves = table.shape[0]
-    d_leaf = mm(onehot, d_inputs[...]).astype(bf16)
+    leaves = onehot.shape[0]
+    d_leaf = mm(onehot[...], d_inputs[...]).astype(bf16)
     leaf_grad[:leaves, :] = d_leaf[:, : width // 2]
     leaf_grad[leaves:, :] = d_leaf[:, width // 2 :]
     permute_rows(late, leaf_grad, grads.at[:, 5 * width :])
     leave(grads.at[half_rows:, SPLIT:], send_late_hbm)
     leave(grads.at[:half_rows, SPLIT:], keep_late_hbm)
-    d_rows_ref[...] = to_tiles(mm(picker, d_inputs[...]).astype(bf16))
+    d_rows_ref[...] = to_tiles(mm(picker[...], d_inputs[...]).astype(bf16))
     for copy in leaving:
         copy.wait()
 
 
-def run_layer(me, lengths, slot, leaf, rows, table, w_in, w_out, tangent):
+def run_layer(me, rows, prepared, w_in, tangent):
+    picker, onehot, leaf_sum, allowed, allowed_scale, d_gated = prepared
     count, width = tangent.shape
     smem = pl.BlockSpec(memory_space=pltpu.SMEM)
     vmem = pl.BlockSpec(memory_space=pltpu.VMEM)
     hbm = pl.BlockSpec(memory_space=pltpu.HBM)
     shape = jax.ShapeDtypeStruct
     columns = 5 * width + width // 2
+    operands = (
+        rows, picker, onehot, leaf_sum, allowed, allowed_scale, d_gated, w_in, tangent
+    )
     return pl.pallas_call(
         layer_kernel,
         name="layer",
         out_shape=(
+            shape((count, width), bf16),
             shape((count, width), bf16),
             shape(rows.shape, bf16),
             shape((width // 2, SPLIT), bf16),
@@ -323,14 +387,13 @@
             shape((width // 2, columns - SPLIT), bf16),
             shape((width // 2, columns - SPLIT), bf16),
         ),
-        in_specs=[smem, smem] + [vmem] * 3 + [hbm] * 4,
-        out_specs=(hbm, vmem, hbm, hbm, hbm, hbm),
+        in_specs=[smem] + [hbm] * 9,
+        out_specs=(hbm, hbm, vmem) + (hbm,) * 4,
         scratch_shapes=[
             pltpu.VMEM((count, width), bf16),
             pltpu.VMEM((count, width), bf16),
             pltpu.VMEM((count, 4 * width), bf16),
             pltpu.VMEM((width, columns), bf16),
-            pltpu.VMEM((count, width), bf16),
             pltpu.VMEM((count, width), bf16),
             pltpu.VMEM((width, count), bf16),
             pltpu.VMEM((width, count), bf16),
@@ -341,23 +404,24 @@
             pltpu.VMEM((count, width), f32),
             pltpu.VMEM((count, width), bf16),
             pltpu.VMEM((HEADS, count, count), bf16),
-            pltpu.VMEM((count, width), bf16),
-            pltpu.VMEM((count, count), bf16),
-            pltpu.VMEM((count, count), bf16),
+        ]
+        + [
+            pltpu.VMEM(array.shape, array.dtype)
+            for array in (
+                rows, picker, onehot, leaf_sum, allowed, allowed_scale, d_gated, w_in, tangent
+            )
+        ]
+        + [
             pltpu.VMEM((width, count), bf16),
             pltpu.VMEM((width, count), bf16),
             pltpu.VMEM((count, width), bf16),
             pltpu.VMEM((width, width // 2), bf16),
-            pltpu.VMEM(table.shape, bf16),
-            pltpu.VMEM(w_in.shape, bf16),
-            pltpu.VMEM(w_out.shape, bf16),
-            pltpu.VMEM(tangent.shape, bf16),
-            pltpu.SemaphoreType.DMA((4,)),
-            pltpu.SemaphoreType.DMA((5,)),
+            pltpu.SemaphoreType.DMA((9,)),
+            pltpu.SemaphoreType.DMA((6,)),
         ],
         compiler_params=pltpu.CompilerParams(vmem_limit_bytes=LAYER_VMEM),
-        cost_estimate=pl.CostEstimate(flops=6 * 10**9, bytes_accessed=10**7, transcendentals=10**6),
-    )(me, lengths, slot, leaf, rows, table, w_in, w_out, tangent)
+        cost_estimate=pl.CostEstimate(flops=5 * 10**9, bytes_accessed=10**7, transcendentals=10**6),
+    )(me, *operands)
 
 
 def write_chunks(me, half, early_ref, late_ref, leaf_hbm, in_hbm, out_hbm, grads, sems):
@@ -540,7 +604,7 @@
     return jnp.concatenate([block] + pieces, axis=0)
 
 
-def reduce_and_gather(early, late, d_rows, count):
+def reduce_and_gather(early, late, d_rows, inputs, gated, w_out, count):
     _, near, far = EARLY
     _, first, second = LATE
     early_other, late_other = swap(early[1], 1, count), swap(late[1], 1, count)
@@ -565,10 +629,12 @@
     early = join(early, far, count)
     early, late = lax.optimization_barrier((early, (late * (1.0 / count)).astype(bf16)))
     pieces = swap_all([early] * (2 ** len(near) - 1), near, count)
-    late = join(join(late, second, count), first, count)
-    pieces, late = lax.optimization_barrier((pieces, late))
+    late, gated = lax.optimization_barrier((join(late, second, count), gated))
+    output = (mm(gated, w_out) + inputs.astype(f32)).astype(bf16)
+    late = join(late, first, count)
+    pieces, late, output = lax.optimization_barrier((pieces, late, output))
     early = jnp.concatenate([early] + pieces, axis=0)
-    return returned, early, swap(early, 1, count), late, swap(late, 1, count)
+    return returned, early, swap(early, 1, count), late, swap(late, 1, count), output
 
 
 def on_device(
@@ -583,11 +649,12 @@
     (table,) = run_load(item_table)
     fetched, chosen = run_lookup(asked, table)
     arrived = exchange(fetched)
-    output, d_rows, keep, send, keep_late, send_late = run_layer(
-        me, lengths, slot, leaf, arrived, leaf_table, w_in, w_out, cotangent
-    )
-    returned, early, early_other, late, late_other = reduce_and_gather(
-        (keep, send), (keep_late, send_late), d_rows, count
+    prepared = run_prepare(
+        lengths, slot, leaf, leaf_table, w_out, cotangent, requests.shape[1] * requests.shape[2]
+    )
+    inputs, gated, d_rows, *halves = run_layer(me, arrived, prepared, w_in, cotangent)
+    returned, early, early_other, late, late_other, output = reduce_and_gather(
+        halves[:2], halves[2:], d_rows, inputs, gated, w_out, count
     )
     table_grad, leaf_mean, in_mean, out_mean = run_finish(
         me, chosen, returned, early, early_other, late, late_other, leaf_table.shape[0]

time: 100 us -> 102 us (1.020)
  waiting for transfers between devices: 38.7 us -> 33.7 us
  Pallas kernels: 20.8 us -> 24 us
  other arithmetic: 0.36 us -> 1.93 us
  matrix products: 0 us -> 1.23 us
    all_to_all x3, waiting for transfers between devices: 13.6 us -> 9.88 us  [exchange(): lax.all_to_all(blocks, ('dp', 'rep'), split_axis=0, concat_axis=0, tiled=...]
    pallas_call x0 -> x1, Pallas kernels: none -> 3.67 us  [run_prepare(): pl.pallas_call(prepare_kernel, name='prepare', out_shape=(shape((slots, c...]
    ppermute x22, waiting for transfers between devices: 25.1 us -> 23.8 us  [swap(): lax.ppermute(block, ('dp', 'rep'), [(i, i ^ mask) for i in range(count)])]
    dot_general x0 -> x1, matrix products: none -> 1.23 us  [dot(): lax.dot_general(a, b, ((contract[0], contract[1]), ((), ())), preferred_e...]
    unnamed x11 -> x19, local copies, waits for them, and re-layouts: 3.8 us -> 3.82 us
  transfers between devices with their start and end apart: 25 -> 25, of which waited for: 15 -> 14; matrix products, arithmetic and copies ran while one was open for 0% -> 4% of each run, Pallas kernels for 3% -> 7%
where the time goes in v4:
time: 102 us; the launch traced here: 101 us
  waiting for transfers between devices  33.7 us (33%)
  starting transfers between devices  33.2 us (33%)
  Pallas kernels  24 us (24%)
  local copies, waits for them, and re-layouts  6.12 us (6%)
  other arithmetic  1.93 us (2%)
  matrix products  1.23 us (1%)
  between operations  1.05 us (1%)
    ppermute x22, waiting for transfers between devices, swap(): lax.ppermute(block, ('dp', 'rep'), [(i, i ^ mask) for i in range(count)])  23.8 us
    ppermute x22, starting transfers between devices, swap(): lax.ppermute(block, ('dp', 'rep'), [(i, i ^ mask) for i in range(count)])  20.5 us
    pallas_call x1, Pallas kernels, run_layer(): pl.pallas_call(layer_kernel, name='layer', out_shape=(shape((count, width...  14 us
    all_to_all x3, starting transfers between devices, exchange(): lax.all_to_all(blocks, ('dp', 'rep'), split_axis=0, concat_axis=0, tiled=...  12.6 us
    all_to_all x3, waiting for transfers between devices, exchange(): lax.all_to_all(blocks, ('dp', 'rep'), split_axis=0, concat_axis=0, tiled=...  9.88 us
    unnamed x19, local copies, waits for them, and re-layouts  3.82 us
    pallas_call x1, Pallas kernels, run_prepare(): pl.pallas_call(prepare_kernel, name='prepare', out_shape=(shape((slots, c...  3.67 us
    pallas_call x1, Pallas kernels, run_finish(): pl.pallas_call(finish_own_kernel, name='finish_own', out_shape=shapes, in...  2.84 us
  transfers between devices with their start and end apart: 25, of which 14 were waited for; matrix products, arithmetic and copies ran while one was open for 4% of the time, Pallas kernels for 7%

profile of v4, /device:TPU:0, one launch (start us, length us, event | category | flops | bytes accessed | tf_op | source)
XLA Modules:
  0.0 101.2 jit_solution(16833842924341905621)
XLA Ops:
  0.6 1.4 %copy.18 = s32[32,1,2]{2,1,0:T(1,128)} copy(s32[32,1,2]{0,2,1:T(2,128)} %bitcast.14) | data formatting | bytes 512 | tf_op jit(solution)/shard_map/all_to_all | solution.py:564
  2.0 7.3 %all-to-all-start = ((s32[32,1,2]{2,1,0:T(1,128)}), s32[32,1,2]{2,1,0:T(1,128)S(1)}, u32[]{:S(2)}, u32[]{:S(2)}) async-start(s32[32,1,2]{2,1,0:T(1,128)} %copy.18), calls=%async_computation | async-start | bytes 32768 | tf_op jit(solution)/shard_map/all_to_all | solution.py:564
  9.3 0.9 copy-done.2
  10.2 6.2 %all-to-all-done = s32[32,1,2]{2,1,0:T(1,128)S(1)} async-done(((s32[32,1,2]{2,1,0:T(1,128)}), s32[32,1,2]{2,1,0:T(1,128)S(1)}, u32[]{:S(2)}, u32[]{:S(2)}) %all-to-all-start) | async-done | bytes 288 | tf_op jit(solution)/shard_map/all_to_all | solution.py:564
  16.4 1.0 %lookup.1 = (bf16[256,128]{1,0:T(8,128)(2,1)}, bf16[256,128]{1,0:T(8,128)(2,1)S(1)}) custom-call(s32[32,2]{1,0:T(8,128)S(1)} %bitcast.12, bf16[128,512]{1,0:T(8,128)(2,1)S(1)} %load.2.table_ref), custom_call_target="tpu_custom_call" | custom-call | tf_op jit(solution)/shard_map/lookup/pallas_call | solution.py:150
  17.4 2.6 %all-to-all-start.1 = ((bf16[32,8,128]{2,1,0:T(8,128)(2,1)}), bf16[32,8,128]{2,1,0:T(8,128)(2,1)S(1)}, u32[]{:S(2)}, u32[]{:S(2)}) async-start(bf16[32,8,128]{2,1,0:T(8,128)(2,1)} %bitcast.3), calls=%async_computation.1 | async-start | bytes 131072 | tf_op jit(solution)/shard_map/all_to_all | solution.py:564
  20.0 3.7 %prepare.1 = (bf16[64,512]{1,0:T(8,128)(2,1)}, bf16[256,512]{1,0:T(8,128)(2,1)}, f32[512,512]{1,0:T(8,128)}, bf16[512,512]{1,0:T(8,128)(2,1)}, bf16[512,512]{1,0:T(8,128)(2,1)}, /*index=5*/bf16[512,512]{1,0:T(8,128)(2,1)}) custom-call(s32[1,4]{1,0:T(1,128)} %lengths_ref.1, s32[1,512]{1,0:T(1,128)} %bitcast.16, s32[8,512]{1,0:T(8,128)} %bitcast.15, ...), custom_call_target="tpu_custom_call" | custom-call | flops 600000000 | bytes 5000000 | tf_op jit(solution)/shard_map/prepare/pallas_call | solution.py:214
  23.7 3.7 %all-to-all-done.1 = bf16[32,8,128]{2,1,0:T(8,128)(2,1)S(1)} async-done(((bf16[32,8,128]{2,1,0:T(8,128)(2,1)}), bf16[32,8,128]{2,1,0:T(8,128)(2,1)S(1)}, u32[]{:S(2)}, u32[]{:S(2)}) %all-to-all-start.1) | async-done | bytes 65568 | tf_op jit(solution)/shard_map/all_to_all | solution.py:564
  27.4 0.6 copy-done.7
  28.0 14.0 %layer.1 = (bf16[512,512]{1,0:T(8,128)(2,1)}, bf16[512,512]{1,0:T(8,128)(2,1)}, bf16[256,128]{1,0:T(8,128)(2,1)}, bf16[256,2048]{1,0:T(8,128)(2,1)}, bf16[256,20...) custom-call(s32[1]{0:T(128)} %bitcast.me_ref, bf16[256,128]{1,0:T(8,128)(2,1)} %bitcast.13, ...), custom_call_target="tpu_custom_call" | custom-call | flops 5000000000 | bytes 10000000 | tf_op jit(solution)/shard_map/layer/pallas_call | solution.py:378
  42.6 1.2 %copy-done = bf16[256,2048]{1,0:T(8,128)(2,1)S(1)} copy-done((bf16[256,2048]{1,0:T(8,128)(2,1)S(1)}, bf16[256,2048]{1,0:T(8,128)(2,1)}, u32[]{:S(2)}) %copy-start) | copy-done | bytes 1048600
  43.9 1.0 copy-done.1
  45.0 0.6 collective-permute-done.1.other_ref
  45.9 0.7 collective-permute-start.3
  46.6 0.4 collective-permute-start.2
  47.0 0.9 collective-permute-start.4
  47.9 2.2 %collective-permute-start.5 = (bf16[64,2048]{1,0:T(8,128)(2,1)S(1)}, bf16[64,2048]{1,0:T(8,128)(2,1)S(1)}, u32[]{:S(2)}, u32[]{:S(2)}) collective-permute-start(bf16[64,2048]{1,0:T(8,128)(2,1)S(1)} %get-tuple-element.84), channel_id=1, source_target_pairs={{0,6},{1,7},{2,4},{3,5},{4,2},{5,3},{6,0},{7,1},{8,14},{9,15},{10,... | collective-permute-start | bytes 786440 | tf_op jit(solution)/shard_map/ppermute | solution.py:568
  50.1 2.8 %collective-permute-done.3 = bf16[128,768]{1,0:T(8,128)(2,1)S(1)} collective-permute-done((bf16[128,768]{1,0:T(8,128)(2,1)S(1)}, bf16[128,768]{1,0:T(8,128)(2,1)S(1)}, u32[]{:S(2)}, u32[]{:S(2)}) %collective-permute-start.3) | collective-permute-done | bytes 196640 | tf_op jit(solution)/shard_map/ppermute | solution.py:568
  52.9 0.7 add_convert_fusion.2
  53.6 0.7 collective-permute-start.6
  54.3 1.5 %collective-permute-done.2 = bf16[64,2048]{1,0:T(8,128)(2,1)S(1)} collective-permute-done((bf16[64,2048]{1,0:T(8,128)(2,1)S(1)}, bf16[64,2048]{1,0:T(8,128)(2,1)S(1)}, u32[]{:S(2)}, u32[]{:S(2)}) %collective-permute-start.2) | collective-permute-done | bytes 262176 | tf_op jit(solution)/shard_map/ppermute | solution.py:568
  55.8 2.7 %all-to-all-start.2 = ((bf16[32,8,128]{2,1,0:T(8,128)(2,1)}), bf16[32,8,128]{2,1,0:T(8,128)(2,1)S(1)}, u32[]{:S(2)}, u32[]{:S(2)}) async-start(bf16[32,8,128]{2,1,0:T(8,128)(2,1)} %bitcast.7), calls=%async_computation.2 | async-start | bytes 131072 | tf_op jit(solution)/shard_map/all_to_all | solution.py:564
  58.5 0.9 slice.62
  59.5 1.0 collective-permute-done.4
  60.4 0.5 collective-permute-done.6
  61.1 1.0 collective-permute-start.7
  62.0 1.8 %collective-permute-start.9 = (bf16[16,2048]{1,0:T(8,128)(2,1)S(1)}, bf16[16,2048]{1,0:T(8,128)(2,1)S(1)}, u32[]{:S(2)}, u32[]{:S(2)}) collective-permute-start(bf16[16,2048]{1,0:T(8,128)(2,1)S(1)} %get-tuple-element.116), channel_id=1, source_target_pairs={{0,24},{1,25},{2,26},{3,27},{4,28},{5,29},{6,30},{7,31},{8,16},{9,... | collective-permute-start | bytes 196616 | tf_op jit(solution)/shard_map/ppermute | solution.py:568
  63.8 0.8 collective-permute-start.8
  64.6 0.9 add_convert_fusion.1
  65.6 0.9 collective-permute-start.13
  66.4 1.9 %collective-permute-done.9 = bf16[16,2048]{1,0:T(8,128)(2,1)S(1)} collective-permute-done((bf16[16,2048]{1,0:T(8,128)(2,1)S(1)}, bf16[16,2048]{1,0:T(8,128)(2,1)S(1)}, u32[]{:S(2)}, u32[]{:S(2)}) %collective-permute-start.9) | collective-permute-done | bytes 65568 | tf_op jit(solution)/shard_map/ppermute | solution.py:568
  68.3 2.5 %collective-permute-done.8 = bf16[16,2048]{1,0:T(8,128)(2,1)S(1)} collective-permute-done((bf16[16,2048]{1,0:T(8,128)(2,1)S(1)}, bf16[16,2048]{1,0:T(8,128)(2,1)S(1)}, u32[]{:S(2)}, u32[]{:S(2)}) %collective-permute-start.8) | collective-permute-done | bytes 65568 | tf_op jit(solution)/shard_map/ppermute | solution.py:568
  70.9 2.3 %collective-permute-start.12 = (bf16[16,2048]{1,0:T(8,128)(2,1)S(1)}, bf16[16,2048]{1,0:T(8,128)(2,1)S(1)}, u32[]{:S(2)}, u32[]{:S(2)}) collective-permute-start(bf16[16,2048]{1,0:T(8,128)(2,1)S(1)} %multiply_convert_fusion.1), channel_id=1, source_target_pairs={{0,24},{1,25},{2,26},{3,27},{4,28},{5,29},{6,30},{7,31},{8,16},{9,... | collective-permute-start | bytes 196616 | tf_op jit(solution)/shard_map/ppermute | solution.py:568
  73.1 2.2 %collective-permute-start.10 = (bf16[16,2048]{1,0:T(8,128)(2,1)S(1)}, bf16[16,2048]{1,0:T(8,128)(2,1)S(1)}, u32[]{:S(2)}, u32[]{:S(2)}) collective-permute-start(bf16[16,2048]{1,0:T(8,128)(2,1)S(1)} %multiply_convert_fusion.1), channel_id=1, source_target_pairs={{0,8},{1,9},{2,10},{3,11},{4,12},{5,13},{6,14},{7,15},{8,0},{9,1},... | collective-permute-start | bytes 196616 | tf_op jit(solution)/shard_map/ppermute | solution.py:568
  75.4 1.3 %collective-permute-start.14 = (bf16[64,768]{1,0:T(8,128)(2,1)S(1)}, bf16[64,768]{1,0:T(8,128)(2,1)S(1)}, u32[]{:S(2)}, u32[]{:S(2)}) collective-permute-start(bf16[64,768]{1,0:T(8,128)(2,1)S(1)} %add_convert_fusion), channel_id=1, source_target_pairs={{0,2},{1,3},{2,0},{3,1},{4,6},{5,7},{6,4},{7,5},{8,10},{9,11},{10,... | collective-permute-start | bytes 294920 | tf_op jit(solution)/shard_map/ppermute | solution.py:568
  76.7 0.9 collective-permute-done.12
  77.6 1.6 %collective-permute-done.11 = bf16[16,2048]{1,0:T(8,128)(2,1)S(1)} collective-permute-done((bf16[16,2048]{1,0:T(8,128)(2,1)S(1)}, bf16[16,2048]{1,0:T(8,128)(2,1)S(1)}, u32[]{:S(2)}, u32[]{:S(2)}) %collective-permute-start.11) | collective-permute-done | bytes 65568 | tf_op jit(solution)/shard_map/ppermute | solution.py:568
  79.3 0.8 collective-permute-done.14
  80.1 2.0 %collective-permute-start.17 = (bf16[64,2048]{1,0:T(8,128)(2,1)S(1)}, bf16[64,2048]{1,0:T(8,128)(2,1)S(1)}, u32[]{:S(2)}, u32[]{:S(2)}) collective-permute-start(bf16[64,2048]{1,0:T(8,128)(2,1)S(1)} %pad_maximum_fusion.1), channel_id=1, source_target_pairs={{0,6},{1,7},{2,4},{3,5},{4,2},{5,3},{6,0},{7,1},{8,14},{9,15},{10,... | collective-permute-start | bytes 786440 | tf_op jit(solution)/shard_map/ppermute | solution.py:568
  82.1 0.8 collective-permute-start.16
  82.9 0.8 collective-permute-start.15
  83.6 0.7 collective-permute-start.18
  84.4 5.3 %collective-permute-done.18 = bf16[64,768]{1,0:T(8,128)(2,1)S(1)} collective-permute-done((bf16[64,768]{1,0:T(8,128)(2,1)S(1)}, bf16[64,768]{1,0:T(8,128)(2,1)S(1)}, u32[]{:S(2)}, u32[]{:S(2)}) %collective-permute-start.18) | collective-permute-done | bytes 98336 | tf_op jit(solution)/shard_map/ppermute | solution.py:568
  89.8 1.2 %fusion = bf16[512,512]{1,0:T(8,128)(2,1)} fusion(bf16[512,512]{1,0:T(8,128)(2,1)S(1)} %copy-done.5, bf16[512,512]{1,0:T(8,128)(2,1)S(1)} %copy-done.3, bf16[512,512]{1,0:T(8,128)(2,1)S(1)} %copy-done.4), kind=kOutput, calls=%fused_computation.1 | convolution fusion | flops 269221888 | bytes 2097152 | tf_op jit(solution)/shard_map/dot_general | solution.py:27
  91.1 4.4 %collective-permute-done.19 = bf16[128,768]{1,0:T(8,128)(2,1)S(1)} collective-permute-done((bf16[128,768]{1,0:T(8,128)(2,1)S(1)}, bf16[128,768]{1,0:T(8,128)(2,1)S(1)}, u32[]{:S(2)}, u32[]{:S(2)}) %collective-permute-start.19) | collective-permute-done | bytes 196640 | tf_op jit(solution)/shard_map/ppermute | solution.py:568
  95.7 0.5 collective-permute-start.21
  96.2 2.8 %finish_own.1 = (f32[128,512]{1,0:T(8,128)}, f32[256,512]{1,0:T(8,128)}, f32[512,2048]{1,0:T(8,128)}, f32[512,512]{1,0:T(8,128)}) custom-call(s32[1]{0:T(128)} %bitcast.me_ref, bf16[256,128]{1,0:T(8,128)(2,1)S(1)} %get-tuple-element.102.chosen_ref, bf16[256,128]{1,0:T(8,128)(2,1)S(1)} %bitcast.11, ...), custom_call_target="tpu_custom_call" | custom-call | flops 100000000 | bytes 5000000 | tf_op jit(solution)/shard_map/finish_own/pallas_call | solution.py:501
  99.0 2.0 %finish_other.1 = (f32[256,512]{1,0:T(8,128)}, f32[512,2048]{1,0:T(8,128)}, f32[512,512]{1,0:T(8,128)}) custom-call(s32[1]{0:T(128)} %bitcast.me_ref, bf16[256,2048]{1,0:T(8,128)(2,1)S(1)} %collective-permute-done.20.early_ref, bf16[256,768]{1,0:T(8,128)(2,1)S(1)} %collective-permute-done.21.late_ref, ...), custom_call_target="tpu_custom_call", output_to_operand_aliasing={{0}: (3, {}), {1}: (4, {}), {2}: (5, {})} | custom-call | bytes 5000000 | tf_op jit(solution)/shard_map/finish_other/pallas_call | solution.py:511
  (44 shorter events, 1.6 us)
Async XLA Ops:
  2.0 14.4 %all-to-all-start = ((s32[32,1,2]{2,1,0:T(1,128)}), s32[32,1,2]{2,1,0:T(1,128)S(1)}, u32[]{:S(2)}, u32[]{:S(2)}) async-start(s32[32,1,2]{2,1,0:T(1,128)} %copy.18), calls=%async_computation | async-start | bytes 32768 | tf_op jit(solution)/shard_map/all_to_all | solution.py:564
  9.3 0.9 copy-start.2
  17.4 10.0 %all-to-all-start.1 = ((bf16[32,8,128]{2,1,0:T(8,128)(2,1)}), bf16[32,8,128]{2,1,0:T(8,128)(2,1)S(1)}, u32[]{:S(2)}, u32[]{:S(2)}) async-start(bf16[32,8,128]{2,1,0:T(8,128)(2,1)} %bitcast.3), calls=%async_computation.1 | async-start | bytes 131072 | tf_op jit(solution)/shard_map/all_to_all | solution.py:564
  27.4 0.6 copy-start.7
  42.1 3.6 %collective-permute-start = (bf16[256,2048]{1,0:T(8,128)(2,1)}, bf16[256,2048]{1,0:T(8,128)(2,1)S(1)}, u32[]{:S(2)}, u32[]{:S(2)}) collective-permute-start(bf16[256,2048]{1,0:T(8,128)(2,1)} %get-tuple-element.70), channel_id=1, source_target_pairs={{0,1},{1,0},{2,3},{3,2},{4,5},{5,4},{6,7},{7,6},{8,9},{9,8},{10,11... | collective-permute-start | bytes 3145736 | tf_op jit(solution)/shard_map/ppermute | solution.py:568
  42.2 3.3 %collective-permute-start.1 = (bf16[256,768]{1,0:T(8,128)(2,1)}, bf16[256,768]{1,0:T(8,128)(2,1)S(1)}, u32[]{:S(2)}, u32[]{:S(2)}) collective-permute-start(bf16[256,768]{1,0:T(8,128)(2,1)} %get-tuple-element.76), channel_id=1, source_target_pairs={{0,1},{1,0},{2,3},{3,2},{4,5},{5,4},{6,7},{7,6},{8,9},{9,8},{10,11... | collective-permute-start | bytes 1179656 | tf_op jit(solution)/shard_map/ppermute | solution.py:568
  42.6 1.2 %copy-start = (bf16[256,2048]{1,0:T(8,128)(2,1)S(1)}, bf16[256,2048]{1,0:T(8,128)(2,1)}, u32[]{:S(2)}) copy-start(bf16[256,2048]{1,0:T(8,128)(2,1)} %get-tuple-element.67.refs_0_) | copy-start | bytes 3145732
  43.9 1.0 copy-start.1
  44.9 44.9 %copy-start.3 = (bf16[512,512]{1,0:T(8,128)(2,1)S(1)}, bf16[512,512]{1,0:T(8,128)(2,1)}, u32[]{:S(2)}) copy-start(bf16[512,512]{1,0:T(8,128)(2,1)} %out_hbm.1) | copy-start | bytes 1572868
  44.9 44.9 %copy-start.4 = (bf16[512,512]{1,0:T(8,128)(2,1)S(1)}, bf16[512,512]{1,0:T(8,128)(2,1)}, u32[]{:S(2)}) copy-start(bf16[512,512]{1,0:T(8,128)(2,1)} %get-tuple-element.100) | copy-start | bytes 1572868
  44.9 45.0 %copy-start.5 = (bf16[512,512]{1,0:T(8,128)(2,1)S(1)}, bf16[512,512]{1,0:T(8,128)(2,1)}, u32[]{:S(2)}) copy-start(bf16[512,512]{1,0:T(8,128)(2,1)} %get-tuple-element.99) | copy-start | bytes 1572868
  45.9 7.0 %collective-permute-start.3 = (bf16[128,768]{1,0:T(8,128)(2,1)S(1)}, bf16[128,768]{1,0:T(8,128)(2,1)S(1)}, u32[]{:S(2)}, u32[]{:S(2)}) collective-permute-start(bf16[128,768]{1,0:T(8,128)(2,1)S(1)} %get-tuple-element.80), channel_id=1, source_target_pairs={{0,8},{1,9},{2,10},{3,11},{4,12},{5,13},{6,14},{7,15},{8,0},{9,1},... | collective-permute-start | bytes 589832 | tf_op jit(solution)/shard_map/ppermute | solution.py:568
  46.6 9.2 %collective-permute-start.2 = (bf16[64,2048]{1,0:T(8,128)(2,1)S(1)}, bf16[64,2048]{1,0:T(8,128)(2,1)S(1)}, u32[]{:S(2)}, u32[]{:S(2)}) collective-permute-start(bf16[64,2048]{1,0:T(8,128)(2,1)S(1)} %get-tuple-element.78), channel_id=1, source_target_pairs={{0,2},{1,3},{2,0},{3,1},{4,6},{5,7},{6,4},{7,5},{8,10},{9,11},{10,... | collective-permute-start | bytes 786440 | tf_op jit(solution)/shard_map/ppermute | solution.py:568
  47.0 13.4 %collective-permute-start.4 = (bf16[64,2048]{1,0:T(8,128)(2,1)S(1)}, bf16[64,2048]{1,0:T(8,128)(2,1)S(1)}, u32[]{:S(2)}, u32[]{:S(2)}) collective-permute-start(bf16[64,2048]{1,0:T(8,128)(2,1)S(1)} %get-tuple-element.83), channel_id=1, source_target_pairs={{0,4},{1,5},{2,6},{3,7},{4,0},{5,1},{6,2},{7,3},{8,12},{9,13},{10,... | collective-permute-start | bytes 786440 | tf_op jit(solution)/shard_map/ppermute | solution.py:568
  47.9 12.5 %collective-permute-start.5 = (bf16[64,2048]{1,0:T(8,128)(2,1)S(1)}, bf16[64,2048]{1,0:T(8,128)(2,1)S(1)}, u32[]{:S(2)}, u32[]{:S(2)}) collective-permute-start(bf16[64,2048]{1,0:T(8,128)(2,1)S(1)} %get-tuple-element.84), channel_id=1, source_target_pairs={{0,6},{1,7},{2,4},{3,5},{4,2},{5,3},{6,0},{7,1},{8,14},{9,15},{10,... | collective-permute-start | bytes 786440 | tf_op jit(solution)/shard_map/ppermute | solution.py:568
  52.9 2.9 %copy-start.6 = (bf16[128,768]{1,0:T(8,128)(2,1)}, bf16[128,768]{1,0:T(8,128)(2,1)S(1)}, u32[]{:S(2)}) copy-start(bf16[128,768]{1,0:T(8,128)(2,1)S(1)} %collective-permute-done.3) | copy-start | bytes 589828
  53.6 7.3 %collective-permute-start.6 = (bf16[64,768]{1,0:T(8,128)(2,1)}, bf16[64,768]{1,0:T(8,128)(2,1)}, u32[]{:S(2)}, u32[]{:S(2)}) collective-permute-start(bf16[64,768]{1,0:T(8,128)(2,1)} %add_convert_fusion.2), channel_id=1, source_target_pairs={{0,16},{1,17},{2,18},{3,19},{4,20},{5,21},{6,22},{7,23},{8,24},{9,... | collective-permute-start | bytes 294920 | tf_op jit(solution)/shard_map/ppermute | solution.py:568
  55.8 15.1 %all-to-all-start.2 = ((bf16[32,8,128]{2,1,0:T(8,128)(2,1)}), bf16[32,8,128]{2,1,0:T(8,128)(2,1)S(1)}, u32[]{:S(2)}, u32[]{:S(2)}) async-start(bf16[32,8,128]{2,1,0:T(8,128)(2,1)} %bitcast.7), calls=%async_computation.2 | async-start | bytes 131072 | tf_op jit(solution)/shard_map/all_to_all | solution.py:564
  61.1 5.4 %collective-permute-start.7 = (bf16[16,2048]{1,0:T(8,128)(2,1)S(1)}, bf16[16,2048]{1,0:T(8,128)(2,1)S(1)}, u32[]{:S(2)}, u32[]{:S(2)}) collective-permute-start(bf16[16,2048]{1,0:T(8,128)(2,1)S(1)} %get-tuple-element.115), channel_id=1, source_target_pairs={{0,8},{1,9},{2,10},{3,11},{4,12},{5,13},{6,14},{7,15},{8,0},{9,1},... | collective-permute-start | bytes 196616 | tf_op jit(solution)/shard_map/ppermute | solution.py:568
  62.0 6.3 %collective-permute-start.9 = (bf16[16,2048]{1,0:T(8,128)(2,1)S(1)}, bf16[16,2048]{1,0:T(8,128)(2,1)S(1)}, u32[]{:S(2)}, u32[]{:S(2)}) collective-permute-start(bf16[16,2048]{1,0:T(8,128)(2,1)S(1)} %get-tuple-element.116), channel_id=1, source_target_pairs={{0,24},{1,25},{2,26},{3,27},{4,28},{5,29},{6,30},{7,31},{8,16},{9,... | collective-permute-start | bytes 196616 | tf_op jit(solution)/shard_map/ppermute | solution.py:568
  63.8 7.0 %collective-permute-start.8 = (bf16[16,2048]{1,0:T(8,128)(2,1)S(1)}, bf16[16,2048]{1,0:T(8,128)(2,1)S(1)}, u32[]{:S(2)}, u32[]{:S(2)}) collective-permute-start(bf16[16,2048]{1,0:T(8,128)(2,1)S(1)} %get-tuple-element.117), channel_id=1, source_target_pairs={{0,16},{1,17},{2,18},{3,19},{4,20},{5,21},{6,22},{7,23},{8,24},{9,... | collective-permute-start | bytes 196616 | tf_op jit(solution)/shard_map/ppermute | solution.py:568
  65.6 9.8 %collective-permute-start.13 = (bf16[64,768]{1,0:T(8,128)(2,1)S(1)}, bf16[64,768]{1,0:T(8,128)(2,1)S(1)}, u32[]{:S(2)}, u32[]{:S(2)}) collective-permute-start(bf16[64,768]{1,0:T(8,128)(2,1)S(1)} %add_convert_fusion.1), channel_id=1, source_target_pairs={{0,4},{1,5},{2,6},{3,7},{4,0},{5,1},{6,2},{7,3},{8,12},{9,13},{10,... | collective-permute-start | bytes 294920 | tf_op jit(solution)/shard_map/ppermute | solution.py:568
  70.9 6.8 %collective-permute-start.12 = (bf16[16,2048]{1,0:T(8,128)(2,1)S(1)}, bf16[16,2048]{1,0:T(8,128)(2,1)S(1)}, u32[]{:S(2)}, u32[]{:S(2)}) collective-permute-start(bf16[16,2048]{1,0:T(8,128)(2,1)S(1)} %multiply_convert_fusion.1), channel_id=1, source_target_pairs={{0,24},{1,25},{2,26},{3,27},{4,28},{5,29},{6,30},{7,31},{8,16},{9,... | collective-permute-start | bytes 196616 | tf_op jit(solution)/shard_map/ppermute | solution.py:568
  73.1 6.1 %collective-permute-start.11 = (bf16[16,2048]{1,0:T(8,128)(2,1)S(1)}, bf16[16,2048]{1,0:T(8,128)(2,1)S(1)}, u32[]{:S(2)}, u32[]{:S(2)}) collective-permute-start(bf16[16,2048]{1,0:T(8,128)(2,1)S(1)} %multiply_convert_fusion.1), channel_id=1, source_target_pairs={{0,16},{1,17},{2,18},{3,19},{4,20},{5,21},{6,22},{7,23},{8,24},{9,... | collective-permute-start | bytes 196616 | tf_op jit(solution)/shard_map/ppermute | solution.py:568
  73.1 6.1 %collective-permute-start.10 = (bf16[16,2048]{1,0:T(8,128)(2,1)S(1)}, bf16[16,2048]{1,0:T(8,128)(2,1)S(1)}, u32[]{:S(2)}, u32[]{:S(2)}) collective-permute-start(bf16[16,2048]{1,0:T(8,128)(2,1)S(1)} %multiply_convert_fusion.1), channel_id=1, source_target_pairs={{0,8},{1,9},{2,10},{3,11},{4,12},{5,13},{6,14},{7,15},{8,0},{9,1},... | collective-permute-start | bytes 196616 | tf_op jit(solution)/shard_map/ppermute | solution.py:568
  75.4 4.7 %collective-permute-start.14 = (bf16[64,768]{1,0:T(8,128)(2,1)S(1)}, bf16[64,768]{1,0:T(8,128)(2,1)S(1)}, u32[]{:S(2)}, u32[]{:S(2)}) collective-permute-start(bf16[64,768]{1,0:T(8,128)(2,1)S(1)} %add_convert_fusion), channel_id=1, source_target_pairs={{0,2},{1,3},{2,0},{3,1},{4,6},{5,7},{6,4},{7,5},{8,10},{9,11},{10,... | collective-permute-start | bytes 294920 | tf_op jit(solution)/shard_map/ppermute | solution.py:568
  80.1 15.4 %collective-permute-start.17 = (bf16[64,2048]{1,0:T(8,128)(2,1)S(1)}, bf16[64,2048]{1,0:T(8,128)(2,1)S(1)}, u32[]{:S(2)}, u32[]{:S(2)}) collective-permute-start(bf16[64,2048]{1,0:T(8,128)(2,1)S(1)} %pad_maximum_fusion.1), channel_id=1, source_target_pairs={{0,6},{1,7},{2,4},{3,5},{4,2},{5,3},{6,0},{7,1},{8,14},{9,15},{10,... | collective-permute-start | bytes 786440 | tf_op jit(solution)/shard_map/ppermute | solution.py:568
  82.1 13.4 %collective-permute-start.16 = (bf16[64,2048]{1,0:T(8,128)(2,1)S(1)}, bf16[64,2048]{1,0:T(8,128)(2,1)S(1)}, u32[]{:S(2)}, u32[]{:S(2)}) collective-permute-start(bf16[64,2048]{1,0:T(8,128)(2,1)S(1)} %pad_maximum_fusion.1), channel_id=1, source_target_pairs={{0,4},{1,5},{2,6},{3,7},{4,0},{5,1},{6,2},{7,3},{8,12},{9,13},{10,... | collective-permute-start | bytes 786440 | tf_op jit(solution)/shard_map/ppermute | solution.py:568
  82.9 12.6 %collective-permute-start.15 = (bf16[64,2048]{1,0:T(8,128)(2,1)S(1)}, bf16[64,2048]{1,0:T(8,128)(2,1)S(1)}, u32[]{:S(2)}, u32[]{:S(2)}) collective-permute-start(bf16[64,2048]{1,0:T(8,128)(2,1)S(1)} %pad_maximum_fusion.1), channel_id=1, source_target_pairs={{0,2},{1,3},{2,0},{3,1},{4,6},{5,7},{6,4},{7,5},{8,10},{9,11},{10,... | collective-permute-start | bytes 786440 | tf_op jit(solution)/shard_map/ppermute | solution.py:568
  83.6 6.1 %collective-permute-start.18 = (bf16[64,768]{1,0:T(8,128)(2,1)S(1)}, bf16[64,768]{1,0:T(8,128)(2,1)S(1)}, u32[]{:S(2)}, u32[]{:S(2)}) collective-permute-start(bf16[64,768]{1,0:T(8,128)(2,1)S(1)} %multiply_convert_fusion), channel_id=1, source_target_pairs={{0,16},{1,17},{2,18},{3,19},{4,20},{5,21},{6,22},{7,23},{8,24},{9,... | collective-permute-start | bytes 294920 | tf_op jit(solution)/shard_map/ppermute | solution.py:568
  89.7 5.7 %collective-permute-start.19 = (bf16[128,768]{1,0:T(8,128)(2,1)S(1)}, bf16[128,768]{1,0:T(8,128)(2,1)S(1)}, u32[]{:S(2)}, u32[]{:S(2)}) collective-permute-start(bf16[128,768]{1,0:T(8,128)(2,1)S(1)} %pad_maximum_fusion.2), channel_id=1, source_target_pairs={{0,8},{1,9},{2,10},{3,11},{4,12},{5,13},{6,14},{7,15},{8,0},{9,1},... | collective-permute-start | bytes 589832 | tf_op jit(solution)/shard_map/ppermute | solution.py:568
  95.6 3.4 %collective-permute-start.20 = (bf16[256,2048]{1,0:T(8,128)(2,1)S(1)}, bf16[256,2048]{1,0:T(8,128)(2,1)S(1)}, u32[]{:S(2)}, u32[]{:S(2)}) collective-permute-start(bf16[256,2048]{1,0:T(8,128)(2,1)S(1)} %constant_dynamic-update-slice_fusion.early_ref), channel_id=1, source_target_pairs={{0,1},{1,0},{2,3},{3,2},{4,5},{5,4},{6,7},{7,6},{8,9},{9,8},{10,11... | collective-permute-start | bytes 3145736 | tf_op jit(solution)/shard_map/ppermute | solution.py:568
  95.7 3.4 %collective-permute-start.21 = (bf16[256,768]{1,0:T(8,128)(2,1)S(1)}, bf16[256,768]{1,0:T(8,128)(2,1)S(1)}, u32[]{:S(2)}, u32[]{:S(2)}) collective-permute-start(bf16[256,768]{1,0:T(8,128)(2,1)S(1)} %pad_maximum_fusion.late_ref), channel_id=1, source_target_pairs={{0,1},{1,0},{2,3},{3,2},{4,5},{5,4},{6,7},{7,6},{8,9},{9,8},{10,11... | collective-permute-start | bytes 1179656 | tf_op jit(solution)/shard_map/ppermute | solution.py:568

commit v5 on v3

--- a/solution.py
+++ b/solution.py
@@ -164,7 +164,7 @@
     me_ref, lengths_ref, slot_ref, leaf_ref, rows_ref, table_hbm, in_hbm, out_hbm, tangent_hbm,
     output_hbm, d_rows_ref, keep_hbm, send_hbm, keep_late_hbm, send_late_hbm,
     inputs, gated, d_pre, grads, output,
-    normed, turned, moved, hidden, slope, weights, weights_slope, mixed, d_mixed,
+    normed, turned, moved, turned_gated, moved_gated, hidden, slope, weights, weights_slope, mixed, d_mixed,
     d_score, d_gated, allowed, allowed_scale, keys_t, values_t, d_inputs, leaf_grad, table, w_in, w_out, tangent, sems, out_sems,
 ):
     count, width = inputs.shape
@@ -283,9 +283,9 @@
         grads[:, to] = mm(moved[...], d_pre[:, to]).astype(bf16)
     leave(grads.at[half_rows:, :SPLIT], send_hbm)
     leave(grads.at[:half_rows, :SPLIT], keep_hbm)
-    turned[...] = gated[...].T
-    permute_rows(late, turned, moved)
-    grads[:, 4 * width : 5 * width] = mm(moved[...], tangent[...]).astype(bf16)
+    turned_gated[...] = gated[...].T
+    permute_rows(late, turned_gated, moved_gated)
+    grads[:, 4 * width : 5 * width] = mm(moved_gated[...], tangent[...]).astype(bf16)
     output[...] = (mm(gated[...], w_out[...]) + inputs[...].astype(f32)).astype(bf16)
     leave(output, output_hbm)
     normed_change = mm_nt(d_pre[...], w_in[...])
@@ -334,6 +334,8 @@
             pltpu.VMEM((count, width), bf16),
             pltpu.VMEM((width, count), bf16),
             pltpu.VMEM((width, count), bf16),
+            pltpu.VMEM((width, count), bf16),
+            pltpu.VMEM((width, count), bf16),
             pltpu.VMEM((count, 4 * width), bf16),
             pltpu.VMEM((count, 4 * width), bf16),
             pltpu.VMEM((HEADS, count, count), bf16),

time: 100 us -> 100 us (level)
  no operation moved by 1% of the time
where the time goes in v5:
time: 100 us; the launch traced here: 99.6 us
  waiting for transfers between devices  38.7 us (39%)
  starting transfers between devices  33.5 us (34%)
  Pallas kernels  20.9 us (21%)
  local copies, waits for them, and re-layouts  5.2 us (5%)
  between operations  1.01 us (1%)
    ppermute x22, waiting for transfers between devices, swap(): lax.ppermute(block, ('dp', 'rep'), [(i, i ^ mask) for i in range(count)])  25.1 us
    ppermute x22, starting transfers between devices, swap(): lax.ppermute(block, ('dp', 'rep'), [(i, i ^ mask) for i in range(count)])  20.9 us
    pallas_call x1, Pallas kernels, run_layer(): pl.pallas_call(layer_kernel, name='layer', out_shape=(shape((count, width...  14.5 us
    all_to_all x3, waiting for transfers between devices, exchange(): lax.all_to_all(blocks, ('dp', 'rep'), split_axis=0, concat_axis=0, tiled=...  13.6 us
    all_to_all x3, starting transfers between devices, exchange(): lax.all_to_all(blocks, ('dp', 'rep'), split_axis=0, concat_axis=0, tiled=...  12.6 us
    unnamed x11, local copies, waits for them, and re-layouts  3.8 us
    pallas_call x1, Pallas kernels, run_finish(): pl.pallas_call(finish_own_kernel, name='finish_own', out_shape=shapes, in...  2.84 us
    pallas_call x1, Pallas kernels, run_finish(): pl.pallas_call(finish_other_kernel, name='finish_other', out_shape=shapes...  2.02 us
  transfers between devices with their start and end apart: 25, of which 15 were waited for; matrix products, arithmetic and copies ran while one was open for 0% of the time, Pallas kernels for 3%

profile of v5, /device:TPU:0, one launch (start us, length us, event | category | flops | bytes accessed | tf_op | source)
XLA Modules:
  0.0 99.6 jit_solution(1929228603401822354)
XLA Ops:
  0.6 1.4 %copy.18 = s32[32,1,2]{2,1,0:T(1,128)} copy(s32[32,1,2]{0,2,1:T(2,128)} %bitcast.12) | data formatting | bytes 512 | tf_op jit(solution)/shard_map/all_to_all | solution.py:502
  2.0 7.3 %all-to-all-start = ((s32[32,1,2]{2,1,0:T(1,128)}), s32[32,1,2]{2,1,0:T(1,128)S(1)}, u32[]{:S(2)}, u32[]{:S(2)}) async-start(s32[32,1,2]{2,1,0:T(1,128)} %copy.18), calls=%async_computation | async-start | bytes 32768 | tf_op jit(solution)/shard_map/all_to_all | solution.py:502
  9.3 0.9 copy-done.2
  10.2 6.2 %all-to-all-done = s32[32,1,2]{2,1,0:T(1,128)S(1)} async-done(((s32[32,1,2]{2,1,0:T(1,128)}), s32[32,1,2]{2,1,0:T(1,128)S(1)}, u32[]{:S(2)}, u32[]{:S(2)}) %all-to-all-start) | async-done | bytes 288 | tf_op jit(solution)/shard_map/all_to_all | solution.py:502
  16.4 1.0 %lookup.1 = (bf16[256,128]{1,0:T(8,128)(2,1)}, bf16[256,128]{1,0:T(8,128)(2,1)S(1)}) custom-call(s32[32,2]{1,0:T(8,128)S(1)} %bitcast.10, bf16[128,512]{1,0:T(8,128)(2,1)S(1)} %load.2.table_ref), custom_call_target="tpu_custom_call" | custom-call | tf_op jit(solution)/shard_map/lookup/pallas_call | solution.py:150
  17.4 2.6 %all-to-all-start.1 = ((bf16[32,8,128]{2,1,0:T(8,128)(2,1)}), bf16[32,8,128]{2,1,0:T(8,128)(2,1)S(1)}, u32[]{:S(2)}, u32[]{:S(2)}) async-start(bf16[32,8,128]{2,1,0:T(8,128)(2,1)} %bitcast.5), calls=%async_computation.1 | async-start | bytes 131072 | tf_op jit(solution)/shard_map/all_to_all | solution.py:502
  20.0 7.4 %all-to-all-done.1 = bf16[32,8,128]{2,1,0:T(8,128)(2,1)S(1)} async-done(((bf16[32,8,128]{2,1,0:T(8,128)(2,1)}), bf16[32,8,128]{2,1,0:T(8,128)(2,1)S(1)}, u32[]{:S(2)}, u32[]{:S(2)}) %all-to-all-start.1) | async-done | bytes 65568 | tf_op jit(solution)/shard_map/all_to_all | solution.py:502
  27.4 0.6 copy-done.3
  28.0 14.5 %layer.1 = (bf16[512,512]{1,0:T(8,128)(2,1)}, bf16[256,128]{1,0:T(8,128)(2,1)}, bf16[256,2048]{1,0:T(8,128)(2,1)}, bf16[256,2048]{1,0:T(8,128)(2,1)}, bf16[256,7...) custom-call(s32[1]{0:T(128)} %bitcast.me_ref, s32[1,4]{1,0:T(1,128)} %lengths_ref.1, s32[1,512]{1,0:T(1,128)} %bitcast.14, ...), custom_call_target="tpu_custom_call" | custom-call | flops 6000000000 | bytes 10000000 | tf_op jit(solution)/shard_map/layer/pallas_call | solution.py:315
  42.6 0.2 collective-permute-start
  42.7 0.4 collective-permute-start.1
  43.1 1.2 %copy-done = bf16[256,2048]{1,0:T(8,128)(2,1)S(1)} copy-done((bf16[256,2048]{1,0:T(8,128)(2,1)S(1)}, bf16[256,2048]{1,0:T(8,128)(2,1)}, u32[]{:S(2)}) %copy-start) | copy-done | bytes 1048600
  44.4 1.0 copy-done.1
  45.4 0.6 collective-permute-done.1.other_ref
  46.2 0.2 merge.2
  46.4 0.7 collective-permute-start.3
  47.1 0.4 collective-permute-start.2
  47.5 0.9 collective-permute-start.4
  48.4 2.2 %collective-permute-start.5 = (bf16[64,2048]{1,0:T(8,128)(2,1)S(1)}, bf16[64,2048]{1,0:T(8,128)(2,1)S(1)}, u32[]{:S(2)}, u32[]{:S(2)}) collective-permute-start(bf16[64,2048]{1,0:T(8,128)(2,1)S(1)} %get-tuple-element.70), channel_id=1, source_target_pairs={{0,6},{1,7},{2,4},{3,5},{4,2},{5,3},{6,0},{7,1},{8,14},{9,15},{10,... | collective-permute-start | bytes 786440 | tf_op jit(solution)/shard_map/ppermute | solution.py:506
  50.6 2.8 %collective-permute-done.3 = bf16[128,768]{1,0:T(8,128)(2,1)S(1)} collective-permute-done((bf16[128,768]{1,0:T(8,128)(2,1)S(1)}, bf16[128,768]{1,0:T(8,128)(2,1)S(1)}, u32[]{:S(2)}, u32[]{:S(2)}) %collective-permute-start.3) | collective-permute-done | bytes 196640 | tf_op jit(solution)/shard_map/ppermute | solution.py:506
  53.4 0.7 collective-permute-start.6
  54.2 2.1 %collective-permute-done.2 = bf16[64,2048]{1,0:T(8,128)(2,1)S(1)} collective-permute-done((bf16[64,2048]{1,0:T(8,128)(2,1)S(1)}, bf16[64,2048]{1,0:T(8,128)(2,1)S(1)}, u32[]{:S(2)}, u32[]{:S(2)}) %collective-permute-start.2) | collective-permute-done | bytes 262176 | tf_op jit(solution)/shard_map/ppermute | solution.py:506
  56.3 2.7 %all-to-all-start.2 = ((bf16[32,8,128]{2,1,0:T(8,128)(2,1)}), bf16[32,8,128]{2,1,0:T(8,128)(2,1)S(1)}, u32[]{:S(2)}, u32[]{:S(2)}) async-start(bf16[32,8,128]{2,1,0:T(8,128)(2,1)} %bitcast.7), calls=%async_computation.2 | async-start | bytes 131072 | tf_op jit(solution)/shard_map/all_to_all | solution.py:502
  59.1 1.9 %collective-permute-done.4 = bf16[64,2048]{1,0:T(8,128)(2,1)S(1)} collective-permute-done((bf16[64,2048]{1,0:T(8,128)(2,1)S(1)}, bf16[64,2048]{1,0:T(8,128)(2,1)S(1)}, u32[]{:S(2)}, u32[]{:S(2)}) %collective-permute-start.4) | collective-permute-done | bytes 262176 | tf_op jit(solution)/shard_map/ppermute | solution.py:506
  60.9 0.1 add_convert_fusion.5
  61.0 1.5 %collective-permute-start.7 = (bf16[16,2048]{1,0:T(8,128)(2,1)S(1)}, bf16[16,2048]{1,0:T(8,128)(2,1)S(1)}, u32[]{:S(2)}, u32[]{:S(2)}) collective-permute-start(bf16[16,2048]{1,0:T(8,128)(2,1)S(1)} %get-tuple-element.95), channel_id=1, source_target_pairs={{0,8},{1,9},{2,10},{3,11},{4,12},{5,13},{6,14},{7,15},{8,0},{9,1},... | collective-permute-start | bytes 196616 | tf_op jit(solution)/shard_map/ppermute | solution.py:506
  62.5 0.9 collective-permute-start.9
  63.4 1.2 %collective-permute-start.8 = (bf16[16,2048]{1,0:T(8,128)(2,1)S(1)}, bf16[16,2048]{1,0:T(8,128)(2,1)S(1)}, u32[]{:S(2)}, u32[]{:S(2)}) collective-permute-start(bf16[16,2048]{1,0:T(8,128)(2,1)S(1)} %get-tuple-element.97), channel_id=1, source_target_pairs={{0,16},{1,17},{2,18},{3,19},{4,20},{5,21},{6,22},{7,23},{8,24},{9,... | collective-permute-start | bytes 196616 | tf_op jit(solution)/shard_map/ppermute | solution.py:506
  64.6 1.4 %collective-permute-start.13 = (bf16[64,768]{1,0:T(8,128)(2,1)S(1)}, bf16[64,768]{1,0:T(8,128)(2,1)S(1)}, u32[]{:S(2)}, u32[]{:S(2)}) collective-permute-start(bf16[64,768]{1,0:T(8,128)(2,1)S(1)} %add_convert_fusion.1), channel_id=1, source_target_pairs={{0,4},{1,5},{2,6},{3,7},{4,0},{5,1},{6,2},{7,3},{8,12},{9,13},{10,... | collective-permute-start | bytes 294920 | tf_op jit(solution)/shard_map/ppermute | solution.py:506
  66.0 2.6 %collective-permute-done.9 = bf16[16,2048]{1,0:T(8,128)(2,1)S(1)} collective-permute-done((bf16[16,2048]{1,0:T(8,128)(2,1)S(1)}, bf16[16,2048]{1,0:T(8,128)(2,1)S(1)}, u32[]{:S(2)}, u32[]{:S(2)}) %collective-permute-start.9) | collective-permute-done | bytes 65568 | tf_op jit(solution)/shard_map/ppermute | solution.py:506
  68.6 2.2 %collective-permute-done.8 = bf16[16,2048]{1,0:T(8,128)(2,1)S(1)} collective-permute-done((bf16[16,2048]{1,0:T(8,128)(2,1)S(1)}, bf16[16,2048]{1,0:T(8,128)(2,1)S(1)}, u32[]{:S(2)}, u32[]{:S(2)}) %collective-permute-start.8) | collective-permute-done | bytes 65568 | tf_op jit(solution)/shard_map/ppermute | solution.py:506
  70.8 1.7 %collective-permute-start.12 = (bf16[16,2048]{1,0:T(8,128)(2,1)S(1)}, bf16[16,2048]{1,0:T(8,128)(2,1)S(1)}, u32[]{:S(2)}, u32[]{:S(2)}) collective-permute-start(bf16[16,2048]{1,0:T(8,128)(2,1)S(1)} %multiply_convert_fusion.1), channel_id=1, source_target_pairs={{0,24},{1,25},{2,26},{3,27},{4,28},{5,29},{6,30},{7,31},{8,16},{9,... | collective-permute-start | bytes 196616 | tf_op jit(solution)/shard_map/ppermute | solution.py:506
  72.5 2.7 %collective-permute-start.10 = (bf16[16,2048]{1,0:T(8,128)(2,1)S(1)}, bf16[16,2048]{1,0:T(8,128)(2,1)S(1)}, u32[]{:S(2)}, u32[]{:S(2)}) collective-permute-start(bf16[16,2048]{1,0:T(8,128)(2,1)S(1)} %multiply_convert_fusion.1), channel_id=1, source_target_pairs={{0,8},{1,9},{2,10},{3,11},{4,12},{5,13},{6,14},{7,15},{8,0},{9,1},... | collective-permute-start | bytes 196616 | tf_op jit(solution)/shard_map/ppermute | solution.py:506
  75.3 1.6 %collective-permute-start.14 = (bf16[64,768]{1,0:T(8,128)(2,1)S(1)}, bf16[64,768]{1,0:T(8,128)(2,1)S(1)}, u32[]{:S(2)}, u32[]{:S(2)}) collective-permute-start(bf16[64,768]{1,0:T(8,128)(2,1)S(1)} %add_convert_fusion), channel_id=1, source_target_pairs={{0,2},{1,3},{2,0},{3,1},{4,6},{5,7},{6,4},{7,5},{8,10},{9,11},{10,... | collective-permute-start | bytes 294920 | tf_op jit(solution)/shard_map/ppermute | solution.py:506
  76.9 0.5 collective-permute-done.12
  77.4 1.5 %collective-permute-done.11 = bf16[16,2048]{1,0:T(8,128)(2,1)S(1)} collective-permute-done((bf16[16,2048]{1,0:T(8,128)(2,1)S(1)}, bf16[16,2048]{1,0:T(8,128)(2,1)S(1)}, u32[]{:S(2)}, u32[]{:S(2)}) %collective-permute-start.11) | collective-permute-done | bytes 65568 | tf_op jit(solution)/shard_map/ppermute | solution.py:506
  79.0 1.0 collective-permute-done.14
  80.0 0.2 collective-permute-start.18
  80.3 2.5 %collective-permute-start.17 = (bf16[64,2048]{1,0:T(8,128)(2,1)S(1)}, bf16[64,2048]{1,0:T(8,128)(2,1)S(1)}, u32[]{:S(2)}, u32[]{:S(2)}) collective-permute-start(bf16[64,2048]{1,0:T(8,128)(2,1)S(1)} %pad_maximum_fusion.1), channel_id=1, source_target_pairs={{0,6},{1,7},{2,4},{3,5},{4,2},{5,3},{6,0},{7,1},{8,14},{9,15},{10,... | collective-permute-start | bytes 786440 | tf_op jit(solution)/shard_map/ppermute | solution.py:506
  82.7 0.5 collective-permute-start.16
  83.2 0.5 collective-permute-start.15
  83.8 2.3 %collective-permute-done.18 = bf16[64,768]{1,0:T(8,128)(2,1)S(1)} collective-permute-done((bf16[64,768]{1,0:T(8,128)(2,1)S(1)}, bf16[64,768]{1,0:T(8,128)(2,1)S(1)}, u32[]{:S(2)}, u32[]{:S(2)}) %collective-permute-start.18) | collective-permute-done | bytes 98336 | tf_op jit(solution)/shard_map/ppermute | solution.py:506
  86.2 5.6 %collective-permute-done.19 = bf16[128,768]{1,0:T(8,128)(2,1)S(1)} collective-permute-done((bf16[128,768]{1,0:T(8,128)(2,1)S(1)}, bf16[128,768]{1,0:T(8,128)(2,1)S(1)}, u32[]{:S(2)}, u32[]{:S(2)}) %collective-permute-start.19) | collective-permute-done | bytes 196640 | tf_op jit(solution)/shard_map/ppermute | solution.py:506
  91.9 1.8 %collective-permute-done.16 = bf16[64,2048]{1,0:T(8,128)(2,1)S(1)} collective-permute-done((bf16[64,2048]{1,0:T(8,128)(2,1)S(1)}, bf16[64,2048]{1,0:T(8,128)(2,1)S(1)}, u32[]{:S(2)}, u32[]{:S(2)}) %collective-permute-start.16) | collective-permute-done | bytes 262176 | tf_op jit(solution)/shard_map/ppermute | solution.py:506
  93.7 0.1 collective-permute-done.15
  94.0 0.5 collective-permute-start.21
  94.5 2.8 %finish_own.1 = (f32[128,512]{1,0:T(8,128)}, f32[256,512]{1,0:T(8,128)}, f32[512,2048]{1,0:T(8,128)}, f32[512,512]{1,0:T(8,128)}) custom-call(s32[1]{0:T(128)} %bitcast.me_ref, bf16[256,128]{1,0:T(8,128)(2,1)S(1)} %get-tuple-element.52.chosen_ref, bf16[256,128]{1,0:T(8,128)(2,1)S(1)} %bitcast.9, ...), custom_call_target="tpu_custom_call" | custom-call | flops 100000000 | bytes 5000000 | tf_op jit(solution)/shard_map/finish_own/pallas_call | solution.py:439
  97.4 2.0 %finish_other.1 = (f32[256,512]{1,0:T(8,128)}, f32[512,2048]{1,0:T(8,128)}, f32[512,512]{1,0:T(8,128)}) custom-call(s32[1]{0:T(128)} %bitcast.me_ref, bf16[256,2048]{1,0:T(8,128)(2,1)S(1)} %collective-permute-done.20.early_ref, bf16[256,768]{1,0:T(8,128)(2,1)S(1)} %collective-permute-done.21.late_ref, ...), custom_call_target="tpu_custom_call", output_to_operand_aliasing={{0}: (3, {}), {1}: (4, {}), {2}: (5, {})} | custom-call | bytes 5000000 | tf_op jit(solution)/shard_map/finish_other/pallas_call | solution.py:449
  (34 shorter events, 0.7 us)
Async XLA Ops:
  2.0 14.4 %all-to-all-start = ((s32[32,1,2]{2,1,0:T(1,128)}), s32[32,1,2]{2,1,0:T(1,128)S(1)}, u32[]{:S(2)}, u32[]{:S(2)}) async-start(s32[32,1,2]{2,1,0:T(1,128)} %copy.18), calls=%async_computation | async-start | bytes 32768 | tf_op jit(solution)/shard_map/all_to_all | solution.py:502
  9.3 0.9 copy-start.2
  17.4 10.0 %all-to-all-start.1 = ((bf16[32,8,128]{2,1,0:T(8,128)(2,1)}), bf16[32,8,128]{2,1,0:T(8,128)(2,1)S(1)}, u32[]{:S(2)}, u32[]{:S(2)}) async-start(bf16[32,8,128]{2,1,0:T(8,128)(2,1)} %bitcast.5), calls=%async_computation.1 | async-start | bytes 131072 | tf_op jit(solution)/shard_map/all_to_all | solution.py:502
  27.4 0.6 copy-start.3
  42.6 3.6 %collective-permute-start = (bf16[256,2048]{1,0:T(8,128)(2,1)}, bf16[256,2048]{1,0:T(8,128)(2,1)S(1)}, u32[]{:S(2)}, u32[]{:S(2)}) collective-permute-start(bf16[256,2048]{1,0:T(8,128)(2,1)} %get-tuple-element.56), channel_id=1, source_target_pairs={{0,1},{1,0},{2,3},{3,2},{4,5},{5,4},{6,7},{7,6},{8,9},{9,8},{10,11... | collective-permute-start | bytes 3145736 | tf_op jit(solution)/shard_map/ppermute | solution.py:506
  42.7 3.3 %collective-permute-start.1 = (bf16[256,768]{1,0:T(8,128)(2,1)}, bf16[256,768]{1,0:T(8,128)(2,1)S(1)}, u32[]{:S(2)}, u32[]{:S(2)}) collective-permute-start(bf16[256,768]{1,0:T(8,128)(2,1)} %get-tuple-element.62), channel_id=1, source_target_pairs={{0,1},{1,0},{2,3},{3,2},{4,5},{5,4},{6,7},{7,6},{8,9},{9,8},{10,11... | collective-permute-start | bytes 1179656 | tf_op jit(solution)/shard_map/ppermute | solution.py:506
  43.1 1.2 %copy-start = (bf16[256,2048]{1,0:T(8,128)(2,1)S(1)}, bf16[256,2048]{1,0:T(8,128)(2,1)}, u32[]{:S(2)}) copy-start(bf16[256,2048]{1,0:T(8,128)(2,1)} %get-tuple-element.53.refs_0_) | copy-start | bytes 3145732
  44.4 1.0 copy-start.1
  46.4 7.0 %collective-permute-start.3 = (bf16[128,768]{1,0:T(8,128)(2,1)S(1)}, bf16[128,768]{1,0:T(8,128)(2,1)S(1)}, u32[]{:S(2)}, u32[]{:S(2)}) collective-permute-start(bf16[128,768]{1,0:T(8,128)(2,1)S(1)} %get-tuple-element.66), channel_id=1, source_target_pairs={{0,8},{1,9},{2,10},{3,11},{4,12},{5,13},{6,14},{7,15},{8,0},{9,1},... | collective-permute-start | bytes 589832 | tf_op jit(solution)/shard_map/ppermute | solution.py:506
  47.1 9.2 %collective-permute-start.2 = (bf16[64,2048]{1,0:T(8,128)(2,1)S(1)}, bf16[64,2048]{1,0:T(8,128)(2,1)S(1)}, u32[]{:S(2)}, u32[]{:S(2)}) collective-permute-start(bf16[64,2048]{1,0:T(8,128)(2,1)S(1)} %get-tuple-element.64), channel_id=1, source_target_pairs={{0,2},{1,3},{2,0},{3,1},{4,6},{5,7},{6,4},{7,5},{8,10},{9,11},{10,... | collective-permute-start | bytes 786440 | tf_op jit(solution)/shard_map/ppermute | solution.py:506
  47.5 13.4 %collective-permute-start.4 = (bf16[64,2048]{1,0:T(8,128)(2,1)S(1)}, bf16[64,2048]{1,0:T(8,128)(2,1)S(1)}, u32[]{:S(2)}, u32[]{:S(2)}) collective-permute-start(bf16[64,2048]{1,0:T(8,128)(2,1)S(1)} %get-tuple-element.69), channel_id=1, source_target_pairs={{0,4},{1,5},{2,6},{3,7},{4,0},{5,1},{6,2},{7,3},{8,12},{9,13},{10,... | collective-permute-start | bytes 786440 | tf_op jit(solution)/shard_map/ppermute | solution.py:506
  48.4 12.5 %collective-permute-start.5 = (bf16[64,2048]{1,0:T(8,128)(2,1)S(1)}, bf16[64,2048]{1,0:T(8,128)(2,1)S(1)}, u32[]{:S(2)}, u32[]{:S(2)}) collective-permute-start(bf16[64,2048]{1,0:T(8,128)(2,1)S(1)} %get-tuple-element.70), channel_id=1, source_target_pairs={{0,6},{1,7},{2,4},{3,5},{4,2},{5,3},{6,0},{7,1},{8,14},{9,15},{10,... | collective-permute-start | bytes 786440 | tf_op jit(solution)/shard_map/ppermute | solution.py:506
  53.4 7.5 %collective-permute-start.6 = (bf16[64,768]{1,0:T(8,128)(2,1)S(1)}, bf16[64,768]{1,0:T(8,128)(2,1)S(1)}, u32[]{:S(2)}, u32[]{:S(2)}) collective-permute-start(bf16[64,768]{1,0:T(8,128)(2,1)S(1)} %add_convert_fusion.2), channel_id=1, source_target_pairs={{0,16},{1,17},{2,18},{3,19},{4,20},{5,21},{6,22},{7,23},{8,24},{9,... | collective-permute-start | bytes 294920 | tf_op jit(solution)/shard_map/ppermute | solution.py:506
  56.3 14.5 %all-to-all-start.2 = ((bf16[32,8,128]{2,1,0:T(8,128)(2,1)}), bf16[32,8,128]{2,1,0:T(8,128)(2,1)S(1)}, u32[]{:S(2)}, u32[]{:S(2)}) async-start(bf16[32,8,128]{2,1,0:T(8,128)(2,1)} %bitcast.7), calls=%async_computation.2 | async-start | bytes 131072 | tf_op jit(solution)/shard_map/all_to_all | solution.py:502
  61.0 5.0 %collective-permute-start.7 = (bf16[16,2048]{1,0:T(8,128)(2,1)S(1)}, bf16[16,2048]{1,0:T(8,128)(2,1)S(1)}, u32[]{:S(2)}, u32[]{:S(2)}) collective-permute-start(bf16[16,2048]{1,0:T(8,128)(2,1)S(1)} %get-tuple-element.95), channel_id=1, source_target_pairs={{0,8},{1,9},{2,10},{3,11},{4,12},{5,13},{6,14},{7,15},{8,0},{9,1},... | collective-permute-start | bytes 196616 | tf_op jit(solution)/shard_map/ppermute | solution.py:506
  62.5 6.1 %collective-permute-start.9 = (bf16[16,2048]{1,0:T(8,128)(2,1)S(1)}, bf16[16,2048]{1,0:T(8,128)(2,1)S(1)}, u32[]{:S(2)}, u32[]{:S(2)}) collective-permute-start(bf16[16,2048]{1,0:T(8,128)(2,1)S(1)} %get-tuple-element.96), channel_id=1, source_target_pairs={{0,24},{1,25},{2,26},{3,27},{4,28},{5,29},{6,30},{7,31},{8,16},{9,... | collective-permute-start | bytes 196616 | tf_op jit(solution)/shard_map/ppermute | solution.py:506
  63.4 7.4 %collective-permute-start.8 = (bf16[16,2048]{1,0:T(8,128)(2,1)S(1)}, bf16[16,2048]{1,0:T(8,128)(2,1)S(1)}, u32[]{:S(2)}, u32[]{:S(2)}) collective-permute-start(bf16[16,2048]{1,0:T(8,128)(2,1)S(1)} %get-tuple-element.97), channel_id=1, source_target_pairs={{0,16},{1,17},{2,18},{3,19},{4,20},{5,21},{6,22},{7,23},{8,24},{9,... | collective-permute-start | bytes 196616 | tf_op jit(solution)/shard_map/ppermute | solution.py:506
  64.6 10.7 %collective-permute-start.13 = (bf16[64,768]{1,0:T(8,128)(2,1)S(1)}, bf16[64,768]{1,0:T(8,128)(2,1)S(1)}, u32[]{:S(2)}, u32[]{:S(2)}) collective-permute-start(bf16[64,768]{1,0:T(8,128)(2,1)S(1)} %add_convert_fusion.1), channel_id=1, source_target_pairs={{0,4},{1,5},{2,6},{3,7},{4,0},{5,1},{6,2},{7,3},{8,12},{9,13},{10,... | collective-permute-start | bytes 294920 | tf_op jit(solution)/shard_map/ppermute | solution.py:506
  70.8 6.6 %collective-permute-start.12 = (bf16[16,2048]{1,0:T(8,128)(2,1)S(1)}, bf16[16,2048]{1,0:T(8,128)(2,1)S(1)}, u32[]{:S(2)}, u32[]{:S(2)}) collective-permute-start(bf16[16,2048]{1,0:T(8,128)(2,1)S(1)} %multiply_convert_fusion.1), channel_id=1, source_target_pairs={{0,24},{1,25},{2,26},{3,27},{4,28},{5,29},{6,30},{7,31},{8,16},{9,... | collective-permute-start | bytes 196616 | tf_op jit(solution)/shard_map/ppermute | solution.py:506
  72.5 6.5 %collective-permute-start.11 = (bf16[16,2048]{1,0:T(8,128)(2,1)S(1)}, bf16[16,2048]{1,0:T(8,128)(2,1)S(1)}, u32[]{:S(2)}, u32[]{:S(2)}) collective-permute-start(bf16[16,2048]{1,0:T(8,128)(2,1)S(1)} %multiply_convert_fusion.1), channel_id=1, source_target_pairs={{0,16},{1,17},{2,18},{3,19},{4,20},{5,21},{6,22},{7,23},{8,24},{9,... | collective-permute-start | bytes 196616 | tf_op jit(solution)/shard_map/ppermute | solution.py:506
  72.5 6.5 %collective-permute-start.10 = (bf16[16,2048]{1,0:T(8,128)(2,1)S(1)}, bf16[16,2048]{1,0:T(8,128)(2,1)S(1)}, u32[]{:S(2)}, u32[]{:S(2)}) collective-permute-start(bf16[16,2048]{1,0:T(8,128)(2,1)S(1)} %multiply_convert_fusion.1), channel_id=1, source_target_pairs={{0,8},{1,9},{2,10},{3,11},{4,12},{5,13},{6,14},{7,15},{8,0},{9,1},... | collective-permute-start | bytes 196616 | tf_op jit(solution)/shard_map/ppermute | solution.py:506
  75.3 4.7 %collective-permute-start.14 = (bf16[64,768]{1,0:T(8,128)(2,1)S(1)}, bf16[64,768]{1,0:T(8,128)(2,1)S(1)}, u32[]{:S(2)}, u32[]{:S(2)}) collective-permute-start(bf16[64,768]{1,0:T(8,128)(2,1)S(1)} %add_convert_fusion), channel_id=1, source_target_pairs={{0,2},{1,3},{2,0},{3,1},{4,6},{5,7},{6,4},{7,5},{8,10},{9,11},{10,... | collective-permute-start | bytes 294920 | tf_op jit(solution)/shard_map/ppermute | solution.py:506
  80.0 6.1 %collective-permute-start.18 = (bf16[64,768]{1,0:T(8,128)(2,1)S(1)}, bf16[64,768]{1,0:T(8,128)(2,1)S(1)}, u32[]{:S(2)}, u32[]{:S(2)}) collective-permute-start(bf16[64,768]{1,0:T(8,128)(2,1)S(1)} %multiply_convert_fusion), channel_id=1, source_target_pairs={{0,16},{1,17},{2,18},{3,19},{4,20},{5,21},{6,22},{7,23},{8,24},{9,... | collective-permute-start | bytes 294920 | tf_op jit(solution)/shard_map/ppermute | solution.py:506
  80.3 11.6 %collective-permute-start.17 = (bf16[64,2048]{1,0:T(8,128)(2,1)S(1)}, bf16[64,2048]{1,0:T(8,128)(2,1)S(1)}, u32[]{:S(2)}, u32[]{:S(2)}) collective-permute-start(bf16[64,2048]{1,0:T(8,128)(2,1)S(1)} %pad_maximum_fusion.1), channel_id=1, source_target_pairs={{0,6},{1,7},{2,4},{3,5},{4,2},{5,3},{6,0},{7,1},{8,14},{9,15},{10,... | collective-permute-start | bytes 786440 | tf_op jit(solution)/shard_map/ppermute | solution.py:506
  82.7 11.0 %collective-permute-start.16 = (bf16[64,2048]{1,0:T(8,128)(2,1)S(1)}, bf16[64,2048]{1,0:T(8,128)(2,1)S(1)}, u32[]{:S(2)}, u32[]{:S(2)}) collective-permute-start(bf16[64,2048]{1,0:T(8,128)(2,1)S(1)} %pad_maximum_fusion.1), channel_id=1, source_target_pairs={{0,4},{1,5},{2,6},{3,7},{4,0},{5,1},{6,2},{7,3},{8,12},{9,13},{10,... | collective-permute-start | bytes 786440 | tf_op jit(solution)/shard_map/ppermute | solution.py:506
  83.2 10.7 %collective-permute-start.15 = (bf16[64,2048]{1,0:T(8,128)(2,1)S(1)}, bf16[64,2048]{1,0:T(8,128)(2,1)S(1)}, u32[]{:S(2)}, u32[]{:S(2)}) collective-permute-start(bf16[64,2048]{1,0:T(8,128)(2,1)S(1)} %pad_maximum_fusion.1), channel_id=1, source_target_pairs={{0,2},{1,3},{2,0},{3,1},{4,6},{5,7},{6,4},{7,5},{8,10},{9,11},{10,... | collective-permute-start | bytes 786440 | tf_op jit(solution)/shard_map/ppermute | solution.py:506
  86.1 5.7 %collective-permute-start.19 = (bf16[128,768]{1,0:T(8,128)(2,1)S(1)}, bf16[128,768]{1,0:T(8,128)(2,1)S(1)}, u32[]{:S(2)}, u32[]{:S(2)}) collective-permute-start(bf16[128,768]{1,0:T(8,128)(2,1)S(1)} %pad_maximum_fusion.2), channel_id=1, source_target_pairs={{0,8},{1,9},{2,10},{3,11},{4,12},{5,13},{6,14},{7,15},{8,0},{9,1},... | collective-permute-start | bytes 589832 | tf_op jit(solution)/shard_map/ppermute | solution.py:506
  94.0 3.4 %collective-permute-start.20 = (bf16[256,2048]{1,0:T(8,128)(2,1)S(1)}, bf16[256,2048]{1,0:T(8,128)(2,1)S(1)}, u32[]{:S(2)}, u32[]{:S(2)}) collective-permute-start(bf16[256,2048]{1,0:T(8,128)(2,1)S(1)} %constant_dynamic-update-slice_fusion.early_ref), channel_id=1, source_target_pairs={{0,1},{1,0},{2,3},{3,2},{4,5},{5,4},{6,7},{7,6},{8,9},{9,8},{10,11... | collective-permute-start | bytes 3145736 | tf_op jit(solution)/shard_map/ppermute | solution.py:506
  94.0 3.4 %collective-permute-start.21 = (bf16[256,768]{1,0:T(8,128)(2,1)S(1)}, bf16[256,768]{1,0:T(8,128)(2,1)S(1)}, u32[]{:S(2)}, u32[]{:S(2)}) collective-permute-start(bf16[256,768]{1,0:T(8,128)(2,1)S(1)} %pad_maximum_fusion.late_ref), channel_id=1, source_target_pairs={{0,1},{1,0},{2,3},{3,2},{4,5},{5,4},{6,7},{7,6},{8,9},{9,8},{10,11... | collective-permute-start | bytes 1179656 | tf_op jit(solution)/shard_map/ppermute | solution.py:506

commit v6 on v5

--- a/solution.py
+++ b/solution.py
@@ -9,6 +9,7 @@
 HEADS = 4
 MAXLEN = 256
 BLOCK = 128
+SPAN = 256
 ROWS = 16
 epsilon = 1e-06
 f32 = jnp.float32
@@ -53,9 +54,9 @@
 
 
 def spans(count):
-    for start in range(0, count, BLOCK):
+    for start in range(0, count, SPAN):
         low = max(0, start - (MAXLEN - 1)) // BLOCK * BLOCK
-        yield start, low, start + BLOCK
+        yield start, low, start + SPAN
 
 
 def strips(start, stop):
@@ -194,9 +195,9 @@
         total = total + lengths_ref[0, place]
         ends.append(total)
     for start, low, high in spans(count):
-        at = slice(start, start + BLOCK)
-        row = start + lax.broadcasted_iota(jnp.int32, (BLOCK, high - low), 0)
-        column = low + lax.broadcasted_iota(jnp.int32, (BLOCK, high - low), 1)
+        at = slice(start, start + SPAN)
+        row = start + lax.broadcasted_iota(jnp.int32, (SPAN, high - low), 0)
+        column = low + lax.broadcasted_iota(jnp.int32, (SPAN, high - low), 1)
         first = jnp.zeros_like(row)
         for end in ends[:-1]:
             first = jnp.where(row >= end, end, first)
@@ -220,11 +221,11 @@
     keys_t[...] = hidden[:, 3 * width :].T
     values_t[...] = hidden[:, width : 2 * width].T
     for start, low, high in spans(count):
-        at = slice(start, start + BLOCK)
+        at = slice(start, start + SPAN)
         end = start // (2 * BLOCK) * 2 * BLOCK + 2 * BLOCK
         for out in (slice(0, low), slice(high, end)):
             if out.start < out.stop:
-                nothing = jnp.zeros((HEADS, BLOCK, out.stop - out.start), bf16)
+                nothing = jnp.zeros((HEADS, SPAN, out.stop - out.start), bf16)
                 weights[:, at, out] = nothing
                 d_score[:, at, out] = nothing
     for h in range(HEADS):
@@ -233,9 +234,9 @@
         query_at = slice(2 * width + h * head, 2 * width + (h + 1) * head)
         key_at = slice(3 * width + h * head, 3 * width + (h + 1) * head)
         for start, low, high in spans(count):
-            at = slice(start, start + BLOCK)
+            at = slice(start, start + SPAN)
             halves = mm(hidden[at, query_at], keys_t[own, low:high]) * half_scale
-            for strip in strips(0, BLOCK):
+            for strip in strips(0, SPAN):
                 to = slice(start + strip.start, start + strip.stop)
                 value, slope_at = silu(halves[strip, :])
                 weights[h, to, low:high] = value * allowed[to, low:high]
@@ -263,7 +264,7 @@
         query_at = slice(2 * width + h * head, 2 * width + (h + 1) * head)
         key_at = slice(3 * width + h * head, 3 * width + (h + 1) * head)
         for start, low, high in spans(count):
-            at = slice(start, start + BLOCK)
+            at = slice(start, start + SPAN)
             d_weights = mm(d_mixed[at, own], values_t[own, low:high]).astype(bf16)
             d_score[h, at, low:high] = d_weights * weights_slope[h, at, low:high]
         for start in range(0, count, 2 * BLOCK):

time: 100 us -> 100 us (level)
  transfers between devices with their start and end apart: 25 -> 25, of which waited for: 15 -> 14; matrix products, arithmetic and copies ran while one was open for 0% -> 0% of each run, Pallas kernels for 3% -> 3%
where the time goes in v6:
time: 100 us; the launch traced here: 99.7 us
  waiting for transfers between devices  38.7 us (39%)
  starting transfers between devices  33.6 us (34%)
  Pallas kernels  20.9 us (21%)
  local copies, waits for them, and re-layouts  5.2 us (5%)
  between operations  1.01 us (1%)
    ppermute x22, waiting for transfers between devices, swap(): lax.ppermute(block, ('dp', 'rep'), [(i, i ^ mask) for i in range(count)])  25.2 us
    ppermute x22, starting transfers between devices, swap(): lax.ppermute(block, ('dp', 'rep'), [(i, i ^ mask) for i in range(count)])  20.9 us
    pallas_call x1, Pallas kernels, run_layer(): pl.pallas_call(layer_kernel, name='layer', out_shape=(shape((count, width...  14.6 us
    all_to_all x3, waiting for transfers between devices, exchange(): lax.all_to_all(blocks, ('dp', 'rep'), split_axis=0, concat_axis=0, tiled=...  13.6 us
    all_to_all x3, starting transfers between devices, exchange(): lax.all_to_all(blocks, ('dp', 'rep'), split_axis=0, concat_axis=0, tiled=...  12.6 us
    unnamed x11, local copies, waits for them, and re-layouts  3.8 us
    pallas_call x1, Pallas kernels, run_finish(): pl.pallas_call(finish_own_kernel, name='finish_own', out_shape=shapes, in...  2.84 us
    pallas_call x1, Pallas kernels, run_finish(): pl.pallas_call(finish_other_kernel, name='finish_other', out_shape=shapes...  2.02 us
  transfers between devices with their start and end apart: 25, of which 14 were waited for; matrix products, arithmetic and copies ran while one was open for 0% of the time, Pallas kernels for 3%

profile of v6, /device:TPU:0, one launch (start us, length us, event | category | flops | bytes accessed | tf_op | source)
XLA Modules:
  0.0 99.7 jit_solution(8230294656628929198)
XLA Ops:
  0.6 1.4 %copy.18 = s32[32,1,2]{2,1,0:T(1,128)} copy(s32[32,1,2]{0,2,1:T(2,128)} %bitcast.12) | data formatting | bytes 512 | tf_op jit(solution)/shard_map/all_to_all | solution.py:503
  2.0 7.3 %all-to-all-start = ((s32[32,1,2]{2,1,0:T(1,128)}), s32[32,1,2]{2,1,0:T(1,128)S(1)}, u32[]{:S(2)}, u32[]{:S(2)}) async-start(s32[32,1,2]{2,1,0:T(1,128)} %copy.18), calls=%async_computation | async-start | bytes 32768 | tf_op jit(solution)/shard_map/all_to_all | solution.py:503
  9.3 0.9 copy-done.2
  10.2 6.2 %all-to-all-done = s32[32,1,2]{2,1,0:T(1,128)S(1)} async-done(((s32[32,1,2]{2,1,0:T(1,128)}), s32[32,1,2]{2,1,0:T(1,128)S(1)}, u32[]{:S(2)}, u32[]{:S(2)}) %all-to-all-start) | async-done | bytes 288 | tf_op jit(solution)/shard_map/all_to_all | solution.py:503
  16.4 1.0 %lookup.1 = (bf16[256,128]{1,0:T(8,128)(2,1)}, bf16[256,128]{1,0:T(8,128)(2,1)S(1)}) custom-call(s32[32,2]{1,0:T(8,128)S(1)} %bitcast.10, bf16[128,512]{1,0:T(8,128)(2,1)S(1)} %load.2.table_ref), custom_call_target="tpu_custom_call" | custom-call | tf_op jit(solution)/shard_map/lookup/pallas_call | solution.py:151
  17.4 2.6 %all-to-all-start.1 = ((bf16[32,8,128]{2,1,0:T(8,128)(2,1)}), bf16[32,8,128]{2,1,0:T(8,128)(2,1)S(1)}, u32[]{:S(2)}, u32[]{:S(2)}) async-start(bf16[32,8,128]{2,1,0:T(8,128)(2,1)} %bitcast.5), calls=%async_computation.1 | async-start | bytes 131072 | tf_op jit(solution)/shard_map/all_to_all | solution.py:503
  20.0 7.4 %all-to-all-done.1 = bf16[32,8,128]{2,1,0:T(8,128)(2,1)S(1)} async-done(((bf16[32,8,128]{2,1,0:T(8,128)(2,1)}), bf16[32,8,128]{2,1,0:T(8,128)(2,1)S(1)}, u32[]{:S(2)}, u32[]{:S(2)}) %all-to-all-start.1) | async-done | bytes 65568 | tf_op jit(solution)/shard_map/all_to_all | solution.py:503
  27.4 0.6 copy-done.3
  28.0 14.6 %layer.1 = (bf16[512,512]{1,0:T(8,128)(2,1)}, bf16[256,128]{1,0:T(8,128)(2,1)}, bf16[256,2048]{1,0:T(8,128)(2,1)}, bf16[256,2048]{1,0:T(8,128)(2,1)}, bf16[256,7...) custom-call(s32[1]{0:T(128)} %bitcast.me_ref, s32[1,4]{1,0:T(1,128)} %lengths_ref.1, s32[1,512]{1,0:T(1,128)} %bitcast.14, ...), custom_call_target="tpu_custom_call" | custom-call | flops 6000000000 | bytes 10000000 | tf_op jit(solution)/shard_map/layer/pallas_call | solution.py:316
  42.6 0.2 collective-permute-start
  42.8 0.4 collective-permute-start.1
  43.2 1.2 %copy-done = bf16[256,2048]{1,0:T(8,128)(2,1)S(1)} copy-done((bf16[256,2048]{1,0:T(8,128)(2,1)S(1)}, bf16[256,2048]{1,0:T(8,128)(2,1)}, u32[]{:S(2)}) %copy-start) | copy-done | bytes 1048600
  44.4 1.0 copy-done.1
  45.4 0.1 load.3
  45.5 0.6 collective-permute-done.1.other_ref
  46.2 0.2 merge.2
  46.4 0.7 collective-permute-start.3
  47.1 0.4 collective-permute-start.2
  47.5 0.9 collective-permute-start.4
  48.4 2.2 %collective-permute-start.5 = (bf16[64,2048]{1,0:T(8,128)(2,1)S(1)}, bf16[64,2048]{1,0:T(8,128)(2,1)S(1)}, u32[]{:S(2)}, u32[]{:S(2)}) collective-permute-start(bf16[64,2048]{1,0:T(8,128)(2,1)S(1)} %get-tuple-element.70), channel_id=1, source_target_pairs={{0,6},{1,7},{2,4},{3,5},{4,2},{5,3},{6,0},{7,1},{8,14},{9,15},{10,... | collective-permute-start | bytes 786440 | tf_op jit(solution)/shard_map/ppermute | solution.py:507
  50.6 2.8 %collective-permute-done.3 = bf16[128,768]{1,0:T(8,128)(2,1)S(1)} collective-permute-done((bf16[128,768]{1,0:T(8,128)(2,1)S(1)}, bf16[128,768]{1,0:T(8,128)(2,1)S(1)}, u32[]{:S(2)}, u32[]{:S(2)}) %collective-permute-start.3) | collective-permute-done | bytes 196640 | tf_op jit(solution)/shard_map/ppermute | solution.py:507
  53.5 0.7 collective-permute-start.6
  54.2 2.1 %collective-permute-done.2 = bf16[64,2048]{1,0:T(8,128)(2,1)S(1)} collective-permute-done((bf16[64,2048]{1,0:T(8,128)(2,1)S(1)}, bf16[64,2048]{1,0:T(8,128)(2,1)S(1)}, u32[]{:S(2)}, u32[]{:S(2)}) %collective-permute-start.2) | collective-permute-done | bytes 262176 | tf_op jit(solution)/shard_map/ppermute | solution.py:507
  56.3 2.7 %all-to-all-start.2 = ((bf16[32,8,128]{2,1,0:T(8,128)(2,1)}), bf16[32,8,128]{2,1,0:T(8,128)(2,1)S(1)}, u32[]{:S(2)}, u32[]{:S(2)}) async-start(bf16[32,8,128]{2,1,0:T(8,128)(2,1)} %bitcast.7), calls=%async_computation.2 | async-start | bytes 131072 | tf_op jit(solution)/shard_map/all_to_all | solution.py:503
  59.1 1.9 %collective-permute-done.4 = bf16[64,2048]{1,0:T(8,128)(2,1)S(1)} collective-permute-done((bf16[64,2048]{1,0:T(8,128)(2,1)S(1)}, bf16[64,2048]{1,0:T(8,128)(2,1)S(1)}, u32[]{:S(2)}, u32[]{:S(2)}) %collective-permute-start.4) | collective-permute-done | bytes 262176 | tf_op jit(solution)/shard_map/ppermute | solution.py:507
  60.9 0.1 add_convert_fusion.5
  61.1 1.5 %collective-permute-start.7 = (bf16[16,2048]{1,0:T(8,128)(2,1)S(1)}, bf16[16,2048]{1,0:T(8,128)(2,1)S(1)}, u32[]{:S(2)}, u32[]{:S(2)}) collective-permute-start(bf16[16,2048]{1,0:T(8,128)(2,1)S(1)} %get-tuple-element.95), channel_id=1, source_target_pairs={{0,8},{1,9},{2,10},{3,11},{4,12},{5,13},{6,14},{7,15},{8,0},{9,1},... | collective-permute-start | bytes 196616 | tf_op jit(solution)/shard_map/ppermute | solution.py:507
  62.5 0.9 collective-permute-start.9
  63.4 1.2 %collective-permute-start.8 = (bf16[16,2048]{1,0:T(8,128)(2,1)S(1)}, bf16[16,2048]{1,0:T(8,128)(2,1)S(1)}, u32[]{:S(2)}, u32[]{:S(2)}) collective-permute-start(bf16[16,2048]{1,0:T(8,128)(2,1)S(1)} %get-tuple-element.97), channel_id=1, source_target_pairs={{0,16},{1,17},{2,18},{3,19},{4,20},{5,21},{6,22},{7,23},{8,24},{9,... | collective-permute-start | bytes 196616 | tf_op jit(solution)/shard_map/ppermute | solution.py:507
  64.7 1.4 %collective-permute-start.13 = (bf16[64,768]{1,0:T(8,128)(2,1)S(1)}, bf16[64,768]{1,0:T(8,128)(2,1)S(1)}, u32[]{:S(2)}, u32[]{:S(2)}) collective-permute-start(bf16[64,768]{1,0:T(8,128)(2,1)S(1)} %add_convert_fusion.1), channel_id=1, source_target_pairs={{0,4},{1,5},{2,6},{3,7},{4,0},{5,1},{6,2},{7,3},{8,12},{9,13},{10,... | collective-permute-start | bytes 294920 | tf_op jit(solution)/shard_map/ppermute | solution.py:507
  66.0 2.6 %collective-permute-done.9 = bf16[16,2048]{1,0:T(8,128)(2,1)S(1)} collective-permute-done((bf16[16,2048]{1,0:T(8,128)(2,1)S(1)}, bf16[16,2048]{1,0:T(8,128)(2,1)S(1)}, u32[]{:S(2)}, u32[]{:S(2)}) %collective-permute-start.9) | collective-permute-done | bytes 65568 | tf_op jit(solution)/shard_map/ppermute | solution.py:507
  68.6 2.3 %collective-permute-done.8 = bf16[16,2048]{1,0:T(8,128)(2,1)S(1)} collective-permute-done((bf16[16,2048]{1,0:T(8,128)(2,1)S(1)}, bf16[16,2048]{1,0:T(8,128)(2,1)S(1)}, u32[]{:S(2)}, u32[]{:S(2)}) %collective-permute-start.8) | collective-permute-done | bytes 65568 | tf_op jit(solution)/shard_map/ppermute | solution.py:507
  70.9 1.8 %collective-permute-start.12 = (bf16[16,2048]{1,0:T(8,128)(2,1)S(1)}, bf16[16,2048]{1,0:T(8,128)(2,1)S(1)}, u32[]{:S(2)}, u32[]{:S(2)}) collective-permute-start(bf16[16,2048]{1,0:T(8,128)(2,1)S(1)} %multiply_convert_fusion.1), channel_id=1, source_target_pairs={{0,24},{1,25},{2,26},{3,27},{4,28},{5,29},{6,30},{7,31},{8,16},{9,... | collective-permute-start | bytes 196616 | tf_op jit(solution)/shard_map/ppermute | solution.py:507
  72.7 2.6 %collective-permute-start.10 = (bf16[16,2048]{1,0:T(8,128)(2,1)S(1)}, bf16[16,2048]{1,0:T(8,128)(2,1)S(1)}, u32[]{:S(2)}, u32[]{:S(2)}) collective-permute-start(bf16[16,2048]{1,0:T(8,128)(2,1)S(1)} %multiply_convert_fusion.1), channel_id=1, source_target_pairs={{0,8},{1,9},{2,10},{3,11},{4,12},{5,13},{6,14},{7,15},{8,0},{9,1},... | collective-permute-start | bytes 196616 | tf_op jit(solution)/shard_map/ppermute | solution.py:507
  75.4 1.6 %collective-permute-start.14 = (bf16[64,768]{1,0:T(8,128)(2,1)S(1)}, bf16[64,768]{1,0:T(8,128)(2,1)S(1)}, u32[]{:S(2)}, u32[]{:S(2)}) collective-permute-start(bf16[64,768]{1,0:T(8,128)(2,1)S(1)} %add_convert_fusion), channel_id=1, source_target_pairs={{0,2},{1,3},{2,0},{3,1},{4,6},{5,7},{6,4},{7,5},{8,10},{9,11},{10,... | collective-permute-start | bytes 294920 | tf_op jit(solution)/shard_map/ppermute | solution.py:507
  77.0 0.5 collective-permute-done.12
  77.5 1.7 %collective-permute-done.11 = bf16[16,2048]{1,0:T(8,128)(2,1)S(1)} collective-permute-done((bf16[16,2048]{1,0:T(8,128)(2,1)S(1)}, bf16[16,2048]{1,0:T(8,128)(2,1)S(1)}, u32[]{:S(2)}, u32[]{:S(2)}) %collective-permute-start.11) | collective-permute-done | bytes 65568 | tf_op jit(solution)/shard_map/ppermute | solution.py:507
  79.2 0.9 collective-permute-done.14
  80.1 0.3 collective-permute-start.18
  80.5 2.5 %collective-permute-start.17 = (bf16[64,2048]{1,0:T(8,128)(2,1)S(1)}, bf16[64,2048]{1,0:T(8,128)(2,1)S(1)}, u32[]{:S(2)}, u32[]{:S(2)}) collective-permute-start(bf16[64,2048]{1,0:T(8,128)(2,1)S(1)} %pad_maximum_fusion.1), channel_id=1, source_target_pairs={{0,6},{1,7},{2,4},{3,5},{4,2},{5,3},{6,0},{7,1},{8,14},{9,15},{10,... | collective-permute-start | bytes 786440 | tf_op jit(solution)/shard_map/ppermute | solution.py:507
  83.0 0.5 collective-permute-start.16
  83.4 0.6 collective-permute-start.15
  84.0 2.2 %collective-permute-done.18 = bf16[64,768]{1,0:T(8,128)(2,1)S(1)} collective-permute-done((bf16[64,768]{1,0:T(8,128)(2,1)S(1)}, bf16[64,768]{1,0:T(8,128)(2,1)S(1)}, u32[]{:S(2)}, u32[]{:S(2)}) %collective-permute-start.18) | collective-permute-done | bytes 98336 | tf_op jit(solution)/shard_map/ppermute | solution.py:507
  86.3 5.6 %collective-permute-done.19 = bf16[128,768]{1,0:T(8,128)(2,1)S(1)} collective-permute-done((bf16[128,768]{1,0:T(8,128)(2,1)S(1)}, bf16[128,768]{1,0:T(8,128)(2,1)S(1)}, u32[]{:S(2)}, u32[]{:S(2)}) %collective-permute-start.19) | collective-permute-done | bytes 196640 | tf_op jit(solution)/shard_map/ppermute | solution.py:507
  92.0 2.0 %collective-permute-done.16 = bf16[64,2048]{1,0:T(8,128)(2,1)S(1)} collective-permute-done((bf16[64,2048]{1,0:T(8,128)(2,1)S(1)}, bf16[64,2048]{1,0:T(8,128)(2,1)S(1)}, u32[]{:S(2)}, u32[]{:S(2)}) %collective-permute-start.16) | collective-permute-done | bytes 262176 | tf_op jit(solution)/shard_map/ppermute | solution.py:507
  94.2 0.5 collective-permute-start.21
  94.7 2.8 %finish_own.1 = (f32[128,512]{1,0:T(8,128)}, f32[256,512]{1,0:T(8,128)}, f32[512,2048]{1,0:T(8,128)}, f32[512,512]{1,0:T(8,128)}) custom-call(s32[1]{0:T(128)} %bitcast.me_ref, bf16[256,128]{1,0:T(8,128)(2,1)S(1)} %get-tuple-element.52.chosen_ref, bf16[256,128]{1,0:T(8,128)(2,1)S(1)} %bitcast.9, ...), custom_call_target="tpu_custom_call" | custom-call | flops 100000000 | bytes 5000000 | tf_op jit(solution)/shard_map/finish_own/pallas_call | solution.py:440
  97.6 2.0 %finish_other.1 = (f32[256,512]{1,0:T(8,128)}, f32[512,2048]{1,0:T(8,128)}, f32[512,512]{1,0:T(8,128)}) custom-call(s32[1]{0:T(128)} %bitcast.me_ref, bf16[256,2048]{1,0:T(8,128)(2,1)S(1)} %collective-permute-done.20.early_ref, bf16[256,768]{1,0:T(8,128)(2,1)S(1)} %collective-permute-done.21.late_ref, ...), custom_call_target="tpu_custom_call", output_to_operand_aliasing={{0}: (3, {}), {1}: (4, {}), {2}: (5, {})} | custom-call | bytes 5000000 | tf_op jit(solution)/shard_map/finish_other/pallas_call | solution.py:450
  (34 shorter events, 0.7 us)
Async XLA Ops:
  2.0 14.4 %all-to-all-start = ((s32[32,1,2]{2,1,0:T(1,128)}), s32[32,1,2]{2,1,0:T(1,128)S(1)}, u32[]{:S(2)}, u32[]{:S(2)}) async-start(s32[32,1,2]{2,1,0:T(1,128)} %copy.18), calls=%async_computation | async-start | bytes 32768 | tf_op jit(solution)/shard_map/all_to_all | solution.py:503
  9.3 0.9 copy-start.2
  17.4 10.0 %all-to-all-start.1 = ((bf16[32,8,128]{2,1,0:T(8,128)(2,1)}), bf16[32,8,128]{2,1,0:T(8,128)(2,1)S(1)}, u32[]{:S(2)}, u32[]{:S(2)}) async-start(bf16[32,8,128]{2,1,0:T(8,128)(2,1)} %bitcast.5), calls=%async_computation.1 | async-start | bytes 131072 | tf_op jit(solution)/shard_map/all_to_all | solution.py:503
  27.4 0.6 copy-start.3
  42.6 3.6 %collective-permute-start = (bf16[256,2048]{1,0:T(8,128)(2,1)}, bf16[256,2048]{1,0:T(8,128)(2,1)S(1)}, u32[]{:S(2)}, u32[]{:S(2)}) collective-permute-start(bf16[256,2048]{1,0:T(8,128)(2,1)} %get-tuple-element.56), channel_id=1, source_target_pairs={{0,1},{1,0},{2,3},{3,2},{4,5},{5,4},{6,7},{7,6},{8,9},{9,8},{10,11... | collective-permute-start | bytes 3145736 | tf_op jit(solution)/shard_map/ppermute | solution.py:507
  42.8 3.3 %collective-permute-start.1 = (bf16[256,768]{1,0:T(8,128)(2,1)}, bf16[256,768]{1,0:T(8,128)(2,1)S(1)}, u32[]{:S(2)}, u32[]{:S(2)}) collective-permute-start(bf16[256,768]{1,0:T(8,128)(2,1)} %get-tuple-element.62), channel_id=1, source_target_pairs={{0,1},{1,0},{2,3},{3,2},{4,5},{5,4},{6,7},{7,6},{8,9},{9,8},{10,11... | collective-permute-start | bytes 1179656 | tf_op jit(solution)/shard_map/ppermute | solution.py:507
  43.2 1.2 %copy-start = (bf16[256,2048]{1,0:T(8,128)(2,1)S(1)}, bf16[256,2048]{1,0:T(8,128)(2,1)}, u32[]{:S(2)}) copy-start(bf16[256,2048]{1,0:T(8,128)(2,1)} %get-tuple-element.53.refs_0_) | copy-start | bytes 3145732
  44.4 1.0 copy-start.1
  46.4 7.0 %collective-permute-start.3 = (bf16[128,768]{1,0:T(8,128)(2,1)S(1)}, bf16[128,768]{1,0:T(8,128)(2,1)S(1)}, u32[]{:S(2)}, u32[]{:S(2)}) collective-permute-start(bf16[128,768]{1,0:T(8,128)(2,1)S(1)} %get-tuple-element.66), channel_id=1, source_target_pairs={{0,8},{1,9},{2,10},{3,11},{4,12},{5,13},{6,14},{7,15},{8,0},{9,1},... | collective-permute-start | bytes 589832 | tf_op jit(solution)/shard_map/ppermute | solution.py:507
  47.1 9.2 %collective-permute-start.2 = (bf16[64,2048]{1,0:T(8,128)(2,1)S(1)}, bf16[64,2048]{1,0:T(8,128)(2,1)S(1)}, u32[]{:S(2)}, u32[]{:S(2)}) collective-permute-start(bf16[64,2048]{1,0:T(8,128)(2,1)S(1)} %get-tuple-element.64), channel_id=1, source_target_pairs={{0,2},{1,3},{2,0},{3,1},{4,6},{5,7},{6,4},{7,5},{8,10},{9,11},{10,... | collective-permute-start | bytes 786440 | tf_op jit(solution)/shard_map/ppermute | solution.py:507
  47.5 13.4 %collective-permute-start.4 = (bf16[64,2048]{1,0:T(8,128)(2,1)S(1)}, bf16[64,2048]{1,0:T(8,128)(2,1)S(1)}, u32[]{:S(2)}, u32[]{:S(2)}) collective-permute-start(bf16[64,2048]{1,0:T(8,128)(2,1)S(1)} %get-tuple-element.69), channel_id=1, source_target_pairs={{0,4},{1,5},{2,6},{3,7},{4,0},{5,1},{6,2},{7,3},{8,12},{9,13},{10,... | collective-permute-start | bytes 786440 | tf_op jit(solution)/shard_map/ppermute | solution.py:507
  48.4 12.5 %collective-permute-start.5 = (bf16[64,2048]{1,0:T(8,128)(2,1)S(1)}, bf16[64,2048]{1,0:T(8,128)(2,1)S(1)}, u32[]{:S(2)}, u32[]{:S(2)}) collective-permute-start(bf16[64,2048]{1,0:T(8,128)(2,1)S(1)} %get-tuple-element.70), channel_id=1, source_target_pairs={{0,6},{1,7},{2,4},{3,5},{4,2},{5,3},{6,0},{7,1},{8,14},{9,15},{10,... | collective-permute-start | bytes 786440 | tf_op jit(solution)/shard_map/ppermute | solution.py:507
  53.5 7.5 %collective-permute-start.6 = (bf16[64,768]{1,0:T(8,128)(2,1)S(1)}, bf16[64,768]{1,0:T(8,128)(2,1)S(1)}, u32[]{:S(2)}, u32[]{:S(2)}) collective-permute-start(bf16[64,768]{1,0:T(8,128)(2,1)S(1)} %add_convert_fusion.2), channel_id=1, source_target_pairs={{0,16},{1,17},{2,18},{3,19},{4,20},{5,21},{6,22},{7,23},{8,24},{9,... | collective-permute-start | bytes 294920 | tf_op jit(solution)/shard_map/ppermute | solution.py:507
  56.3 14.6 %all-to-all-start.2 = ((bf16[32,8,128]{2,1,0:T(8,128)(2,1)}), bf16[32,8,128]{2,1,0:T(8,128)(2,1)S(1)}, u32[]{:S(2)}, u32[]{:S(2)}) async-start(bf16[32,8,128]{2,1,0:T(8,128)(2,1)} %bitcast.7), calls=%async_computation.2 | async-start | bytes 131072 | tf_op jit(solution)/shard_map/all_to_all | solution.py:503
  61.1 5.0 %collective-permute-start.7 = (bf16[16,2048]{1,0:T(8,128)(2,1)S(1)}, bf16[16,2048]{1,0:T(8,128)(2,1)S(1)}, u32[]{:S(2)}, u32[]{:S(2)}) collective-permute-start(bf16[16,2048]{1,0:T(8,128)(2,1)S(1)} %get-tuple-element.95), channel_id=1, source_target_pairs={{0,8},{1,9},{2,10},{3,11},{4,12},{5,13},{6,14},{7,15},{8,0},{9,1},... | collective-permute-start | bytes 196616 | tf_op jit(solution)/shard_map/ppermute | solution.py:507
  62.5 6.1 %collective-permute-start.9 = (bf16[16,2048]{1,0:T(8,128)(2,1)S(1)}, bf16[16,2048]{1,0:T(8,128)(2,1)S(1)}, u32[]{:S(2)}, u32[]{:S(2)}) collective-permute-start(bf16[16,2048]{1,0:T(8,128)(2,1)S(1)} %get-tuple-element.96), channel_id=1, source_target_pairs={{0,24},{1,25},{2,26},{3,27},{4,28},{5,29},{6,30},{7,31},{8,16},{9,... | collective-permute-start | bytes 196616 | tf_op jit(solution)/shard_map/ppermute | solution.py:507
  63.4 7.5 %collective-permute-start.8 = (bf16[16,2048]{1,0:T(8,128)(2,1)S(1)}, bf16[16,2048]{1,0:T(8,128)(2,1)S(1)}, u32[]{:S(2)}, u32[]{:S(2)}) collective-permute-start(bf16[16,2048]{1,0:T(8,128)(2,1)S(1)} %get-tuple-element.97), channel_id=1, source_target_pairs={{0,16},{1,17},{2,18},{3,19},{4,20},{5,21},{6,22},{7,23},{8,24},{9,... | collective-permute-start | bytes 196616 | tf_op jit(solution)/shard_map/ppermute | solution.py:507
  64.7 10.7 %collective-permute-start.13 = (bf16[64,768]{1,0:T(8,128)(2,1)S(1)}, bf16[64,768]{1,0:T(8,128)(2,1)S(1)}, u32[]{:S(2)}, u32[]{:S(2)}) collective-permute-start(bf16[64,768]{1,0:T(8,128)(2,1)S(1)} %add_convert_fusion.1), channel_id=1, source_target_pairs={{0,4},{1,5},{2,6},{3,7},{4,0},{5,1},{6,2},{7,3},{8,12},{9,13},{10,... | collective-permute-start | bytes 294920 | tf_op jit(solution)/shard_map/ppermute | solution.py:507
  70.9 6.6 %collective-permute-start.12 = (bf16[16,2048]{1,0:T(8,128)(2,1)S(1)}, bf16[16,2048]{1,0:T(8,128)(2,1)S(1)}, u32[]{:S(2)}, u32[]{:S(2)}) collective-permute-start(bf16[16,2048]{1,0:T(8,128)(2,1)S(1)} %multiply_convert_fusion.1), channel_id=1, source_target_pairs={{0,24},{1,25},{2,26},{3,27},{4,28},{5,29},{6,30},{7,31},{8,16},{9,... | collective-permute-start | bytes 196616 | tf_op jit(solution)/shard_map/ppermute | solution.py:507
  72.7 6.4 %collective-permute-start.11 = (bf16[16,2048]{1,0:T(8,128)(2,1)S(1)}, bf16[16,2048]{1,0:T(8,128)(2,1)S(1)}, u32[]{:S(2)}, u32[]{:S(2)}) collective-permute-start(bf16[16,2048]{1,0:T(8,128)(2,1)S(1)} %multiply_convert_fusion.1), channel_id=1, source_target_pairs={{0,16},{1,17},{2,18},{3,19},{4,20},{5,21},{6,22},{7,23},{8,24},{9,... | collective-permute-start | bytes 196616 | tf_op jit(solution)/shard_map/ppermute | solution.py:507
  72.7 6.4 %collective-permute-start.10 = (bf16[16,2048]{1,0:T(8,128)(2,1)S(1)}, bf16[16,2048]{1,0:T(8,128)(2,1)S(1)}, u32[]{:S(2)}, u32[]{:S(2)}) collective-permute-start(bf16[16,2048]{1,0:T(8,128)(2,1)S(1)} %multiply_convert_fusion.1), channel_id=1, source_target_pairs={{0,8},{1,9},{2,10},{3,11},{4,12},{5,13},{6,14},{7,15},{8,0},{9,1},... | collective-permute-start | bytes 196616 | tf_op jit(solution)/shard_map/ppermute | solution.py:507
  75.4 4.7 %collective-permute-start.14 = (bf16[64,768]{1,0:T(8,128)(2,1)S(1)}, bf16[64,768]{1,0:T(8,128)(2,1)S(1)}, u32[]{:S(2)}, u32[]{:S(2)}) collective-permute-start(bf16[64,768]{1,0:T(8,128)(2,1)S(1)} %add_convert_fusion), channel_id=1, source_target_pairs={{0,2},{1,3},{2,0},{3,1},{4,6},{5,7},{6,4},{7,5},{8,10},{9,11},{10,... | collective-permute-start | bytes 294920 | tf_op jit(solution)/shard_map/ppermute | solution.py:507
  80.1 6.1 %collective-permute-start.18 = (bf16[64,768]{1,0:T(8,128)(2,1)S(1)}, bf16[64,768]{1,0:T(8,128)(2,1)S(1)}, u32[]{:S(2)}, u32[]{:S(2)}) collective-permute-start(bf16[64,768]{1,0:T(8,128)(2,1)S(1)} %multiply_convert_fusion), channel_id=1, source_target_pairs={{0,16},{1,17},{2,18},{3,19},{4,20},{5,21},{6,22},{7,23},{8,24},{9,... | collective-permute-start | bytes 294920 | tf_op jit(solution)/shard_map/ppermute | solution.py:507
  80.5 11.5 %collective-permute-start.17 = (bf16[64,2048]{1,0:T(8,128)(2,1)S(1)}, bf16[64,2048]{1,0:T(8,128)(2,1)S(1)}, u32[]{:S(2)}, u32[]{:S(2)}) collective-permute-start(bf16[64,2048]{1,0:T(8,128)(2,1)S(1)} %pad_maximum_fusion.1), channel_id=1, source_target_pairs={{0,6},{1,7},{2,4},{3,5},{4,2},{5,3},{6,0},{7,1},{8,14},{9,15},{10,... | collective-permute-start | bytes 786440 | tf_op jit(solution)/shard_map/ppermute | solution.py:507
  83.0 11.0 %collective-permute-start.16 = (bf16[64,2048]{1,0:T(8,128)(2,1)S(1)}, bf16[64,2048]{1,0:T(8,128)(2,1)S(1)}, u32[]{:S(2)}, u32[]{:S(2)}) collective-permute-start(bf16[64,2048]{1,0:T(8,128)(2,1)S(1)} %pad_maximum_fusion.1), channel_id=1, source_target_pairs={{0,4},{1,5},{2,6},{3,7},{4,0},{5,1},{6,2},{7,3},{8,12},{9,13},{10,... | collective-permute-start | bytes 786440 | tf_op jit(solution)/shard_map/ppermute | solution.py:507
  83.4 10.6 %collective-permute-start.15 = (bf16[64,2048]{1,0:T(8,128)(2,1)S(1)}, bf16[64,2048]{1,0:T(8,128)(2,1)S(1)}, u32[]{:S(2)}, u32[]{:S(2)}) collective-permute-start(bf16[64,2048]{1,0:T(8,128)(2,1)S(1)} %pad_maximum_fusion.1), channel_id=1, source_target_pairs={{0,2},{1,3},{2,0},{3,1},{4,6},{5,7},{6,4},{7,5},{8,10},{9,11},{10,... | collective-permute-start | bytes 786440 | tf_op jit(solution)/shard_map/ppermute | solution.py:507
  86.2 5.7 %collective-permute-start.19 = (bf16[128,768]{1,0:T(8,128)(2,1)S(1)}, bf16[128,768]{1,0:T(8,128)(2,1)S(1)}, u32[]{:S(2)}, u32[]{:S(2)}) collective-permute-start(bf16[128,768]{1,0:T(8,128)(2,1)S(1)} %pad_maximum_fusion.2), channel_id=1, source_target_pairs={{0,8},{1,9},{2,10},{3,11},{4,12},{5,13},{6,14},{7,15},{8,0},{9,1},... | collective-permute-start | bytes 589832 | tf_op jit(solution)/shard_map/ppermute | solution.py:507
  94.1 3.4 %collective-permute-start.20 = (bf16[256,2048]{1,0:T(8,128)(2,1)S(1)}, bf16[256,2048]{1,0:T(8,128)(2,1)S(1)}, u32[]{:S(2)}, u32[]{:S(2)}) collective-permute-start(bf16[256,2048]{1,0:T(8,128)(2,1)S(1)} %constant_dynamic-update-slice_fusion.early_ref), channel_id=1, source_target_pairs={{0,1},{1,0},{2,3},{3,2},{4,5},{5,4},{6,7},{7,6},{8,9},{9,8},{10,11... | collective-permute-start | bytes 3145736 | tf_op jit(solution)/shard_map/ppermute | solution.py:507
  94.2 3.3 %collective-permute-start.21 = (bf16[256,768]{1,0:T(8,128)(2,1)S(1)}, bf16[256,768]{1,0:T(8,128)(2,1)S(1)}, u32[]{:S(2)}, u32[]{:S(2)}) collective-permute-start(bf16[256,768]{1,0:T(8,128)(2,1)S(1)} %pad_maximum_fusion.late_ref), channel_id=1, source_target_pairs={{0,1},{1,0},{2,3},{3,2},{4,5},{5,4},{6,7},{7,6},{8,9},{9,8},{10,11... | collective-permute-start | bytes 1179656 | tf_op jit(solution)/shard_map/ppermute | solution.py:507

commit v7 on v5

--- a/solution.py
+++ b/solution.py
@@ -121,7 +121,7 @@
     return jnp.concatenate(pieces, axis=1).astype(bf16)
 
 
-def lookup_kernel(asked_ref, table_ref, rows_ref, chosen_ref):
+def lookup_kernel(asked_ref, table_ref, rows_ref, chosen_ref, spread):
     count, each = asked_ref.shape
     owned, width = table_ref.shape
     parts = width // BLOCK
@@ -136,11 +136,13 @@
         wanted.append(zero_one(spot == asked_ref[:, k : k + 1]))
     chosen = mm(jnp.concatenate(here, axis=1), jnp.concatenate(wanted, axis=0))
     chosen_ref[...] = chosen.astype(bf16)
-    part_of = lax.broadcasted_iota(jnp.int32, (many, owned), 0) & (parts - 1)
-    mine = [jnp.where(part_of == part, chosen, 0.0).astype(bf16) for part in range(parts)]
-    blocks = [table_ref[:, part * BLOCK : (part + 1) * BLOCK] for part in range(parts)]
-    total = mm(jnp.concatenate(mine, axis=1), jnp.concatenate(blocks, axis=0))
-    rows_ref[...] = total.astype(bf16)
+    for k in range(each):
+        rows = mm(wanted[k], table_ref[...])
+        for part in range(parts):
+            spread[pl.ds(k * parts + part, count, stride=each * parts), :] = rows[
+                :, part * BLOCK : (part + 1) * BLOCK
+            ]
+    rows_ref[...] = spread[...].astype(bf16)
 
 
 def run_lookup(asked, table):
@@ -156,6 +158,7 @@
         ),
         in_specs=[vmem, vmem],
         out_specs=(vmem,) * 2,
+        scratch_shapes=[pltpu.VMEM((many, BLOCK), f32)],
         compiler_params=pltpu.CompilerParams(vmem_limit_bytes=16 * 2**20),
     )(asked, table)
 

time: 100 us -> 99.8 us (level)
  no operation moved by 1% of the time
where the time goes in v7:
time: 99.8 us; the launch traced here: 99.4 us
  waiting for transfers between devices  38.7 us (39%)
  starting transfers between devices  33.5 us (34%)
  Pallas kernels  20.7 us (21%)
  local copies, waits for them, and re-layouts  5.2 us (5%)
  between operations  1.01 us (1%)
    ppermute x22, waiting for transfers between devices, swap(): lax.ppermute(block, ('dp', 'rep'), [(i, i ^ mask) for i in range(count)])  25.1 us
    ppermute x22, starting transfers between devices, swap(): lax.ppermute(block, ('dp', 'rep'), [(i, i ^ mask) for i in range(count)])  20.8 us
    pallas_call x1, Pallas kernels, run_layer(): pl.pallas_call(layer_kernel, name='layer', out_shape=(shape((count, width...  14.5 us
    all_to_all x3, waiting for transfers between devices, exchange(): lax.all_to_all(blocks, ('dp', 'rep'), split_axis=0, concat_axis=0, tiled=...  13.6 us
    all_to_all x3, starting transfers between devices, exchange(): lax.all_to_all(blocks, ('dp', 'rep'), split_axis=0, concat_axis=0, tiled=...  12.6 us
    unnamed x11, local copies, waits for them, and re-layouts  3.8 us
    pallas_call x1, Pallas kernels, run_finish(): pl.pallas_call(finish_own_kernel, name='finish_own', out_shape=shapes, in...  2.84 us
    pallas_call x1, Pallas kernels, run_finish(): pl.pallas_call(finish_other_kernel, name='finish_other', out_shape=shapes...  2.02 us
  transfers between devices with their start and end apart: 25, of which 15 were waited for; matrix products, arithmetic and copies ran while one was open for 0% of the time, Pallas kernels for 3%

profile of v7, /device:TPU:0, one launch (start us, length us, event | category | flops | bytes accessed | tf_op | source)
XLA Modules:
  0.0 99.4 jit_solution(16111442748922450345)
XLA Ops:
  0.6 1.4 %copy.18 = s32[32,1,2]{2,1,0:T(1,128)} copy(s32[32,1,2]{0,2,1:T(2,128)} %bitcast.12) | data formatting | bytes 512 | tf_op jit(solution)/shard_map/all_to_all | solution.py:505
  2.0 7.3 %all-to-all-start = ((s32[32,1,2]{2,1,0:T(1,128)}), s32[32,1,2]{2,1,0:T(1,128)S(1)}, u32[]{:S(2)}, u32[]{:S(2)}) async-start(s32[32,1,2]{2,1,0:T(1,128)} %copy.18), calls=%async_computation | async-start | bytes 32768 | tf_op jit(solution)/shard_map/all_to_all | solution.py:505
  9.3 0.9 copy-done.2
  10.2 6.2 %all-to-all-done = s32[32,1,2]{2,1,0:T(1,128)S(1)} async-done(((s32[32,1,2]{2,1,0:T(1,128)}), s32[32,1,2]{2,1,0:T(1,128)S(1)}, u32[]{:S(2)}, u32[]{:S(2)}) %all-to-all-start) | async-done | bytes 288 | tf_op jit(solution)/shard_map/all_to_all | solution.py:505
  16.4 0.9 lookup.1
  17.3 2.6 %all-to-all-start.1 = ((bf16[32,8,128]{2,1,0:T(8,128)(2,1)}), bf16[32,8,128]{2,1,0:T(8,128)(2,1)S(1)}, u32[]{:S(2)}, u32[]{:S(2)}) async-start(bf16[32,8,128]{2,1,0:T(8,128)(2,1)} %bitcast.5), calls=%async_computation.1 | async-start | bytes 131072 | tf_op jit(solution)/shard_map/all_to_all | solution.py:505
  19.8 7.4 %all-to-all-done.1 = bf16[32,8,128]{2,1,0:T(8,128)(2,1)S(1)} async-done(((bf16[32,8,128]{2,1,0:T(8,128)(2,1)}), bf16[32,8,128]{2,1,0:T(8,128)(2,1)S(1)}, u32[]{:S(2)}, u32[]{:S(2)}) %all-to-all-start.1) | async-done | bytes 65568 | tf_op jit(solution)/shard_map/all_to_all | solution.py:505
  27.2 0.6 copy-done.3
  27.9 14.5 %layer.1 = (bf16[512,512]{1,0:T(8,128)(2,1)}, bf16[256,128]{1,0:T(8,128)(2,1)}, bf16[256,2048]{1,0:T(8,128)(2,1)}, bf16[256,2048]{1,0:T(8,128)(2,1)}, bf16[256,7...) custom-call(s32[1]{0:T(128)} %bitcast.me_ref, s32[1,4]{1,0:T(1,128)} %lengths_ref.1, s32[1,512]{1,0:T(1,128)} %bitcast.14, ...), custom_call_target="tpu_custom_call" | custom-call | flops 6000000000 | bytes 10000000 | tf_op jit(solution)/shard_map/layer/pallas_call | solution.py:318
  42.4 0.2 collective-permute-start
  42.6 0.4 collective-permute-start.1
  43.0 1.2 %copy-done = bf16[256,2048]{1,0:T(8,128)(2,1)S(1)} copy-done((bf16[256,2048]{1,0:T(8,128)(2,1)S(1)}, bf16[256,2048]{1,0:T(8,128)(2,1)}, u32[]{:S(2)}) %copy-start) | copy-done | bytes 1048600
  44.2 1.0 copy-done.1
  45.3 0.6 collective-permute-done.1.other_ref
  46.0 0.2 merge.2
  46.3 0.7 collective-permute-start.3
  46.9 0.4 collective-permute-start.2
  47.4 0.9 collective-permute-start.4
  48.2 2.2 %collective-permute-start.5 = (bf16[64,2048]{1,0:T(8,128)(2,1)S(1)}, bf16[64,2048]{1,0:T(8,128)(2,1)S(1)}, u32[]{:S(2)}, u32[]{:S(2)}) collective-permute-start(bf16[64,2048]{1,0:T(8,128)(2,1)S(1)} %get-tuple-element.70), channel_id=1, source_target_pairs={{0,6},{1,7},{2,4},{3,5},{4,2},{5,3},{6,0},{7,1},{8,14},{9,15},{10,... | collective-permute-start | bytes 786440 | tf_op jit(solution)/shard_map/ppermute | solution.py:509
  50.4 2.8 %collective-permute-done.3 = bf16[128,768]{1,0:T(8,128)(2,1)S(1)} collective-permute-done((bf16[128,768]{1,0:T(8,128)(2,1)S(1)}, bf16[128,768]{1,0:T(8,128)(2,1)S(1)}, u32[]{:S(2)}, u32[]{:S(2)}) %collective-permute-start.3) | collective-permute-done | bytes 196640 | tf_op jit(solution)/shard_map/ppermute | solution.py:509
  53.3 0.7 collective-permute-start.6
  54.0 2.1 %collective-permute-done.2 = bf16[64,2048]{1,0:T(8,128)(2,1)S(1)} collective-permute-done((bf16[64,2048]{1,0:T(8,128)(2,1)S(1)}, bf16[64,2048]{1,0:T(8,128)(2,1)S(1)}, u32[]{:S(2)}, u32[]{:S(2)}) %collective-permute-start.2) | collective-permute-done | bytes 262176 | tf_op jit(solution)/shard_map/ppermute | solution.py:509
  56.1 2.7 %all-to-all-start.2 = ((bf16[32,8,128]{2,1,0:T(8,128)(2,1)}), bf16[32,8,128]{2,1,0:T(8,128)(2,1)S(1)}, u32[]{:S(2)}, u32[]{:S(2)}) async-start(bf16[32,8,128]{2,1,0:T(8,128)(2,1)} %bitcast.7), calls=%async_computation.2 | async-start | bytes 131072 | tf_op jit(solution)/shard_map/all_to_all | solution.py:505
  58.9 1.9 %collective-permute-done.4 = bf16[64,2048]{1,0:T(8,128)(2,1)S(1)} collective-permute-done((bf16[64,2048]{1,0:T(8,128)(2,1)S(1)}, bf16[64,2048]{1,0:T(8,128)(2,1)S(1)}, u32[]{:S(2)}, u32[]{:S(2)}) %collective-permute-start.4) | collective-permute-done | bytes 262176 | tf_op jit(solution)/shard_map/ppermute | solution.py:509
  60.8 0.1 add_convert_fusion.5
  60.9 1.5 %collective-permute-start.7 = (bf16[16,2048]{1,0:T(8,128)(2,1)S(1)}, bf16[16,2048]{1,0:T(8,128)(2,1)S(1)}, u32[]{:S(2)}, u32[]{:S(2)}) collective-permute-start(bf16[16,2048]{1,0:T(8,128)(2,1)S(1)} %get-tuple-element.95), channel_id=1, source_target_pairs={{0,8},{1,9},{2,10},{3,11},{4,12},{5,13},{6,14},{7,15},{8,0},{9,1},... | collective-permute-start | bytes 196616 | tf_op jit(solution)/shard_map/ppermute | solution.py:509
  62.4 0.9 collective-permute-start.9
  63.2 1.2 %collective-permute-start.8 = (bf16[16,2048]{1,0:T(8,128)(2,1)S(1)}, bf16[16,2048]{1,0:T(8,128)(2,1)S(1)}, u32[]{:S(2)}, u32[]{:S(2)}) collective-permute-start(bf16[16,2048]{1,0:T(8,128)(2,1)S(1)} %get-tuple-element.97), channel_id=1, source_target_pairs={{0,16},{1,17},{2,18},{3,19},{4,20},{5,21},{6,22},{7,23},{8,24},{9,... | collective-permute-start | bytes 196616 | tf_op jit(solution)/shard_map/ppermute | solution.py:509
  64.5 1.4 %collective-permute-start.13 = (bf16[64,768]{1,0:T(8,128)(2,1)S(1)}, bf16[64,768]{1,0:T(8,128)(2,1)S(1)}, u32[]{:S(2)}, u32[]{:S(2)}) collective-permute-start(bf16[64,768]{1,0:T(8,128)(2,1)S(1)} %add_convert_fusion.1), channel_id=1, source_target_pairs={{0,4},{1,5},{2,6},{3,7},{4,0},{5,1},{6,2},{7,3},{8,12},{9,13},{10,... | collective-permute-start | bytes 294920 | tf_op jit(solution)/shard_map/ppermute | solution.py:509
  65.9 2.6 %collective-permute-done.9 = bf16[16,2048]{1,0:T(8,128)(2,1)S(1)} collective-permute-done((bf16[16,2048]{1,0:T(8,128)(2,1)S(1)}, bf16[16,2048]{1,0:T(8,128)(2,1)S(1)}, u32[]{:S(2)}, u32[]{:S(2)}) %collective-permute-start.9) | collective-permute-done | bytes 65568 | tf_op jit(solution)/shard_map/ppermute | solution.py:509
  68.4 2.2 %collective-permute-done.8 = bf16[16,2048]{1,0:T(8,128)(2,1)S(1)} collective-permute-done((bf16[16,2048]{1,0:T(8,128)(2,1)S(1)}, bf16[16,2048]{1,0:T(8,128)(2,1)S(1)}, u32[]{:S(2)}, u32[]{:S(2)}) %collective-permute-start.8) | collective-permute-done | bytes 65568 | tf_op jit(solution)/shard_map/ppermute | solution.py:509
  70.7 1.7 %collective-permute-start.12 = (bf16[16,2048]{1,0:T(8,128)(2,1)S(1)}, bf16[16,2048]{1,0:T(8,128)(2,1)S(1)}, u32[]{:S(2)}, u32[]{:S(2)}) collective-permute-start(bf16[16,2048]{1,0:T(8,128)(2,1)S(1)} %multiply_convert_fusion.1), channel_id=1, source_target_pairs={{0,24},{1,25},{2,26},{3,27},{4,28},{5,29},{6,30},{7,31},{8,16},{9,... | collective-permute-start | bytes 196616 | tf_op jit(solution)/shard_map/ppermute | solution.py:509
  72.4 2.8 %collective-permute-start.10 = (bf16[16,2048]{1,0:T(8,128)(2,1)S(1)}, bf16[16,2048]{1,0:T(8,128)(2,1)S(1)}, u32[]{:S(2)}, u32[]{:S(2)}) collective-permute-start(bf16[16,2048]{1,0:T(8,128)(2,1)S(1)} %multiply_convert_fusion.1), channel_id=1, source_target_pairs={{0,8},{1,9},{2,10},{3,11},{4,12},{5,13},{6,14},{7,15},{8,0},{9,1},... | collective-permute-start | bytes 196616 | tf_op jit(solution)/shard_map/ppermute | solution.py:509
  75.2 1.6 %collective-permute-start.14 = (bf16[64,768]{1,0:T(8,128)(2,1)S(1)}, bf16[64,768]{1,0:T(8,128)(2,1)S(1)}, u32[]{:S(2)}, u32[]{:S(2)}) collective-permute-start(bf16[64,768]{1,0:T(8,128)(2,1)S(1)} %add_convert_fusion), channel_id=1, source_target_pairs={{0,2},{1,3},{2,0},{3,1},{4,6},{5,7},{6,4},{7,5},{8,10},{9,11},{10,... | collective-permute-start | bytes 294920 | tf_op jit(solution)/shard_map/ppermute | solution.py:509
  76.8 0.5 collective-permute-done.12
  77.3 1.5 %collective-permute-done.11 = bf16[16,2048]{1,0:T(8,128)(2,1)S(1)} collective-permute-done((bf16[16,2048]{1,0:T(8,128)(2,1)S(1)}, bf16[16,2048]{1,0:T(8,128)(2,1)S(1)}, u32[]{:S(2)}, u32[]{:S(2)}) %collective-permute-start.11) | collective-permute-done | bytes 65568 | tf_op jit(solution)/shard_map/ppermute | solution.py:509
  78.9 1.0 collective-permute-done.14
  79.9 0.2 collective-permute-start.18
  80.1 2.5 %collective-permute-start.17 = (bf16[64,2048]{1,0:T(8,128)(2,1)S(1)}, bf16[64,2048]{1,0:T(8,128)(2,1)S(1)}, u32[]{:S(2)}, u32[]{:S(2)}) collective-permute-start(bf16[64,2048]{1,0:T(8,128)(2,1)S(1)} %pad_maximum_fusion.1), channel_id=1, source_target_pairs={{0,6},{1,7},{2,4},{3,5},{4,2},{5,3},{6,0},{7,1},{8,14},{9,15},{10,... | collective-permute-start | bytes 786440 | tf_op jit(solution)/shard_map/ppermute | solution.py:509
  82.6 0.5 collective-permute-start.16
  83.1 0.5 collective-permute-start.15
  83.6 2.3 %collective-permute-done.18 = bf16[64,768]{1,0:T(8,128)(2,1)S(1)} collective-permute-done((bf16[64,768]{1,0:T(8,128)(2,1)S(1)}, bf16[64,768]{1,0:T(8,128)(2,1)S(1)}, u32[]{:S(2)}, u32[]{:S(2)}) %collective-permute-start.18) | collective-permute-done | bytes 98336 | tf_op jit(solution)/shard_map/ppermute | solution.py:509
  86.1 5.6 %collective-permute-done.19 = bf16[128,768]{1,0:T(8,128)(2,1)S(1)} collective-permute-done((bf16[128,768]{1,0:T(8,128)(2,1)S(1)}, bf16[128,768]{1,0:T(8,128)(2,1)S(1)}, u32[]{:S(2)}, u32[]{:S(2)}) %collective-permute-start.19) | collective-permute-done | bytes 196640 | tf_op jit(solution)/shard_map/ppermute | solution.py:509
  91.8 1.8 %collective-permute-done.16 = bf16[64,2048]{1,0:T(8,128)(2,1)S(1)} collective-permute-done((bf16[64,2048]{1,0:T(8,128)(2,1)S(1)}, bf16[64,2048]{1,0:T(8,128)(2,1)S(1)}, u32[]{:S(2)}, u32[]{:S(2)}) %collective-permute-start.16) | collective-permute-done | bytes 262176 | tf_op jit(solution)/shard_map/ppermute | solution.py:509
  93.6 0.1 collective-permute-done.15
  93.9 0.5 collective-permute-start.21
  94.4 2.8 %finish_own.1 = (f32[128,512]{1,0:T(8,128)}, f32[256,512]{1,0:T(8,128)}, f32[512,2048]{1,0:T(8,128)}, f32[512,512]{1,0:T(8,128)}) custom-call(s32[1]{0:T(128)} %bitcast.me_ref, bf16[256,128]{1,0:T(8,128)(2,1)S(1)} %get-tuple-element.52.chosen_ref, bf16[256,128]{1,0:T(8,128)(2,1)S(1)} %bitcast.9, ...), custom_call_target="tpu_custom_call" | custom-call | flops 100000000 | bytes 5000000 | tf_op jit(solution)/shard_map/finish_own/pallas_call | solution.py:442
  97.3 2.0 %finish_other.1 = (f32[256,512]{1,0:T(8,128)}, f32[512,2048]{1,0:T(8,128)}, f32[512,512]{1,0:T(8,128)}) custom-call(s32[1]{0:T(128)} %bitcast.me_ref, bf16[256,2048]{1,0:T(8,128)(2,1)S(1)} %collective-permute-done.20.early_ref, bf16[256,768]{1,0:T(8,128)(2,1)S(1)} %collective-permute-done.21.late_ref, ...), custom_call_target="tpu_custom_call", output_to_operand_aliasing={{0}: (3, {}), {1}: (4, {}), {2}: (5, {})} | custom-call | bytes 5000000 | tf_op jit(solution)/shard_map/finish_other/pallas_call | solution.py:452
  (34 shorter events, 0.7 us)
Async XLA Ops:
  2.0 14.4 %all-to-all-start = ((s32[32,1,2]{2,1,0:T(1,128)}), s32[32,1,2]{2,1,0:T(1,128)S(1)}, u32[]{:S(2)}, u32[]{:S(2)}) async-start(s32[32,1,2]{2,1,0:T(1,128)} %copy.18), calls=%async_computation | async-start | bytes 32768 | tf_op jit(solution)/shard_map/all_to_all | solution.py:505
  9.3 0.9 copy-start.2
  17.3 10.0 %all-to-all-start.1 = ((bf16[32,8,128]{2,1,0:T(8,128)(2,1)}), bf16[32,8,128]{2,1,0:T(8,128)(2,1)S(1)}, u32[]{:S(2)}, u32[]{:S(2)}) async-start(bf16[32,8,128]{2,1,0:T(8,128)(2,1)} %bitcast.5), calls=%async_computation.1 | async-start | bytes 131072 | tf_op jit(solution)/shard_map/all_to_all | solution.py:505
  27.2 0.6 copy-start.3
  42.4 3.6 %collective-permute-start = (bf16[256,2048]{1,0:T(8,128)(2,1)}, bf16[256,2048]{1,0:T(8,128)(2,1)S(1)}, u32[]{:S(2)}, u32[]{:S(2)}) collective-permute-start(bf16[256,2048]{1,0:T(8,128)(2,1)} %get-tuple-element.56), channel_id=1, source_target_pairs={{0,1},{1,0},{2,3},{3,2},{4,5},{5,4},{6,7},{7,6},{8,9},{9,8},{10,11... | collective-permute-start | bytes 3145736 | tf_op jit(solution)/shard_map/ppermute | solution.py:509
  42.6 3.3 %collective-permute-start.1 = (bf16[256,768]{1,0:T(8,128)(2,1)}, bf16[256,768]{1,0:T(8,128)(2,1)S(1)}, u32[]{:S(2)}, u32[]{:S(2)}) collective-permute-start(bf16[256,768]{1,0:T(8,128)(2,1)} %get-tuple-element.62), channel_id=1, source_target_pairs={{0,1},{1,0},{2,3},{3,2},{4,5},{5,4},{6,7},{7,6},{8,9},{9,8},{10,11... | collective-permute-start | bytes 1179656 | tf_op jit(solution)/shard_map/ppermute | solution.py:509
  43.0 1.2 %copy-start = (bf16[256,2048]{1,0:T(8,128)(2,1)S(1)}, bf16[256,2048]{1,0:T(8,128)(2,1)}, u32[]{:S(2)}) copy-start(bf16[256,2048]{1,0:T(8,128)(2,1)} %get-tuple-element.53.refs_0_) | copy-start | bytes 3145732
  44.2 1.0 %copy-start.1 = (bf16[256,768]{1,0:T(8,128)(2,1)S(1)}, bf16[256,768]{1,0:T(8,128)(2,1)}, u32[]{:S(2)}) copy-start(bf16[256,768]{1,0:T(8,128)(2,1)} %get-tuple-element.54.refs_1_) | copy-start | bytes 1179652
  46.3 7.0 %collective-permute-start.3 = (bf16[128,768]{1,0:T(8,128)(2,1)S(1)}, bf16[128,768]{1,0:T(8,128)(2,1)S(1)}, u32[]{:S(2)}, u32[]{:S(2)}) collective-permute-start(bf16[128,768]{1,0:T(8,128)(2,1)S(1)} %get-tuple-element.66), channel_id=1, source_target_pairs={{0,8},{1,9},{2,10},{3,11},{4,12},{5,13},{6,14},{7,15},{8,0},{9,1},... | collective-permute-start | bytes 589832 | tf_op jit(solution)/shard_map/ppermute | solution.py:509
  46.9 9.2 %collective-permute-start.2 = (bf16[64,2048]{1,0:T(8,128)(2,1)S(1)}, bf16[64,2048]{1,0:T(8,128)(2,1)S(1)}, u32[]{:S(2)}, u32[]{:S(2)}) collective-permute-start(bf16[64,2048]{1,0:T(8,128)(2,1)S(1)} %get-tuple-element.64), channel_id=1, source_target_pairs={{0,2},{1,3},{2,0},{3,1},{4,6},{5,7},{6,4},{7,5},{8,10},{9,11},{10,... | collective-permute-start | bytes 786440 | tf_op jit(solution)/shard_map/ppermute | solution.py:509
  47.4 13.4 %collective-permute-start.4 = (bf16[64,2048]{1,0:T(8,128)(2,1)S(1)}, bf16[64,2048]{1,0:T(8,128)(2,1)S(1)}, u32[]{:S(2)}, u32[]{:S(2)}) collective-permute-start(bf16[64,2048]{1,0:T(8,128)(2,1)S(1)} %get-tuple-element.69), channel_id=1, source_target_pairs={{0,4},{1,5},{2,6},{3,7},{4,0},{5,1},{6,2},{7,3},{8,12},{9,13},{10,... | collective-permute-start | bytes 786440 | tf_op jit(solution)/shard_map/ppermute | solution.py:509
  48.2 12.5 %collective-permute-start.5 = (bf16[64,2048]{1,0:T(8,128)(2,1)S(1)}, bf16[64,2048]{1,0:T(8,128)(2,1)S(1)}, u32[]{:S(2)}, u32[]{:S(2)}) collective-permute-start(bf16[64,2048]{1,0:T(8,128)(2,1)S(1)} %get-tuple-element.70), channel_id=1, source_target_pairs={{0,6},{1,7},{2,4},{3,5},{4,2},{5,3},{6,0},{7,1},{8,14},{9,15},{10,... | collective-permute-start | bytes 786440 | tf_op jit(solution)/shard_map/ppermute | solution.py:509
  53.3 7.5 %collective-permute-start.6 = (bf16[64,768]{1,0:T(8,128)(2,1)S(1)}, bf16[64,768]{1,0:T(8,128)(2,1)S(1)}, u32[]{:S(2)}, u32[]{:S(2)}) collective-permute-start(bf16[64,768]{1,0:T(8,128)(2,1)S(1)} %add_convert_fusion.2), channel_id=1, source_target_pairs={{0,16},{1,17},{2,18},{3,19},{4,20},{5,21},{6,22},{7,23},{8,24},{9,... | collective-permute-start | bytes 294920 | tf_op jit(solution)/shard_map/ppermute | solution.py:509
  56.1 14.5 %all-to-all-start.2 = ((bf16[32,8,128]{2,1,0:T(8,128)(2,1)}), bf16[32,8,128]{2,1,0:T(8,128)(2,1)S(1)}, u32[]{:S(2)}, u32[]{:S(2)}) async-start(bf16[32,8,128]{2,1,0:T(8,128)(2,1)} %bitcast.7), calls=%async_computation.2 | async-start | bytes 131072 | tf_op jit(solution)/shard_map/all_to_all | solution.py:505
  60.9 5.0 %collective-permute-start.7 = (bf16[16,2048]{1,0:T(8,128)(2,1)S(1)}, bf16[16,2048]{1,0:T(8,128)(2,1)S(1)}, u32[]{:S(2)}, u32[]{:S(2)}) collective-permute-start(bf16[16,2048]{1,0:T(8,128)(2,1)S(1)} %get-tuple-element.95), channel_id=1, source_target_pairs={{0,8},{1,9},{2,10},{3,11},{4,12},{5,13},{6,14},{7,15},{8,0},{9,1},... | collective-permute-start | bytes 196616 | tf_op jit(solution)/shard_map/ppermute | solution.py:509
  62.4 6.1 %collective-permute-start.9 = (bf16[16,2048]{1,0:T(8,128)(2,1)S(1)}, bf16[16,2048]{1,0:T(8,128)(2,1)S(1)}, u32[]{:S(2)}, u32[]{:S(2)}) collective-permute-start(bf16[16,2048]{1,0:T(8,128)(2,1)S(1)} %get-tuple-element.96), channel_id=1, source_target_pairs={{0,24},{1,25},{2,26},{3,27},{4,28},{5,29},{6,30},{7,31},{8,16},{9,... | collective-permute-start | bytes 196616 | tf_op jit(solution)/shard_map/ppermute | solution.py:509
  63.2 7.4 %collective-permute-start.8 = (bf16[16,2048]{1,0:T(8,128)(2,1)S(1)}, bf16[16,2048]{1,0:T(8,128)(2,1)S(1)}, u32[]{:S(2)}, u32[]{:S(2)}) collective-permute-start(bf16[16,2048]{1,0:T(8,128)(2,1)S(1)} %get-tuple-element.97), channel_id=1, source_target_pairs={{0,16},{1,17},{2,18},{3,19},{4,20},{5,21},{6,22},{7,23},{8,24},{9,... | collective-permute-start | bytes 196616 | tf_op jit(solution)/shard_map/ppermute | solution.py:509
  64.5 10.6 %collective-permute-start.13 = (bf16[64,768]{1,0:T(8,128)(2,1)S(1)}, bf16[64,768]{1,0:T(8,128)(2,1)S(1)}, u32[]{:S(2)}, u32[]{:S(2)}) collective-permute-start(bf16[64,768]{1,0:T(8,128)(2,1)S(1)} %add_convert_fusion.1), channel_id=1, source_target_pairs={{0,4},{1,5},{2,6},{3,7},{4,0},{5,1},{6,2},{7,3},{8,12},{9,13},{10,... | collective-permute-start | bytes 294920 | tf_op jit(solution)/shard_map/ppermute | solution.py:509
  70.7 6.6 %collective-permute-start.12 = (bf16[16,2048]{1,0:T(8,128)(2,1)S(1)}, bf16[16,2048]{1,0:T(8,128)(2,1)S(1)}, u32[]{:S(2)}, u32[]{:S(2)}) collective-permute-start(bf16[16,2048]{1,0:T(8,128)(2,1)S(1)} %multiply_convert_fusion.1), channel_id=1, source_target_pairs={{0,24},{1,25},{2,26},{3,27},{4,28},{5,29},{6,30},{7,31},{8,16},{9,... | collective-permute-start | bytes 196616 | tf_op jit(solution)/shard_map/ppermute | solution.py:509
  72.4 6.5 %collective-permute-start.11 = (bf16[16,2048]{1,0:T(8,128)(2,1)S(1)}, bf16[16,2048]{1,0:T(8,128)(2,1)S(1)}, u32[]{:S(2)}, u32[]{:S(2)}) collective-permute-start(bf16[16,2048]{1,0:T(8,128)(2,1)S(1)} %multiply_convert_fusion.1), channel_id=1, source_target_pairs={{0,16},{1,17},{2,18},{3,19},{4,20},{5,21},{6,22},{7,23},{8,24},{9,... | collective-permute-start | bytes 196616 | tf_op jit(solution)/shard_map/ppermute | solution.py:509
  72.4 6.5 %collective-permute-start.10 = (bf16[16,2048]{1,0:T(8,128)(2,1)S(1)}, bf16[16,2048]{1,0:T(8,128)(2,1)S(1)}, u32[]{:S(2)}, u32[]{:S(2)}) collective-permute-start(bf16[16,2048]{1,0:T(8,128)(2,1)S(1)} %multiply_convert_fusion.1), channel_id=1, source_target_pairs={{0,8},{1,9},{2,10},{3,11},{4,12},{5,13},{6,14},{7,15},{8,0},{9,1},... | collective-permute-start | bytes 196616 | tf_op jit(solution)/shard_map/ppermute | solution.py:509
  75.2 4.7 %collective-permute-start.14 = (bf16[64,768]{1,0:T(8,128)(2,1)S(1)}, bf16[64,768]{1,0:T(8,128)(2,1)S(1)}, u32[]{:S(2)}, u32[]{:S(2)}) collective-permute-start(bf16[64,768]{1,0:T(8,128)(2,1)S(1)} %add_convert_fusion), channel_id=1, source_target_pairs={{0,2},{1,3},{2,0},{3,1},{4,6},{5,7},{6,4},{7,5},{8,10},{9,11},{10,... | collective-permute-start | bytes 294920 | tf_op jit(solution)/shard_map/ppermute | solution.py:509
  79.9 6.1 %collective-permute-start.18 = (bf16[64,768]{1,0:T(8,128)(2,1)S(1)}, bf16[64,768]{1,0:T(8,128)(2,1)S(1)}, u32[]{:S(2)}, u32[]{:S(2)}) collective-permute-start(bf16[64,768]{1,0:T(8,128)(2,1)S(1)} %multiply_convert_fusion), channel_id=1, source_target_pairs={{0,16},{1,17},{2,18},{3,19},{4,20},{5,21},{6,22},{7,23},{8,24},{9,... | collective-permute-start | bytes 294920 | tf_op jit(solution)/shard_map/ppermute | solution.py:509
  80.1 11.6 %collective-permute-start.17 = (bf16[64,2048]{1,0:T(8,128)(2,1)S(1)}, bf16[64,2048]{1,0:T(8,128)(2,1)S(1)}, u32[]{:S(2)}, u32[]{:S(2)}) collective-permute-start(bf16[64,2048]{1,0:T(8,128)(2,1)S(1)} %pad_maximum_fusion.1), channel_id=1, source_target_pairs={{0,6},{1,7},{2,4},{3,5},{4,2},{5,3},{6,0},{7,1},{8,14},{9,15},{10,... | collective-permute-start | bytes 786440 | tf_op jit(solution)/shard_map/ppermute | solution.py:509
  82.6 11.0 %collective-permute-start.16 = (bf16[64,2048]{1,0:T(8,128)(2,1)S(1)}, bf16[64,2048]{1,0:T(8,128)(2,1)S(1)}, u32[]{:S(2)}, u32[]{:S(2)}) collective-permute-start(bf16[64,2048]{1,0:T(8,128)(2,1)S(1)} %pad_maximum_fusion.1), channel_id=1, source_target_pairs={{0,4},{1,5},{2,6},{3,7},{4,0},{5,1},{6,2},{7,3},{8,12},{9,13},{10,... | collective-permute-start | bytes 786440 | tf_op jit(solution)/shard_map/ppermute | solution.py:509
  83.1 10.7 %collective-permute-start.15 = (bf16[64,2048]{1,0:T(8,128)(2,1)S(1)}, bf16[64,2048]{1,0:T(8,128)(2,1)S(1)}, u32[]{:S(2)}, u32[]{:S(2)}) collective-permute-start(bf16[64,2048]{1,0:T(8,128)(2,1)S(1)} %pad_maximum_fusion.1), channel_id=1, source_target_pairs={{0,2},{1,3},{2,0},{3,1},{4,6},{5,7},{6,4},{7,5},{8,10},{9,11},{10,... | collective-permute-start | bytes 786440 | tf_op jit(solution)/shard_map/ppermute | solution.py:509
  86.0 5.7 %collective-permute-start.19 = (bf16[128,768]{1,0:T(8,128)(2,1)S(1)}, bf16[128,768]{1,0:T(8,128)(2,1)S(1)}, u32[]{:S(2)}, u32[]{:S(2)}) collective-permute-start(bf16[128,768]{1,0:T(8,128)(2,1)S(1)} %pad_maximum_fusion.2), channel_id=1, source_target_pairs={{0,8},{1,9},{2,10},{3,11},{4,12},{5,13},{6,14},{7,15},{8,0},{9,1},... | collective-permute-start | bytes 589832 | tf_op jit(solution)/shard_map/ppermute | solution.py:509
  93.8 3.4 %collective-permute-start.20 = (bf16[256,2048]{1,0:T(8,128)(2,1)S(1)}, bf16[256,2048]{1,0:T(8,128)(2,1)S(1)}, u32[]{:S(2)}, u32[]{:S(2)}) collective-permute-start(bf16[256,2048]{1,0:T(8,128)(2,1)S(1)} %constant_dynamic-update-slice_fusion.early_ref), channel_id=1, source_target_pairs={{0,1},{1,0},{2,3},{3,2},{4,5},{5,4},{6,7},{7,6},{8,9},{9,8},{10,11... | collective-permute-start | bytes 3145736 | tf_op jit(solution)/shard_map/ppermute | solution.py:509
  93.9 3.4 %collective-permute-start.21 = (bf16[256,768]{1,0:T(8,128)(2,1)S(1)}, bf16[256,768]{1,0:T(8,128)(2,1)S(1)}, u32[]{:S(2)}, u32[]{:S(2)}) collective-permute-start(bf16[256,768]{1,0:T(8,128)(2,1)S(1)} %pad_maximum_fusion.late_ref), channel_id=1, source_target_pairs={{0,1},{1,0},{2,3},{3,2},{4,5},{5,4},{6,7},{7,6},{8,9},{9,8},{10,11... | collective-permute-start | bytes 1179656 | tf_op jit(solution)/shard_map/ppermute | solution.py:509
